TPU v7x, 32 devices: a whole 2x2x4 slice. The times are simulated.
32 devices in a mesh: group: 2 (over x), wide: 2 (over core), tensor: 8 (over z, y).
Axes of the slice: x: 2, y: 2, z: 4, core: 2. Of those that a mesh axis runs over, the one named last changes fastest.
Arguments:
- tokens: bfloat16 [512, 8192], P(('group', 'wide'), 'tensor'), parts along dimension 0, may hold values from -6 to 6
- gain: float32 [16384], P('group'), parts along dimension 0, may hold values from 0.5 to 2
- gate_weight: bfloat16 [16384, 16384], P(('group', 'wide', 'tensor')), parts along dimension 0, may hold values from -0.09375 to 0.09375
- up_weight: bfloat16 [16384, 16384], P(('group', 'wide', 'tensor')), parts along dimension 0, may hold values from -0.09375 to 0.09375
- gate_mask: int32 [256, 256], P('group'), parts along dimension 0, may hold values from 0 to 1, as said below
- up_mask: int32 [256, 256], P('group'), parts along dimension 0, may hold values from 0 to 1, as said below
Outputs:
- hidden: bfloat16 [512, 16384], P(('group', 'wide'), 'tensor'), parts along dimension 0
There are 2 independent parts, one for each index of `group`. A program takes and returns all parts, laid end to end along the dimension named above; each array names one. Nothing has to cross between parts.
Inputs may be any that keep to these rules, and one draw needn't show every extreme that they name: `gate_mask`: A 1 keeps a block, a 0 prunes it; the share of kept blocks differs between groups of consecutive hidden-unit blocks. `up_mask`: as for gate_mask.
All inputs are finite; a program needn't handle non-finite values.
Results may differ from a plain program's by a relative error of at most 0.0058.
Values may be sent and summed in bfloat16 or wider, within the bound.
No kernel may reach another device: no remote copies, remote signals or barrier semaphores. Data moves between devices by JAX's collectives and lax.ppermute only.
A program may use at most 256 MiB of HBM per device.

v0:
```python
import jax
import jax.numpy as jnp
from jax import lax
from jax.sharding import PartitionSpec as P

D = 8192
FF = 16384
BS = 64


def apply_mask(weight, mask):
    rows, cols = mask.shape
    blocks = weight.reshape(rows, weight.shape[0] // rows, cols, weight.shape[1] // cols)
    blocks = blocks * mask.astype(jnp.bfloat16)[:, None, :, None]
    return blocks.reshape(weight.shape)


def local(tokens, gain, gate_weight, up_weight, gate_mask, up_mask):
    whole = lax.all_gather(tokens, "tensor", axis=1, tiled=True)
    values = whole.astype(jnp.float32)
    scale = lax.rsqrt(jnp.mean(values * values, axis=-1, keepdims=True) + 1e-05)
    normed = (values * scale * gain).astype(jnp.bfloat16)
    shard = lax.axis_index("tensor")
    half = lax.axis_index("wide")
    width = FF // lax.axis_size("tensor")
    half_rows = D // lax.axis_size("wide")
    col_blocks = width // BS
    row_blocks = half_rows // BS
    first_col = shard * col_blocks
    gate_half = lax.all_to_all(gate_weight, "tensor", split_axis=1, concat_axis=0, tiled=True)
    up_half = lax.all_to_all(up_weight, "tensor", split_axis=1, concat_axis=0, tiled=True)
    first_row = half * row_blocks
    gate_kept = apply_mask(
        gate_half, lax.dynamic_slice(gate_mask, (first_row, first_col), (row_blocks, col_blocks))
    )
    up_kept = apply_mask(
        up_half, lax.dynamic_slice(up_mask, (first_row, first_col), (row_blocks, col_blocks))
    )
    features_half = lax.all_to_all(normed, "wide", split_axis=1, concat_axis=0, tiled=True)
    gate_part = jnp.dot(features_half, gate_kept, preferred_element_type=jnp.float32)
    up_part = jnp.dot(features_half, up_kept, preferred_element_type=jnp.float32)
    gate, up = (
        lax.psum_scatter(gate_part, "wide", scatter_dimension=0, tiled=True),
        lax.psum_scatter(up_part, "wide", scatter_dimension=0, tiled=True),
    )
    return (jax.nn.silu(gate) * up).astype(jnp.bfloat16)


def solution(mesh):
    in_specs = (
        P(("group", "wide"), "tensor"),
        P("group"),
        P(("group", "wide", "tensor"), None),
        P(("group", "wide", "tensor"), None),
        P("group", None),
        P("group", None),
    )
    out_specs = P(("group", "wide"), "tensor")
    return jax.shard_map(local, mesh=mesh, in_specs=in_specs, out_specs=out_specs, check_vma=False)
```

profile of v0, /device:TPU:0, one launch (start us, length us, event | category | flops | bytes accessed | tf_op | source)
XLA Modules:
  0.0 877.9 jit_solution(4451933863547242540)
XLA Ops:
  6.5 0.0 all-gather.2.cloned.1.call-start
  6.5 1.8 copy.7
  8.3 0.0 all-gather.2.cloned.1.call-update
  8.4 0.0 copy-start.1
  8.4 22.5 %copy.9 = bf16[512,16384]{0,1:T(8,128)(2,1)} copy(bf16[512,16384]{1,0:T(8,128)(2,1)} %param.8) | data formatting | bytes 33554432 | tf_op args[2]
  30.9 30.6 %all-gather.2.cloned.1.call-done = bf16[128,8192]{0,1:T(8,128)(2,1)} async-done(((bf16[128,1024]{0,1:T(8,128)(2,1)}), bf16[128,8192]{0,1:T(8,128)(2,1)}) %all-gather.2.cloned.1.call-update) | async-done | bytes 2097168 | tf_op jit(solution)/shard_map/all_gather | solution.py:19
  61.5 2.7 fusion
  64.2 0.0 copy-done.1
  64.2 4.6 fusion.2
  68.8 5.4 all_to_all.51
  74.2 5.7 all-to-all-start.1
  80.0 22.5 %copy.12 = bf16[512,16384]{0,1:T(8,128)(2,1)} copy(bf16[512,16384]{1,0:T(8,128)(2,1)} %param.9) | data formatting | bytes 33554432 | tf_op args[3]
  102.4 340.9 %all-to-all-done.1 = bf16[512,8,2048]{0,2,1:T(8,128)(2,1)} async-done(((bf16[512,8,2048]{0,2,1:T(8,128)(2,1)}), bf16[512,8,2048]{0,2,1:T(8,128)(2,1)}, u32[]{:S(2)}, u32[]{:S(2)}) %all-to-all-start.1) | async-done | bytes 16777248 | tf_op jit(solution)/shard_map/all_to_all | solution.py:30
  443.4 5.7 all-to-all-start.2
  449.1 0.0 reduce-scatter.3.cloned.1.call-start
  449.2 0.9 dynamic-slice_convert_fusion
  450.0 11.2 %mul.67 = bf16[64,64,32,64]{3,2,1,0:T(8,128)(2,1)} broadcast(bf16[64,32]{1,0:T(8,128)(2,1)S(1)} %get-tuple-element.6), dimensions={0,2} | broadcast | bytes 16781312 | tf_op jit(solution)/shard_map/mul | solution.py:14
  461.2 45.9 %mul.68 = bf16[8,512,2048]{2,1,0:T(8,128)(2,1)} reshape(bf16[64,64,32,64]{3,2,1,0:T(8,128)(2,1)} %mul.67) | data formatting | bytes 33554432 | tf_op jit(solution)/shard_map/mul | solution.py:14
  507.1 21.6 %copy.10 = bf16[8,512,2048]{1,2,0:T(8,128)(2,1)} copy(bf16[8,512,2048]{2,1,0:T(8,128)(2,1)} %mul.68) | data formatting | bytes 33554432 | tf_op jit(solution)/shard_map/mul | solution.py:14
  528.7 11.1 %mul.72 = bf16[64,64,32,64]{3,2,1,0:T(8,128)(2,1)} broadcast(bf16[64,32]{1,0:T(8,128)(2,1)S(1)} %get-tuple-element.5), dimensions={0,2} | broadcast | bytes 16781312 | tf_op jit(solution)/shard_map/mul | solution.py:14
  539.8 45.9 %mul.73 = bf16[8,512,2048]{2,1,0:T(8,128)(2,1)} reshape(bf16[64,64,32,64]{3,2,1,0:T(8,128)(2,1)} %mul.72) | data formatting | bytes 33554432 | tf_op jit(solution)/shard_map/mul | solution.py:14
  585.6 21.6 %copy.13 = bf16[8,512,2048]{1,2,0:T(8,128)(2,1)} copy(bf16[8,512,2048]{2,1,0:T(8,128)(2,1)} %mul.73) | data formatting | bytes 33554432 | tf_op jit(solution)/shard_map/mul | solution.py:14
  607.3 2.8 copy.8
  610.1 17.2 %bitcast_multiply_fusion.1 = bf16[8,512,2048]{1,2,0:T(8,128)(2,1)} fusion(bf16[8,512,2048]{1,2,0:T(8,128)(2,1)} %copy.10, bf16[512,8,2048]{0,2,1:T(8,128)(2,1)} %all-to-all-done.1), kind=kLoop, calls=%fused_computation.1 | loop fusion | flops 8388608 | bytes 50331648 | tf_op jit(solution)/shard_map/mul | solution.py:14
  627.2 0.0 copy-start
  627.2 21.8 %copy.11 = bf16[8,512,2048]{2,1,0:T(8,128)(2,1)} copy(bf16[8,512,2048]{1,2,0:T(8,128)(2,1)} %bitcast_multiply_fusion.1) | data formatting | bytes 33554432 | tf_op jit(solution)/shard_map/mul | solution.py:14
  649.0 0.0 copy-done
  649.0 9.4 %fusion.3 = f32[256,2048]{1,0:T(8,128)} fusion(bf16[256,4096]{1,0:T(8,128)(2,1)S(1)} %bitcast.25, bf16[4096,2048]{1,0:T(8,128)(2,1)} %bitcast.22), kind=kOutput, calls=%fused_computation.11 | convolution fusion | flops 4294967296 | bytes 20971520 | tf_op jit(solution)/shard_map/dot_general | solution.py:40
  658.5 0.0 reduce-scatter.3.cloned.1.call-update
  658.5 0.2 reduce-scatter.5.cloned.1.call-start
  658.7 153.0 %all-to-all-done.2 = bf16[512,8,2048]{0,2,1:T(8,128)(2,1)} async-done(((bf16[512,8,2048]{0,2,1:T(8,128)(2,1)}), bf16[512,8,2048]{0,2,1:T(8,128)(2,1)}, u32[]{:S(2)}, u32[]{:S(2)}) %all-to-all-start.2) | async-done | bytes 16777248 | tf_op jit(solution)/shard_map/all_to_all | solution.py:31
  811.7 17.2 %bitcast_multiply_fusion = bf16[8,512,2048]{1,2,0:T(8,128)(2,1)} fusion(bf16[8,512,2048]{1,2,0:T(8,128)(2,1)} %copy.13, bf16[512,8,2048]{0,2,1:T(8,128)(2,1)} %all-to-all-done.2), kind=kLoop, calls=%fused_computation | loop fusion | flops 8388608 | bytes 50331648 | tf_op jit(solution)/shard_map/mul | solution.py:14
  828.9 21.7 %copy.14 = bf16[8,512,2048]{2,1,0:T(8,128)(2,1)} copy(bf16[8,512,2048]{1,2,0:T(8,128)(2,1)} %bitcast_multiply_fusion) | data formatting | bytes 33554432 | tf_op jit(solution)/shard_map/mul | solution.py:14
  850.5 9.5 %fusion.4 = f32[256,2048]{1,0:T(8,128)} fusion(bf16[256,4096]{1,0:T(8,128)(2,1)S(1)} %bitcast.26, bf16[4096,2048]{1,0:T(8,128)(2,1)} %bitcast.21), kind=kOutput, calls=%fused_computation.12 | convolution fusion | flops 4294967296 | bytes 20971520 | tf_op jit(solution)/shard_map/dot_general | solution.py:41
  860.0 0.0 reduce-scatter.5.cloned.1.call-update
  860.0 0.0 reduce-scatter.3.cloned.1.call-done
  860.0 8.8 reduce-scatter.5.cloned.1.call-done
  868.8 2.6 multiply_convert_fusion
  (1 shorter events, 0.0 us)
Async XLA Ops:
  6.5 55.0 %all-gather.2.cloned.1.call-start = ((), (), s32[]{:S(2)}) async-start(), calls=%async_computation.5 | async-start | bytes 2359296 | tf_op jit(solution)/shard_map/all_gather | solution.py:19
  8.4 55.9 %copy-start.1 = (f32[8192]{0:T(1024)S(1)}, f32[8192]{0:T(1024)}, u32[]{:S(2)}) copy-start(f32[8192]{0:T(1024)} %param.7) | copy-start | bytes 98308
  74.2 369.1 %all-to-all-start.1 = ((bf16[512,8,2048]{0,2,1:T(8,128)(2,1)}), bf16[512,8,2048]{0,2,1:T(8,128)(2,1)}, u32[]{:S(2)}, u32[]{:S(2)}) async-start(bf16[512,8,2048]{0,2,1:T(8,128)(2,1)} %bitcast.20), calls=%async_computation.1 | async-start | bytes 33554432 | tf_op jit(solution)/shard_map/all_to_all | solution.py:30
  443.4 368.3 %all-to-all-start.2 = ((bf16[512,8,2048]{0,2,1:T(8,128)(2,1)}), bf16[512,8,2048]{0,2,1:T(8,128)(2,1)}, u32[]{:S(2)}, u32[]{:S(2)}) async-start(bf16[512,8,2048]{0,2,1:T(8,128)(2,1)} %bitcast.19), calls=%async_computation.3 | async-start | bytes 33554432 | tf_op jit(solution)/shard_map/all_to_all | solution.py:31
  449.1 410.9 %reduce-scatter.3.cloned.1.call-start = ((), (), s32[]{:S(2)}) async-start(), calls=%async_computation.6 | async-start | bytes 3145728 | tf_op jit(solution)/shard_map/reduce_scatter | solution.py:43
  627.2 21.8 %copy-start = (bf16[2,128,4096]{2,1,0:T(8,128)(2,1)S(1)}, bf16[2,128,4096]{2,1,0:T(8,128)(2,1)}, u32[]{:S(2)}) copy-start(bf16[2,128,4096]{2,1,0:T(8,128)(2,1)} %copy.8) | copy-start | bytes 6291460
  658.5 210.3 %reduce-scatter.5.cloned.1.call-start = ((), (), s32[]{:S(2)}) async-start(), calls=%async_computation.7 | async-start | bytes 3145728 | tf_op jit(solution)/shard_map/reduce_scatter | solution.py:44
Sparse Core Ops, SparseCore 0:
  9.5 51.9 all-gather.1
  658.6 10.8 reduce-scatter.2
  860.1 8.6 reduce-scatter.4
where the time goes:
time: 884 us; the launch traced here: 878 us
  waiting for transfers between devices  533 us (60%)
  local copies, waits for them, and re-layouts  250 us (28%)
  other arithmetic  45.1 us (5%)
  matrix products  18.9 us (2%)
  between operations  13.2 us (1%)
  starting transfers between devices  11.7 us (1%)
    all_to_all x1, waiting for transfers between devices, local(): lax.all_to_all(gate_weight, 'tensor', split_axis=1, concat_axis=0, tiled=...  341 us
    mul x8, local copies, waits for them, and re-layouts, apply_mask(): blocks = blocks * mask.astype(jnp.bfloat16)[:, None, :, None]  201 us
    all_to_all x1, waiting for transfers between devices, local(): lax.all_to_all(up_weight, 'tensor', split_axis=1, concat_axis=0, tiled=True)  153 us
    unnamed x7, local copies, waits for them, and re-layouts  46.8 us
    mul x2, other arithmetic, apply_mask(): blocks = blocks * mask.astype(jnp.bfloat16)[:, None, :, None]  34.3 us
    all_gather x1, waiting for transfers between devices, local(): whole = lax.all_gather(tokens, 'tensor', axis=1, tiled=True)  30.6 us
  transfers between devices with their start and end apart: 5, of which 4 were waited for; matrix products, arithmetic and copies ran while one was open for 34% of the time, Pallas kernels for 0%

commit v1 on v0

v1 whole, which is shorter than its diff:
```python
import functools

import jax
import jax.numpy as jnp
from jax import lax
from jax.experimental import pallas as pl
from jax.experimental.pallas import tpu as pltpu
from jax.sharding import PartitionSpec as P

EPS = 1e-05
LANES = 256


def exchange(value, axis, bit):
    size = lax.axis_size(axis)
    return lax.ppermute(value, axis, [(i, i ^ bit) for i in range(size)])


def product_kernel(shard_ref, x_ref, gate_ref, up_ref, gate_mask_ref, up_mask_ref, own_ref, send_ref):
    rows = x_ref.shape[0] // 2
    for i, (weight_ref, mask_ref) in enumerate(((gate_ref, gate_mask_ref), (up_ref, up_mask_ref))):
        blocks = mask_ref.shape[0]
        side = weight_ref.shape[0] // blocks
        kept = jnp.concatenate(
            [
                weight_ref[b * side : (b + 1) * side, :] * mask_ref[b : b + 1, :].astype(jnp.bfloat16)
                for b in range(blocks)
            ],
            axis=0,
        )
        sums = jnp.dot(x_ref[...], kept, preferred_element_type=jnp.float32)
        own_ref[0, i] = sums[:rows]
        send_ref[0, i] = sums[rows:].astype(jnp.bfloat16)


def products(shard, x, gate_weight, up_weight, gate_mask, up_mask, piece, shards):
    depth, width = gate_weight.shape
    rows = x.shape[0] // 2
    per_shard = width // shards // LANES

    def column(p, shard_ref):
        other = 2 * lax.rem(p, shards // 2) + p // (shards // 2)
        return (0, (shard_ref[0] ^ other) * per_shard + piece)

    grid_spec = pltpu.PrefetchScalarGridSpec(
        num_scalar_prefetch=1,
        grid=(shards,),
        in_specs=[
            pl.BlockSpec(x.shape, lambda p, s: (0, 0)),
            pl.BlockSpec((depth, LANES), column),
            pl.BlockSpec((depth, LANES), column),
            pl.BlockSpec((gate_mask.shape[0], LANES), column),
            pl.BlockSpec((up_mask.shape[0], LANES), column),
        ],
        out_specs=[
            pl.BlockSpec((1, 2, rows, LANES), lambda p, s: (p, 0, 0, 0)),
            pl.BlockSpec((1, 2, rows, LANES), lambda p, s: (p, 0, 0, 0)),
        ],
    )
    return pl.pallas_call(
        product_kernel,
        grid_spec=grid_spec,
        out_shape=[
            jax.ShapeDtypeStruct((shards, 2, rows, LANES), jnp.float32),
            jax.ShapeDtypeStruct((shards, 2, rows, LANES), jnp.bfloat16),
        ],
        compiler_params=pltpu.CompilerParams(vmem_limit_bytes=32 * 1024 * 1024),
        cost_estimate=pl.CostEstimate(
            flops=2 * 2 * x.shape[0] * depth * LANES * shards,
            bytes_accessed=2 * depth * LANES * shards * 2 + 2 * shards * rows * LANES * 6,
            transcendentals=0,
        ),
        name="products",
    )(shard.reshape(1), x, gate_weight, up_weight, gate_mask, up_mask)


def local(tokens, gain, gate_weight, up_weight, gate_mask, up_mask):
    shards = lax.axis_size("tensor")
    shard = lax.axis_index("tensor")
    half = lax.axis_index("wide")
    depth, width = gate_weight.shape
    features = gain.shape[0]
    rows = tokens.shape[0]

    first, second = [], []
    for w in range(2):
        for t in range(shards):
            source = w * (shards // 2) + t // 2
            first.append(((t % 2) * shards + source, w * shards + t))
            second.append(((1 - t % 2) * shards + source, w * shards + t))
    mine = lax.dynamic_slice_in_dim(tokens, half * depth, depth, 1)
    theirs = lax.dynamic_slice_in_dim(tokens, (1 - half) * depth, depth, 1)
    a = lax.ppermute(mine, ("wide", "tensor"), first)
    b = lax.ppermute(theirs, ("wide", "tensor"), second)

    values = tokens.astype(jnp.float32)
    squares = jnp.sum(values * values, axis=-1).reshape(1, rows)
    bit = 1
    while bit < shards:
        squares = squares + exchange(squares, "tensor", bit)
        bit *= 2
    scale = lax.rsqrt(squares / features + EPS)
    scale_other = exchange(scale, "wide", 1)

    straight = (shard % 2) == half
    own_raw = jnp.where(straight, a, b)
    other_raw = jnp.where(straight, b, a)
    raw = jnp.concatenate([own_raw, other_raw], axis=0).astype(jnp.float32)
    scales = jnp.concatenate([scale, scale_other], axis=1).reshape(2 * rows, 1)
    first_row = half * (features // 2) + shard * depth
    gains = lax.dynamic_slice_in_dim(gain, first_row, depth, 0)
    normed = (raw * scales * gains[None, :]).astype(jnp.bfloat16)

    side = features // gate_mask.shape[0]
    first_block = first_row // side
    masks = []
    for mask in (gate_mask, up_mask):
        part = lax.dynamic_slice_in_dim(mask, first_block, depth // side, 0).astype(jnp.float32)
        masks.append(jnp.repeat(part, width // mask.shape[1], axis=1))

    outs = []
    for piece in range(width // shards // LANES):
        own, send = products(shard, normed, gate_weight, up_weight, *masks, piece, shards)
        from_core = exchange(send, "wide", 1)
        pairs = shards // 2
        to_pair = (own[pairs:] + from_core[pairs:].astype(jnp.float32)).astype(jnp.bfloat16)
        from_pair = exchange(to_pair, "tensor", 1)
        received = []
        for p in range(1, pairs):
            to_far = (
                own[p] + from_core[p].astype(jnp.float32) + from_pair[p].astype(jnp.float32)
            ).astype(jnp.bfloat16)
            received.append(exchange(to_far, "tensor", 2 * p))
        total = own[0] + from_core[0].astype(jnp.float32) + from_pair[0].astype(jnp.float32)
        for value in received:
            total = total + value.astype(jnp.float32)
        outs.append((jax.nn.silu(total[0]) * total[1]).astype(jnp.bfloat16))
    return jnp.concatenate(outs, axis=1)


def solution(mesh):
    in_specs = (
        P(("group", "wide"), "tensor"),
        P("group"),
        P(("group", "wide", "tensor"), None),
        P(("group", "wide", "tensor"), None),
        P("group", None),
        P("group", None),
    )
    out_specs = P(("group", "wide"), "tensor")
    return jax.shard_map(local, mesh=mesh, in_specs=in_specs, out_specs=out_specs, check_vma=False)
```

time: 884 us -> 261 us (0.30)
  waiting for transfers between devices: 533 us -> 113 us
  local copies, waits for them, and re-layouts: 250 us -> 12.2 us
  Pallas kernels: 0 us -> 50.8 us
  starting transfers between devices: 11.7 us -> 60.9 us
  other arithmetic: 45.1 us -> 21.5 us
  matrix products: 18.9 us -> 0 us
  between operations: 13.2 us -> 0.44 us
    all_to_all x2 -> x0, waiting for transfers between devices: 494 us -> none  [the longest x1 341 us: local(): lax.all_to_all(gate_weight, 'tensor', split_axis=1, concat_axis=0, tiled=...]
    mul x8 -> x0, local copies, waits for them, and re-layouts: 201 us -> none  [apply_mask(): blocks = blocks * mask.astype(jnp.bfloat16)[:, None, :, None]]
    ppermute x0 -> x46, waiting for transfers between devices: none -> 113 us  [the longest x44 113 us: exchange(): return lax.ppermute(value, axis, [(i, i ^ bit) for i in range(size)])]
    ppermute x0 -> x46, starting transfers between devices: none -> 60.9 us  [the longest x44 54.5 us: exchange(): return lax.ppermute(value, axis, [(i, i ^ bit) for i in range(size)])]
    pallas_call x0 -> x8, Pallas kernels: none -> 50.8 us  [products(): pl.pallas_call(product_kernel, grid_spec=grid_spec, out_shape=[jax.ShapeD...]
    unnamed x7 -> x16, local copies, waits for them, and re-layouts: 46.8 us -> 9.07 us
    mul x2 -> x0, other arithmetic: 34.3 us -> none  [apply_mask(): blocks = blocks * mask.astype(jnp.bfloat16)[:, None, :, None]]
    all_gather x1 -> x0, waiting for transfers between devices: 30.6 us -> none  [local(): whole = lax.all_gather(tokens, 'tensor', axis=1, tiled=True)]
  transfers between devices with their start and end apart: 5 -> 46, of which waited for: 4 -> 18; matrix products, arithmetic and copies ran while one was open for 34% -> 9% of each run, Pallas kernels for 0% -> 17%
where the time goes in v1:
time: 261 us; the launch traced here: 259 us
  waiting for transfers between devices  113 us (43%)
  starting transfers between devices  60.9 us (23%)
  Pallas kernels  50.8 us (19%)
  other arithmetic  21.5 us (8%)
  local copies, waits for them, and re-layouts  12.2 us (5%)
    ppermute x44, waiting for transfers between devices, exchange(): return lax.ppermute(value, axis, [(i, i ^ bit) for i in range(size)])  113 us
    ppermute x44, starting transfers between devices, exchange(): return lax.ppermute(value, axis, [(i, i ^ bit) for i in range(size)])  54.5 us
    pallas_call x8, Pallas kernels, products(): pl.pallas_call(product_kernel, grid_spec=grid_spec, out_shape=[jax.ShapeD...  50.8 us
    unnamed x16, local copies, waits for them, and re-layouts  9.07 us
    convert_element_type x8, other arithmetic, local(): (own[pairs:] + from_core[pairs:].astype(jnp.float32)).astype(jnp.bfloat16)  6.79 us
    convert_element_type x8, other arithmetic, local(): to_far = (own[p] + from_core[p].astype(jnp.float32) + from_pair[p].astype...  6.34 us
    ppermute x1, starting transfers between devices, local(): b = lax.ppermute(theirs, ('wide', 'tensor'), second)  5.78 us
    add x8, other arithmetic, local(): total = total + value.astype(jnp.float32)  5.33 us
  transfers between devices with their start and end apart: 46, of which 18 were waited for; matrix products, arithmetic and copies ran while one was open for 9% of the time, Pallas kernels for 17%

profile of v1, /device:TPU:0, one launch (start us, length us, event | category | flops | bytes accessed | tf_op | source)
XLA Modules:
  0.0 259.2 jit_solution(17736662643230617573)
XLA Ops:
  1.7 5.8 %collective-permute-start.1 = (bf16[128,512]{1,0:T(8,128)(2,1)S(1)}, bf16[128,512]{1,0:T(8,128)(2,1)S(1)}, u32[]{:S(2)}, u32[]{:S(2)}) collective-permute-start(bf16[128,512]{1,0:T(8,128)(2,1)S(1)} %get-tuple-element.64), channel_id=1, source_target_pairs={{8,0},{0,1},{9,2},{1,3},{10,4},{2,5},{11,6},{3,7},{12,8},{4,9},{13... | collective-permute-start | bytes 393224 | tf_op jit(solution)/shard_map/ppermute | solution.py:94
  7.5 1.1 multiply_reduce_fusion
  8.5 2.6 %collective-permute-start.2 = (f32[1,128]{1,0:T(1,128)S(1)}, f32[1,128]{1,0:T(1,128)S(1)}, u32[]{:S(2)}, u32[]{:S(2)}) collective-permute-start(f32[1,128]{1,0:T(1,128)S(1)} %bitcast.213), channel_id=1, source_target_pairs={{0,1},{1,0},{2,3},{3,2},{4,5},{5,4},{6,7},{7,6},{8,9},{9,8},{10,11... | collective-permute-start | bytes 1544 | tf_op jit(solution)/shard_map/ppermute | solution.py:16
  11.2 1.5 collective-permute-done.2
  14.0 2.3 collective-permute-done.3
  16.2 1.6 collective-permute-start.4
  17.8 2.9 %collective-permute-done.4 = f32[1,128]{1,0:T(1,128)S(1)} collective-permute-done((f32[1,128]{1,0:T(1,128)S(1)}, f32[1,128]{1,0:T(1,128)S(1)}, u32[]{:S(2)}, u32[]{:S(2)}) %collective-permute-start.4) | collective-permute-done | bytes 544 | tf_op jit(solution)/shard_map/ppermute | solution.py:16
  23.1 5.8 %copy-done = bf16[512,16384]{1,0:T(8,128)(2,1)S(1)} copy-done((bf16[512,16384]{1,0:T(8,128)(2,1)S(1)}, bf16[512,16384]{1,0:T(8,128)(2,1)}, u32[]{:S(2)}) %copy-start) | copy-done | bytes 16777240
  28.8 6.6 %products.8 = (f32[8,2,128,256]{3,2,1,0:T(8,128)S(1)}, bf16[8,2,128,256]{3,2,1,0:T(8,128)(2,1)}) custom-call(s32[1]{0:T(128)} %bitcast.shard_ref, bf16[256,512]{1,0:T(8,128)(2,1)S(1)} %multiply_convert_fusion.x_ref, bf16[512,16384]{1,0:T(8,128)(2,1)S(1)} %copy-done, bf16[512,16384]{1,0:T(8,128)(2,1)} %up_ref.15, f32[8,16384]{1,0:T(8,128)S(1)} %reshape.176.gate_mask_ref, ...), custom_call_target="tpu_custom_call" | custom-call | flops 1073741824 | bytes 7340032 | tf_op jit(solution)/shard_map/products/pallas_call | solution.py:60
  35.4 1.3 copy-done.3
  37.3 6.6 %products.9 = (f32[8,2,128,256]{3,2,1,0:T(8,128)S(1)}, bf16[8,2,128,256]{3,2,1,0:T(8,128)(2,1)}) custom-call(s32[1]{0:T(128)} %bitcast.shard_ref, bf16[256,512]{1,0:T(8,128)(2,1)S(1)} %multiply_convert_fusion.x_ref, bf16[512,16384]{1,0:T(8,128)(2,1)S(1)} %copy-done, bf16[512,16384]{1,0:T(8,128)(2,1)} %up_ref.15, f32[8,16384]{1,0:T(8,128)S(1)} %reshape.176.gate_mask_ref, ...), custom_call_target="tpu_custom_call" | custom-call | flops 1073741824 | bytes 7340032 | tf_op jit(solution)/shard_map/products/pallas_call | solution.py:60
  43.9 6.8 %products.10 = (f32[8,2,128,256]{3,2,1,0:T(8,128)S(1)}, bf16[8,2,128,256]{3,2,1,0:T(8,128)(2,1)}) custom-call(s32[1]{0:T(128)} %bitcast.shard_ref, bf16[256,512]{1,0:T(8,128)(2,1)S(1)} %multiply_convert_fusion.x_ref, bf16[512,16384]{1,0:T(8,128)(2,1)S(1)} %copy-done, bf16[512,16384]{1,0:T(8,128)(2,1)} %up_ref.15, f32[8,16384]{1,0:T(8,128)S(1)} %reshape.176.gate_mask_ref, ...), custom_call_target="tpu_custom_call" | custom-call | flops 1073741824 | bytes 7340032 | tf_op jit(solution)/shard_map/products/pallas_call | solution.py:60
  51.3 6.6 %products.11 = (f32[8,2,128,256]{3,2,1,0:T(8,128)S(1)}, bf16[8,2,128,256]{3,2,1,0:T(8,128)(2,1)}) custom-call(s32[1]{0:T(128)} %bitcast.shard_ref, bf16[256,512]{1,0:T(8,128)(2,1)S(1)} %multiply_convert_fusion.x_ref, bf16[512,16384]{1,0:T(8,128)(2,1)S(1)} %copy-done, bf16[512,16384]{1,0:T(8,128)(2,1)} %up_ref.15, f32[8,16384]{1,0:T(8,128)S(1)} %reshape.176.gate_mask_ref, ...), custom_call_target="tpu_custom_call" | custom-call | flops 1073741824 | bytes 7340032 | tf_op jit(solution)/shard_map/products/pallas_call | solution.py:60
  57.9 6.6 %products.12 = (f32[8,2,128,256]{3,2,1,0:T(8,128)S(1)}, bf16[8,2,128,256]{3,2,1,0:T(8,128)(2,1)}) custom-call(s32[1]{0:T(128)} %bitcast.shard_ref, bf16[256,512]{1,0:T(8,128)(2,1)S(1)} %multiply_convert_fusion.x_ref, bf16[512,16384]{1,0:T(8,128)(2,1)S(1)} %copy-done, bf16[512,16384]{1,0:T(8,128)(2,1)} %up_ref.15, f32[8,16384]{1,0:T(8,128)S(1)} %reshape.176.gate_mask_ref, ...), custom_call_target="tpu_custom_call" | custom-call | flops 1073741824 | bytes 7340032 | tf_op jit(solution)/shard_map/products/pallas_call | solution.py:60
  64.6 5.8 %products.13 = (f32[8,2,128,256]{3,2,1,0:T(8,128)S(1)}, bf16[8,2,128,256]{3,2,1,0:T(8,128)(2,1)S(1)}) custom-call(s32[1]{0:T(128)} %bitcast.shard_ref, bf16[256,512]{1,0:T(8,128)(2,1)S(1)} %multiply_convert_fusion.x_ref, bf16[512,16384]{1,0:T(8,128)(2,1)S(1)} %copy-done, bf16[512,16384]{1,0:T(8,128)(2,1)} %up_ref.15, f32[8,16384]{1,0:T(8,128)S(1)} %reshape.176.gate_mask_ref, ...), custom_call_target="tpu_custom_call" | custom-call | flops 1073741824 | bytes 7340032 | tf_op jit(solution)/shard_map/products/pallas_call | solution.py:60
  71.8 5.8 %products.14 = (f32[8,2,128,256]{3,2,1,0:T(8,128)S(1)}, bf16[8,2,128,256]{3,2,1,0:T(8,128)(2,1)S(1)}) custom-call(s32[1]{0:T(128)} %bitcast.shard_ref, bf16[256,512]{1,0:T(8,128)(2,1)S(1)} %multiply_convert_fusion.x_ref, bf16[512,16384]{1,0:T(8,128)(2,1)S(1)} %copy-done, bf16[512,16384]{1,0:T(8,128)(2,1)} %up_ref.15, f32[8,16384]{1,0:T(8,128)S(1)} %reshape.176.gate_mask_ref, ...), custom_call_target="tpu_custom_call" | custom-call | flops 1073741824 | bytes 7340032 | tf_op jit(solution)/shard_map/products/pallas_call | solution.py:60
  78.6 5.8 %products.15 = (f32[8,2,128,256]{3,2,1,0:T(8,128)S(1)}, bf16[8,2,128,256]{3,2,1,0:T(8,128)(2,1)S(1)}) custom-call(s32[1]{0:T(128)} %bitcast.shard_ref, bf16[256,512]{1,0:T(8,128)(2,1)S(1)} %multiply_convert_fusion.x_ref, bf16[512,16384]{1,0:T(8,128)(2,1)S(1)} %copy-done, bf16[512,16384]{1,0:T(8,128)(2,1)} %up_ref.15, f32[8,16384]{1,0:T(8,128)S(1)} %reshape.176.gate_mask_ref, ...), custom_call_target="tpu_custom_call" | custom-call | flops 1073741824 | bytes 7340032 | tf_op jit(solution)/shard_map/products/pallas_call | solution.py:60
  84.5 1.6 add_convert_fusion.7
  86.6 1.2 add_convert_fusion.6
  88.0 1.2 add_convert_fusion.5
  89.2 2.1 collective-permute-start.7
  91.3 1.2 add_convert_fusion.4
  92.5 1.2 add_convert_fusion.3
  93.8 2.1 collective-permute-start.17
  96.3 2.1 collective-permute-start.27
  98.5 5.6 %collective-permute-done.7 = bf16[4,2,128,256]{3,2,1,0:T(8,128)(2,1)S(1)} collective-permute-done((bf16[4,2,128,256]{3,2,1,0:T(8,128)(2,1)S(1)}, bf16[4,2,128,256]{3,2,1,0:T(8,128)(2,1)S(1)}, u32[]{:S(2)}, u32[]{:S(2)}) %collective-permute-start.7) | collective-permute-done | bytes 524320 | tf_op jit(solution)/shard_map/ppermute | solution.py:16
  104.0 2.0 collective-permute-start.32
  106.0 1.2 fusion.16
  107.2 8.1 %collective-permute-done.12 = bf16[4,2,128,256]{3,2,1,0:T(8,128)(2,1)S(1)} collective-permute-done((bf16[4,2,128,256]{3,2,1,0:T(8,128)(2,1)S(1)}, bf16[4,2,128,256]{3,2,1,0:T(8,128)(2,1)S(1)}, u32[]{:S(2)}, u32[]{:S(2)}) %collective-permute-start.12) | collective-permute-done | bytes 524320 | tf_op jit(solution)/shard_map/ppermute | solution.py:16
  115.3 2.0 collective-permute-start.37
  117.2 1.2 fusion.19
  118.4 8.1 %collective-permute-done.17 = bf16[4,2,128,256]{3,2,1,0:T(8,128)(2,1)S(1)} collective-permute-done((bf16[4,2,128,256]{3,2,1,0:T(8,128)(2,1)S(1)}, bf16[4,2,128,256]{3,2,1,0:T(8,128)(2,1)S(1)}, u32[]{:S(2)}, u32[]{:S(2)}) %collective-permute-start.17) | collective-permute-done | bytes 524320 | tf_op jit(solution)/shard_map/ppermute | solution.py:16
  126.5 2.0 collective-permute-start.42
  128.5 1.2 fusion.22
  129.6 8.1 %collective-permute-done.22 = bf16[4,2,128,256]{3,2,1,0:T(8,128)(2,1)S(1)} collective-permute-done((bf16[4,2,128,256]{3,2,1,0:T(8,128)(2,1)S(1)}, bf16[4,2,128,256]{3,2,1,0:T(8,128)(2,1)S(1)}, u32[]{:S(2)}, u32[]{:S(2)}) %collective-permute-start.22) | collective-permute-done | bytes 524320 | tf_op jit(solution)/shard_map/ppermute | solution.py:16
  137.7 1.1 collective-permute-start.10
  138.8 1.2 fusion.25
  140.0 9.0 %collective-permute-done.27 = bf16[4,2,128,256]{3,2,1,0:T(8,128)(2,1)S(1)} collective-permute-done((bf16[4,2,128,256]{3,2,1,0:T(8,128)(2,1)S(1)}, bf16[4,2,128,256]{3,2,1,0:T(8,128)(2,1)S(1)}, u32[]{:S(2)}, u32[]{:S(2)}) %collective-permute-start.27) | collective-permute-done | bytes 524320 | tf_op jit(solution)/shard_map/ppermute | solution.py:16
  149.0 1.5 collective-permute-start.9
  150.5 1.2 fusion.28
  151.7 8.5 %collective-permute-done.32 = bf16[4,2,128,256]{3,2,1,0:T(8,128)(2,1)S(1)} collective-permute-done((bf16[4,2,128,256]{3,2,1,0:T(8,128)(2,1)S(1)}, bf16[4,2,128,256]{3,2,1,0:T(8,128)(2,1)S(1)}, u32[]{:S(2)}, u32[]{:S(2)}) %collective-permute-start.32) | collective-permute-done | bytes 524320 | tf_op jit(solution)/shard_map/ppermute | solution.py:16
  160.8 10.6 %collective-permute-done.37 = bf16[4,2,128,256]{3,2,1,0:T(8,128)(2,1)S(1)} collective-permute-done((bf16[4,2,128,256]{3,2,1,0:T(8,128)(2,1)S(1)}, bf16[4,2,128,256]{3,2,1,0:T(8,128)(2,1)S(1)}, u32[]{:S(2)}, u32[]{:S(2)}) %collective-permute-start.37) | collective-permute-done | bytes 524320 | tf_op jit(solution)/shard_map/ppermute | solution.py:16
  171.4 1.1 collective-permute-start.15
  172.7 9.7 %collective-permute-done.42 = bf16[4,2,128,256]{3,2,1,0:T(8,128)(2,1)S(1)} collective-permute-done((bf16[4,2,128,256]{3,2,1,0:T(8,128)(2,1)S(1)}, bf16[4,2,128,256]{3,2,1,0:T(8,128)(2,1)S(1)}, u32[]{:S(2)}, u32[]{:S(2)}) %collective-permute-start.42) | collective-permute-done | bytes 524320 | tf_op jit(solution)/shard_map/ppermute | solution.py:16
  182.4 1.3 collective-permute-start.14
  184.1 2.9 %collective-permute-start.20 = (bf16[2,128,256]{2,1,0:T(8,128)(2,1)S(1)}, bf16[2,128,256]{2,1,0:T(8,128)(2,1)S(1)}, u32[]{:S(2)}, u32[]{:S(2)}) collective-permute-start(bf16[2,128,256]{2,1,0:T(8,128)(2,1)S(1)} %get-tuple-element.53), channel_id=1, source_target_pairs={{0,6},{1,7},{2,4},{3,5},{4,2},{5,3},{6,0},{7,1},{8,14},{9,15},{10,... | collective-permute-start | bytes 393224 | tf_op jit(solution)/shard_map/ppermute | solution.py:16
  188.5 1.1 collective-permute-start.18
  189.6 6.2 %collective-permute-done.14 = bf16[2,128,256]{2,1,0:T(8,128)(2,1)S(1)} collective-permute-done((bf16[2,128,256]{2,1,0:T(8,128)(2,1)S(1)}, bf16[2,128,256]{2,1,0:T(8,128)(2,1)S(1)}, u32[]{:S(2)}, u32[]{:S(2)}) %collective-permute-start.14) | collective-permute-done | bytes 131104 | tf_op jit(solution)/shard_map/ppermute | solution.py:16
  196.9 6.9 %collective-permute-start.23 = (bf16[2,128,256]{2,1,0:T(8,128)(2,1)S(1)}, bf16[2,128,256]{2,1,0:T(8,128)(2,1)S(1)}, u32[]{:S(2)}, u32[]{:S(2)}) collective-permute-start(bf16[2,128,256]{2,1,0:T(8,128)(2,1)S(1)} %get-tuple-element.49), channel_id=1, source_target_pairs={{0,2},{1,3},{2,0},{3,1},{4,6},{5,7},{6,4},{7,5},{8,10},{9,11},{10,... | collective-permute-start | bytes 393224 | tf_op jit(solution)/shard_map/ppermute | solution.py:16
  203.8 4.2 %collective-permute-done.19 = bf16[2,128,256]{2,1,0:T(8,128)(2,1)S(1)} collective-permute-done((bf16[2,128,256]{2,1,0:T(8,128)(2,1)S(1)}, bf16[2,128,256]{2,1,0:T(8,128)(2,1)S(1)}, u32[]{:S(2)}, u32[]{:S(2)}) %collective-permute-start.19) | collective-permute-done | bytes 131104 | tf_op jit(solution)/shard_map/ppermute | solution.py:16
  207.9 2.3 collective-permute-start.30
  211.3 2.1 collective-permute-start.28
  213.4 5.7 %collective-permute-done.24 = bf16[2,128,256]{2,1,0:T(8,128)(2,1)S(1)} collective-permute-done((bf16[2,128,256]{2,1,0:T(8,128)(2,1)S(1)}, bf16[2,128,256]{2,1,0:T(8,128)(2,1)S(1)}, u32[]{:S(2)}, u32[]{:S(2)}) %collective-permute-start.24) | collective-permute-done | bytes 131104 | tf_op jit(solution)/shard_map/ppermute | solution.py:16
  219.1 2.4 collective-permute-start.35
  221.6 1.0 fusion.9
  222.6 2.1 collective-permute-start.33
  224.7 5.7 %collective-permute-done.29 = bf16[2,128,256]{2,1,0:T(8,128)(2,1)S(1)} collective-permute-done((bf16[2,128,256]{2,1,0:T(8,128)(2,1)S(1)}, bf16[2,128,256]{2,1,0:T(8,128)(2,1)S(1)}, u32[]{:S(2)}, u32[]{:S(2)}) %collective-permute-start.29) | collective-permute-done | bytes 131104 | tf_op jit(solution)/shard_map/ppermute | solution.py:16
  230.4 2.4 collective-permute-start.40
  233.9 2.0 collective-permute-start.38
  235.9 5.7 %collective-permute-done.34 = bf16[2,128,256]{2,1,0:T(8,128)(2,1)S(1)} collective-permute-done((bf16[2,128,256]{2,1,0:T(8,128)(2,1)S(1)}, bf16[2,128,256]{2,1,0:T(8,128)(2,1)S(1)}, u32[]{:S(2)}, u32[]{:S(2)}) %collective-permute-start.34) | collective-permute-done | bytes 131104 | tf_op jit(solution)/shard_map/ppermute | solution.py:16
  241.6 2.5 collective-permute-start.45
  244.3 2.5 collective-permute-start.43
  246.8 6.1 %collective-permute-done.39 = bf16[2,128,256]{2,1,0:T(8,128)(2,1)S(1)} collective-permute-done((bf16[2,128,256]{2,1,0:T(8,128)(2,1)S(1)}, bf16[2,128,256]{2,1,0:T(8,128)(2,1)S(1)}, u32[]{:S(2)}, u32[]{:S(2)}) %collective-permute-start.39) | collective-permute-done | bytes 131104 | tf_op jit(solution)/shard_map/ppermute | solution.py:16
  253.0 5.3 %collective-permute-done.44 = bf16[2,128,256]{2,1,0:T(8,128)(2,1)S(1)} collective-permute-done((bf16[2,128,256]{2,1,0:T(8,128)(2,1)S(1)}, bf16[2,128,256]{2,1,0:T(8,128)(2,1)S(1)}, u32[]{:S(2)}, u32[]{:S(2)}) %collective-permute-start.44) | collective-permute-done | bytes 131104 | tf_op jit(solution)/shard_map/ppermute | solution.py:16
  (98 shorter events, 17.0 us)
Async XLA Ops:
  1.0 21.9 %collective-permute-start = (bf16[128,512]{1,0:T(8,128)(2,1)S(1)}, bf16[128,512]{1,0:T(8,128)(2,1)S(1)}, u32[]{:S(2)}, u32[]{:S(2)}) collective-permute-start(bf16[128,512]{1,0:T(8,128)(2,1)S(1)} %get-tuple-element.63), channel_id=1, source_target_pairs={{0,0},{8,1},{1,2},{9,3},{2,4},{10,5},{3,6},{11,7},{4,8},{12,9},{5,... | collective-permute-start | bytes 393224 | tf_op jit(solution)/shard_map/ppermute | solution.py:93
  1.7 21.2 %collective-permute-start.1 = (bf16[128,512]{1,0:T(8,128)(2,1)S(1)}, bf16[128,512]{1,0:T(8,128)(2,1)S(1)}, u32[]{:S(2)}, u32[]{:S(2)}) collective-permute-start(bf16[128,512]{1,0:T(8,128)(2,1)S(1)} %get-tuple-element.64), channel_id=1, source_target_pairs={{8,0},{0,1},{9,2},{1,3},{10,4},{2,5},{11,6},{3,7},{12,8},{4,9},{13... | collective-permute-start | bytes 393224 | tf_op jit(solution)/shard_map/ppermute | solution.py:94
  8.5 4.2 %collective-permute-start.2 = (f32[1,128]{1,0:T(1,128)S(1)}, f32[1,128]{1,0:T(1,128)S(1)}, u32[]{:S(2)}, u32[]{:S(2)}) collective-permute-start(f32[1,128]{1,0:T(1,128)S(1)} %bitcast.213), channel_id=1, source_target_pairs={{0,1},{1,0},{2,3},{3,2},{4,5},{5,4},{6,7},{7,6},{8,9},{9,8},{10,11... | collective-permute-start | bytes 1544 | tf_op jit(solution)/shard_map/ppermute | solution.py:16
  12.7 3.5 %collective-permute-start.3 = (f32[1,128]{1,0:T(1,128)S(1)}, f32[1,128]{1,0:T(1,128)S(1)}, u32[]{:S(2)}, u32[]{:S(2)}) collective-permute-start(f32[1,128]{1,0:T(1,128)S(1)} %bitcast_add_fusion.8), channel_id=1, source_target_pairs={{0,2},{1,3},{2,0},{3,1},{4,6},{5,7},{6,4},{7,5},{8,10},{9,11},{10,... | collective-permute-start | bytes 1544 | tf_op jit(solution)/shard_map/ppermute | solution.py:16
  16.2 4.4 %collective-permute-start.4 = (f32[1,128]{1,0:T(1,128)S(1)}, f32[1,128]{1,0:T(1,128)S(1)}, u32[]{:S(2)}, u32[]{:S(2)}) collective-permute-start(f32[1,128]{1,0:T(1,128)S(1)} %add.433), channel_id=1, source_target_pairs={{0,4},{1,5},{2,6},{3,7},{4,0},{5,1},{6,2},{7,3},{8,12},{9,13},{10,... | collective-permute-start | bytes 1544 | tf_op jit(solution)/shard_map/ppermute | solution.py:16
  20.7 2.2 collective-permute-start.5
  23.1 5.8 %copy-start = (bf16[512,16384]{1,0:T(8,128)(2,1)S(1)}, bf16[512,16384]{1,0:T(8,128)(2,1)}, u32[]{:S(2)}) copy-start(bf16[512,16384]{1,0:T(8,128)(2,1)} %gate_ref.15) | copy-start | bytes 50331652
  35.4 1.3 copy-start.3
  36.8 47.6 %collective-permute-start.6 = (bf16[8,2,128,256]{3,2,1,0:T(8,128)(2,1)}, bf16[8,2,128,256]{3,2,1,0:T(8,128)(2,1)}, u32[]{:S(2)}, u32[]{:S(2)}) collective-permute-start(bf16[8,2,128,256]{3,2,1,0:T(8,128)(2,1)} %get-tuple-element.22), channel_id=1, source_target_pairs={{0,8},{8,0},{1,9},{9,1},{2,10},{10,2},{3,11},{11,3},{4,12},{12,4},... | collective-permute-start | bytes 3145736 | tf_op jit(solution)/shard_map/ppermute | solution.py:16
  43.9 6.9 %copy-start.1 = (f32[8,2,128,256]{3,2,1,0:T(8,128)}, f32[8,2,128,256]{3,2,1,0:T(8,128)S(1)}, u32[]{:S(2)}) copy-start(f32[8,2,128,256]{3,2,1,0:T(8,128)S(1)} %get-tuple-element.23) | copy-start | bytes 6291460
  43.9 42.2 %collective-permute-start.11 = (bf16[8,2,128,256]{3,2,1,0:T(8,128)(2,1)}, bf16[8,2,128,256]{3,2,1,0:T(8,128)(2,1)}, u32[]{:S(2)}, u32[]{:S(2)}) collective-permute-start(bf16[8,2,128,256]{3,2,1,0:T(8,128)(2,1)} %get-tuple-element.24), channel_id=1, source_target_pairs={{0,8},{8,0},{1,9},{9,1},{2,10},{10,2},{3,11},{11,3},{4,12},{12,4},... | collective-permute-start | bytes 3145736 | tf_op jit(solution)/shard_map/ppermute | solution.py:16
  50.8 37.0 %collective-permute-start.16 = (bf16[8,2,128,256]{3,2,1,0:T(8,128)(2,1)}, bf16[8,2,128,256]{3,2,1,0:T(8,128)(2,1)}, u32[]{:S(2)}, u32[]{:S(2)}) collective-permute-start(bf16[8,2,128,256]{3,2,1,0:T(8,128)(2,1)} %get-tuple-element.26), channel_id=1, source_target_pairs={{0,8},{8,0},{1,9},{9,1},{2,10},{10,2},{3,11},{11,3},{4,12},{12,4},... | collective-permute-start | bytes 3145736 | tf_op jit(solution)/shard_map/ppermute | solution.py:16
  57.9 31.3 %collective-permute-start.21 = (bf16[8,2,128,256]{3,2,1,0:T(8,128)(2,1)}, bf16[8,2,128,256]{3,2,1,0:T(8,128)(2,1)}, u32[]{:S(2)}, u32[]{:S(2)}) collective-permute-start(bf16[8,2,128,256]{3,2,1,0:T(8,128)(2,1)} %get-tuple-element.28), channel_id=1, source_target_pairs={{0,8},{8,0},{1,9},{9,1},{2,10},{10,2},{3,11},{11,3},{4,12},{12,4},... | collective-permute-start | bytes 3145736 | tf_op jit(solution)/shard_map/ppermute | solution.py:16
  70.4 1.0 copy-start.6
  71.4 21.1 %collective-permute-start.26 = (bf16[8,2,128,256]{3,2,1,0:T(8,128)(2,1)}, bf16[8,2,128,256]{3,2,1,0:T(8,128)(2,1)}, u32[]{:S(2)}, u32[]{:S(2)}) collective-permute-start(bf16[8,2,128,256]{3,2,1,0:T(8,128)(2,1)} %get-tuple-element.30), channel_id=1, source_target_pairs={{0,8},{8,0},{1,9},{9,1},{2,10},{10,2},{3,11},{11,3},{4,12},{12,4},... | collective-permute-start | bytes 3145736 | tf_op jit(solution)/shard_map/ppermute | solution.py:16
  77.6 1.0 copy-start.5
  84.4 2.2 copy-start.2
  84.4 9.3 %collective-permute-start.31 = (bf16[8,2,128,256]{3,2,1,0:T(8,128)(2,1)}, bf16[8,2,128,256]{3,2,1,0:T(8,128)(2,1)S(1)}, u32[]{:S(2)}, u32[]{:S(2)}) collective-permute-start(bf16[8,2,128,256]{3,2,1,0:T(8,128)(2,1)} %copy-done.6), channel_id=1, source_target_pairs={{0,8},{8,0},{1,9},{9,1},{2,10},{10,2},{3,11},{11,3},{4,12},{12,4},... | collective-permute-start | bytes 3145736 | tf_op jit(solution)/shard_map/ppermute | solution.py:16
  86.2 9.8 %collective-permute-start.36 = (bf16[8,2,128,256]{3,2,1,0:T(8,128)(2,1)}, bf16[8,2,128,256]{3,2,1,0:T(8,128)(2,1)S(1)}, u32[]{:S(2)}, u32[]{:S(2)}) collective-permute-start(bf16[8,2,128,256]{3,2,1,0:T(8,128)(2,1)} %copy-done.5), channel_id=1, source_target_pairs={{0,8},{8,0},{1,9},{9,1},{2,10},{10,2},{3,11},{11,3},{4,12},{12,4},... | collective-permute-start | bytes 3145736 | tf_op jit(solution)/shard_map/ppermute | solution.py:16
  87.8 8.4 %collective-permute-start.41 = (bf16[8,2,128,256]{3,2,1,0:T(8,128)(2,1)S(1)}, bf16[8,2,128,256]{3,2,1,0:T(8,128)(2,1)S(1)}, u32[]{:S(2)}, u32[]{:S(2)}) collective-permute-start(bf16[8,2,128,256]{3,2,1,0:T(8,128)(2,1)S(1)} %get-tuple-element.36), channel_id=1, source_target_pairs={{0,8},{8,0},{1,9},{9,1},{2,10},{10,2},{3,11},{11,3},{4,12},{12,4},... | collective-permute-start | bytes 3145736 | tf_op jit(solution)/shard_map/ppermute | solution.py:16
  89.2 14.9 %collective-permute-start.7 = (bf16[4,2,128,256]{3,2,1,0:T(8,128)(2,1)S(1)}, bf16[4,2,128,256]{3,2,1,0:T(8,128)(2,1)S(1)}, u32[]{:S(2)}, u32[]{:S(2)}) collective-permute-start(bf16[4,2,128,256]{3,2,1,0:T(8,128)(2,1)S(1)} %add_convert_fusion.7), channel_id=1, source_target_pairs={{0,1},{1,0},{2,3},{3,2},{4,5},{5,4},{6,7},{7,6},{8,9},{9,8},{10,11... | collective-permute-start | bytes 1572872 | tf_op jit(solution)/shard_map/ppermute | solution.py:16
  92.5 22.8 %collective-permute-start.12 = (bf16[4,2,128,256]{3,2,1,0:T(8,128)(2,1)S(1)}, bf16[4,2,128,256]{3,2,1,0:T(8,128)(2,1)S(1)}, u32[]{:S(2)}, u32[]{:S(2)}) collective-permute-start(bf16[4,2,128,256]{3,2,1,0:T(8,128)(2,1)S(1)} %add_convert_fusion.6), channel_id=1, source_target_pairs={{0,1},{1,0},{2,3},{3,2},{4,5},{5,4},{6,7},{7,6},{8,9},{9,8},{10,11... | collective-permute-start | bytes 1572872 | tf_op jit(solution)/shard_map/ppermute | solution.py:16
  93.8 32.7 %collective-permute-start.17 = (bf16[4,2,128,256]{3,2,1,0:T(8,128)(2,1)S(1)}, bf16[4,2,128,256]{3,2,1,0:T(8,128)(2,1)S(1)}, u32[]{:S(2)}, u32[]{:S(2)}) collective-permute-start(bf16[4,2,128,256]{3,2,1,0:T(8,128)(2,1)S(1)} %add_convert_fusion.5), channel_id=1, source_target_pairs={{0,1},{1,0},{2,3},{3,2},{4,5},{5,4},{6,7},{7,6},{8,9},{9,8},{10,11... | collective-permute-start | bytes 1572872 | tf_op jit(solution)/shard_map/ppermute | solution.py:16
  96.0 41.7 %collective-permute-start.22 = (bf16[4,2,128,256]{3,2,1,0:T(8,128)(2,1)S(1)}, bf16[4,2,128,256]{3,2,1,0:T(8,128)(2,1)S(1)}, u32[]{:S(2)}, u32[]{:S(2)}) collective-permute-start(bf16[4,2,128,256]{3,2,1,0:T(8,128)(2,1)S(1)} %add_convert_fusion.4), channel_id=1, source_target_pairs={{0,1},{1,0},{2,3},{3,2},{4,5},{5,4},{6,7},{7,6},{8,9},{9,8},{10,11... | collective-permute-start | bytes 1572872 | tf_op jit(solution)/shard_map/ppermute | solution.py:16
  96.1 9.9 %copy-start.4 = (f32[8,2,128,256]{3,2,1,0:T(8,128)S(1)}, f32[8,2,128,256]{3,2,1,0:T(8,128)}, u32[]{:S(2)}) copy-start(f32[8,2,128,256]{3,2,1,0:T(8,128)} %copy-done.3) | copy-start | bytes 6291460
  96.3 52.7 %collective-permute-start.27 = (bf16[4,2,128,256]{3,2,1,0:T(8,128)(2,1)S(1)}, bf16[4,2,128,256]{3,2,1,0:T(8,128)(2,1)S(1)}, u32[]{:S(2)}, u32[]{:S(2)}) collective-permute-start(bf16[4,2,128,256]{3,2,1,0:T(8,128)(2,1)S(1)} %add_convert_fusion.3), channel_id=1, source_target_pairs={{0,1},{1,0},{2,3},{3,2},{4,5},{5,4},{6,7},{7,6},{8,9},{9,8},{10,11... | collective-permute-start | bytes 1572872 | tf_op jit(solution)/shard_map/ppermute | solution.py:16
  104.0 56.2 %collective-permute-start.32 = (bf16[4,2,128,256]{3,2,1,0:T(8,128)(2,1)S(1)}, bf16[4,2,128,256]{3,2,1,0:T(8,128)(2,1)S(1)}, u32[]{:S(2)}, u32[]{:S(2)}) collective-permute-start(bf16[4,2,128,256]{3,2,1,0:T(8,128)(2,1)S(1)} %add_convert_fusion.2), channel_id=1, source_target_pairs={{0,1},{1,0},{2,3},{3,2},{4,5},{5,4},{6,7},{7,6},{8,9},{9,8},{10,11... | collective-permute-start | bytes 1572872 | tf_op jit(solution)/shard_map/ppermute | solution.py:16
  115.3 56.2 %collective-permute-start.37 = (bf16[4,2,128,256]{3,2,1,0:T(8,128)(2,1)S(1)}, bf16[4,2,128,256]{3,2,1,0:T(8,128)(2,1)S(1)}, u32[]{:S(2)}, u32[]{:S(2)}) collective-permute-start(bf16[4,2,128,256]{3,2,1,0:T(8,128)(2,1)S(1)} %add_convert_fusion.1), channel_id=1, source_target_pairs={{0,1},{1,0},{2,3},{3,2},{4,5},{5,4},{6,7},{7,6},{8,9},{9,8},{10,11... | collective-permute-start | bytes 1572872 | tf_op jit(solution)/shard_map/ppermute | solution.py:16
  126.5 55.9 %collective-permute-start.42 = (bf16[4,2,128,256]{3,2,1,0:T(8,128)(2,1)S(1)}, bf16[4,2,128,256]{3,2,1,0:T(8,128)(2,1)S(1)}, u32[]{:S(2)}, u32[]{:S(2)}) collective-permute-start(bf16[4,2,128,256]{3,2,1,0:T(8,128)(2,1)S(1)} %add_convert_fusion), channel_id=1, source_target_pairs={{0,1},{1,0},{2,3},{3,2},{4,5},{5,4},{6,7},{7,6},{8,9},{9,8},{10,11... | collective-permute-start | bytes 1572872 | tf_op jit(solution)/shard_map/ppermute | solution.py:16
  137.7 46.1 %collective-permute-start.10 = (bf16[2,128,256]{2,1,0:T(8,128)(2,1)S(1)}, bf16[2,128,256]{2,1,0:T(8,128)(2,1)S(1)}, u32[]{:S(2)}, u32[]{:S(2)}) collective-permute-start(bf16[2,128,256]{2,1,0:T(8,128)(2,1)S(1)} %get-tuple-element.59), channel_id=1, source_target_pairs={{0,6},{1,7},{2,4},{3,5},{4,2},{5,3},{6,0},{7,1},{8,14},{9,15},{10,... | collective-permute-start | bytes 393224 | tf_op jit(solution)/shard_map/ppermute | solution.py:16
  149.0 35.1 %collective-permute-start.9 = (bf16[2,128,256]{2,1,0:T(8,128)(2,1)S(1)}, bf16[2,128,256]{2,1,0:T(8,128)(2,1)S(1)}, u32[]{:S(2)}, u32[]{:S(2)}) collective-permute-start(bf16[2,128,256]{2,1,0:T(8,128)(2,1)S(1)} %get-tuple-element.60), channel_id=1, source_target_pairs={{0,4},{1,5},{2,6},{3,7},{4,0},{5,1},{6,2},{7,3},{8,12},{9,13},{10,... | collective-permute-start | bytes 393224 | tf_op jit(solution)/shard_map/ppermute | solution.py:16
  160.2 26.8 %collective-permute-start.8 = (bf16[2,128,256]{2,1,0:T(8,128)(2,1)S(1)}, bf16[2,128,256]{2,1,0:T(8,128)(2,1)S(1)}, u32[]{:S(2)}, u32[]{:S(2)}) collective-permute-start(bf16[2,128,256]{2,1,0:T(8,128)(2,1)S(1)} %get-tuple-element.58), channel_id=1, source_target_pairs={{0,2},{1,3},{2,0},{3,1},{4,6},{5,7},{6,4},{7,5},{8,10},{9,11},{10,... | collective-permute-start | bytes 393224 | tf_op jit(solution)/shard_map/ppermute | solution.py:16
  171.4 17.1 %collective-permute-start.15 = (bf16[2,128,256]{2,1,0:T(8,128)(2,1)S(1)}, bf16[2,128,256]{2,1,0:T(8,128)(2,1)S(1)}, u32[]{:S(2)}, u32[]{:S(2)}) collective-permute-start(bf16[2,128,256]{2,1,0:T(8,128)(2,1)S(1)} %get-tuple-element.56), channel_id=1, source_target_pairs={{0,6},{1,7},{2,4},{3,5},{4,2},{5,3},{6,0},{7,1},{8,14},{9,15},{10,... | collective-permute-start | bytes 393224 | tf_op jit(solution)/shard_map/ppermute | solution.py:16
  182.4 13.4 %collective-permute-start.14 = (bf16[2,128,256]{2,1,0:T(8,128)(2,1)S(1)}, bf16[2,128,256]{2,1,0:T(8,128)(2,1)S(1)}, u32[]{:S(2)}, u32[]{:S(2)}) collective-permute-start(bf16[2,128,256]{2,1,0:T(8,128)(2,1)S(1)} %get-tuple-element.57), channel_id=1, source_target_pairs={{0,4},{1,5},{2,6},{3,7},{4,0},{5,1},{6,2},{7,3},{8,12},{9,13},{10,... | collective-permute-start | bytes 393224 | tf_op jit(solution)/shard_map/ppermute | solution.py:16
  183.9 11.9 %collective-permute-start.13 = (bf16[2,128,256]{2,1,0:T(8,128)(2,1)S(1)}, bf16[2,128,256]{2,1,0:T(8,128)(2,1)S(1)}, u32[]{:S(2)}, u32[]{:S(2)}) collective-permute-start(bf16[2,128,256]{2,1,0:T(8,128)(2,1)S(1)} %get-tuple-element.55), channel_id=1, source_target_pairs={{0,2},{1,3},{2,0},{3,1},{4,6},{5,7},{6,4},{7,5},{8,10},{9,11},{10,... | collective-permute-start | bytes 393224 | tf_op jit(solution)/shard_map/ppermute | solution.py:16
  184.1 12.8 %collective-permute-start.20 = (bf16[2,128,256]{2,1,0:T(8,128)(2,1)S(1)}, bf16[2,128,256]{2,1,0:T(8,128)(2,1)S(1)}, u32[]{:S(2)}, u32[]{:S(2)}) collective-permute-start(bf16[2,128,256]{2,1,0:T(8,128)(2,1)S(1)} %get-tuple-element.53), channel_id=1, source_target_pairs={{0,6},{1,7},{2,4},{3,5},{4,2},{5,3},{6,0},{7,1},{8,14},{9,15},{10,... | collective-permute-start | bytes 393224 | tf_op jit(solution)/shard_map/ppermute | solution.py:16
  187.0 20.9 %collective-permute-start.19 = (bf16[2,128,256]{2,1,0:T(8,128)(2,1)S(1)}, bf16[2,128,256]{2,1,0:T(8,128)(2,1)S(1)}, u32[]{:S(2)}, u32[]{:S(2)}) collective-permute-start(bf16[2,128,256]{2,1,0:T(8,128)(2,1)S(1)} %get-tuple-element.54), channel_id=1, source_target_pairs={{0,4},{1,5},{2,6},{3,7},{4,0},{5,1},{6,2},{7,3},{8,12},{9,13},{10,... | collective-permute-start | bytes 393224 | tf_op jit(solution)/shard_map/ppermute | solution.py:16
  188.5 21.8 %collective-permute-start.18 = (bf16[2,128,256]{2,1,0:T(8,128)(2,1)S(1)}, bf16[2,128,256]{2,1,0:T(8,128)(2,1)S(1)}, u32[]{:S(2)}, u32[]{:S(2)}) collective-permute-start(bf16[2,128,256]{2,1,0:T(8,128)(2,1)S(1)} %get-tuple-element.52), channel_id=1, source_target_pairs={{0,2},{1,3},{2,0},{3,1},{4,6},{5,7},{6,4},{7,5},{8,10},{9,11},{10,... | collective-permute-start | bytes 393224 | tf_op jit(solution)/shard_map/ppermute | solution.py:16
  195.8 15.5 %collective-permute-start.25 = (bf16[2,128,256]{2,1,0:T(8,128)(2,1)S(1)}, bf16[2,128,256]{2,1,0:T(8,128)(2,1)S(1)}, u32[]{:S(2)}, u32[]{:S(2)}) collective-permute-start(bf16[2,128,256]{2,1,0:T(8,128)(2,1)S(1)} %get-tuple-element.50), channel_id=1, source_target_pairs={{0,6},{1,7},{2,4},{3,5},{4,2},{5,3},{6,0},{7,1},{8,14},{9,15},{10,... | collective-permute-start | bytes 393224 | tf_op jit(solution)/shard_map/ppermute | solution.py:16
  195.8 23.4 %collective-permute-start.24 = (bf16[2,128,256]{2,1,0:T(8,128)(2,1)S(1)}, bf16[2,128,256]{2,1,0:T(8,128)(2,1)S(1)}, u32[]{:S(2)}, u32[]{:S(2)}) collective-permute-start(bf16[2,128,256]{2,1,0:T(8,128)(2,1)S(1)} %get-tuple-element.51), channel_id=1, source_target_pairs={{0,4},{1,5},{2,6},{3,7},{4,0},{5,1},{6,2},{7,3},{8,12},{9,13},{10,... | collective-permute-start | bytes 393224 | tf_op jit(solution)/shard_map/ppermute | solution.py:16
  196.9 24.7 %collective-permute-start.23 = (bf16[2,128,256]{2,1,0:T(8,128)(2,1)S(1)}, bf16[2,128,256]{2,1,0:T(8,128)(2,1)S(1)}, u32[]{:S(2)}, u32[]{:S(2)}) collective-permute-start(bf16[2,128,256]{2,1,0:T(8,128)(2,1)S(1)} %get-tuple-element.49), channel_id=1, source_target_pairs={{0,2},{1,3},{2,0},{3,1},{4,6},{5,7},{6,4},{7,5},{8,10},{9,11},{10,... | collective-permute-start | bytes 393224 | tf_op jit(solution)/shard_map/ppermute | solution.py:16
  207.9 14.7 %collective-permute-start.30 = (bf16[2,128,256]{2,1,0:T(8,128)(2,1)S(1)}, bf16[2,128,256]{2,1,0:T(8,128)(2,1)S(1)}, u32[]{:S(2)}, u32[]{:S(2)}) collective-permute-start(bf16[2,128,256]{2,1,0:T(8,128)(2,1)S(1)} %get-tuple-element.47), channel_id=1, source_target_pairs={{0,6},{1,7},{2,4},{3,5},{4,2},{5,3},{6,0},{7,1},{8,14},{9,15},{10,... | collective-permute-start | bytes 393224 | tf_op jit(solution)/shard_map/ppermute | solution.py:16
  210.3 20.1 %collective-permute-start.29 = (bf16[2,128,256]{2,1,0:T(8,128)(2,1)S(1)}, bf16[2,128,256]{2,1,0:T(8,128)(2,1)S(1)}, u32[]{:S(2)}, u32[]{:S(2)}) collective-permute-start(bf16[2,128,256]{2,1,0:T(8,128)(2,1)S(1)} %get-tuple-element.48), channel_id=1, source_target_pairs={{0,4},{1,5},{2,6},{3,7},{4,0},{5,1},{6,2},{7,3},{8,12},{9,13},{10,... | collective-permute-start | bytes 393224 | tf_op jit(solution)/shard_map/ppermute | solution.py:16
  211.3 21.5 %collective-permute-start.28 = (bf16[2,128,256]{2,1,0:T(8,128)(2,1)S(1)}, bf16[2,128,256]{2,1,0:T(8,128)(2,1)S(1)}, u32[]{:S(2)}, u32[]{:S(2)}) collective-permute-start(bf16[2,128,256]{2,1,0:T(8,128)(2,1)S(1)} %get-tuple-element.46), channel_id=1, source_target_pairs={{0,2},{1,3},{2,0},{3,1},{4,6},{5,7},{6,4},{7,5},{8,10},{9,11},{10,... | collective-permute-start | bytes 393224 | tf_op jit(solution)/shard_map/ppermute | solution.py:16
  219.1 14.7 %collective-permute-start.35 = (bf16[2,128,256]{2,1,0:T(8,128)(2,1)S(1)}, bf16[2,128,256]{2,1,0:T(8,128)(2,1)S(1)}, u32[]{:S(2)}, u32[]{:S(2)}) collective-permute-start(bf16[2,128,256]{2,1,0:T(8,128)(2,1)S(1)} %get-tuple-element.44), channel_id=1, source_target_pairs={{0,6},{1,7},{2,4},{3,5},{4,2},{5,3},{6,0},{7,1},{8,14},{9,15},{10,... | collective-permute-start | bytes 393224 | tf_op jit(solution)/shard_map/ppermute | solution.py:16
  221.5 20.1 %collective-permute-start.34 = (bf16[2,128,256]{2,1,0:T(8,128)(2,1)S(1)}, bf16[2,128,256]{2,1,0:T(8,128)(2,1)S(1)}, u32[]{:S(2)}, u32[]{:S(2)}) collective-permute-start(bf16[2,128,256]{2,1,0:T(8,128)(2,1)S(1)} %get-tuple-element.45), channel_id=1, source_target_pairs={{0,4},{1,5},{2,6},{3,7},{4,0},{5,1},{6,2},{7,3},{8,12},{9,13},{10,... | collective-permute-start | bytes 393224 | tf_op jit(solution)/shard_map/ppermute | solution.py:16
  222.6 21.5 %collective-permute-start.33 = (bf16[2,128,256]{2,1,0:T(8,128)(2,1)S(1)}, bf16[2,128,256]{2,1,0:T(8,128)(2,1)S(1)}, u32[]{:S(2)}, u32[]{:S(2)}) collective-permute-start(bf16[2,128,256]{2,1,0:T(8,128)(2,1)S(1)} %get-tuple-element.43), channel_id=1, source_target_pairs={{0,2},{1,3},{2,0},{3,1},{4,6},{5,7},{6,4},{7,5},{8,10},{9,11},{10,... | collective-permute-start | bytes 393224 | tf_op jit(solution)/shard_map/ppermute | solution.py:16
  230.4 13.9 %collective-permute-start.40 = (bf16[2,128,256]{2,1,0:T(8,128)(2,1)S(1)}, bf16[2,128,256]{2,1,0:T(8,128)(2,1)S(1)}, u32[]{:S(2)}, u32[]{:S(2)}) collective-permute-start(bf16[2,128,256]{2,1,0:T(8,128)(2,1)S(1)} %get-tuple-element.41), channel_id=1, source_target_pairs={{0,6},{1,7},{2,4},{3,5},{4,2},{5,3},{6,0},{7,1},{8,14},{9,15},{10,... | collective-permute-start | bytes 393224 | tf_op jit(solution)/shard_map/ppermute | solution.py:16
  232.8 20.0 %collective-permute-start.39 = (bf16[2,128,256]{2,1,0:T(8,128)(2,1)S(1)}, bf16[2,128,256]{2,1,0:T(8,128)(2,1)S(1)}, u32[]{:S(2)}, u32[]{:S(2)}) collective-permute-start(bf16[2,128,256]{2,1,0:T(8,128)(2,1)S(1)} %get-tuple-element.42), channel_id=1, source_target_pairs={{0,4},{1,5},{2,6},{3,7},{4,0},{5,1},{6,2},{7,3},{8,12},{9,13},{10,... | collective-permute-start | bytes 393224 | tf_op jit(solution)/shard_map/ppermute | solution.py:16
  233.9 19.0 %collective-permute-start.38 = (bf16[2,128,256]{2,1,0:T(8,128)(2,1)S(1)}, bf16[2,128,256]{2,1,0:T(8,128)(2,1)S(1)}, u32[]{:S(2)}, u32[]{:S(2)}) collective-permute-start(bf16[2,128,256]{2,1,0:T(8,128)(2,1)S(1)} %get-tuple-element.40), channel_id=1, source_target_pairs={{0,2},{1,3},{2,0},{3,1},{4,6},{5,7},{6,4},{7,5},{8,10},{9,11},{10,... | collective-permute-start | bytes 393224 | tf_op jit(solution)/shard_map/ppermute | solution.py:16
  241.6 11.4 %collective-permute-start.45 = (bf16[2,128,256]{2,1,0:T(8,128)(2,1)S(1)}, bf16[2,128,256]{2,1,0:T(8,128)(2,1)S(1)}, u32[]{:S(2)}, u32[]{:S(2)}) collective-permute-start(bf16[2,128,256]{2,1,0:T(8,128)(2,1)S(1)} %get-tuple-element.38), channel_id=1, source_target_pairs={{0,6},{1,7},{2,4},{3,5},{4,2},{5,3},{6,0},{7,1},{8,14},{9,15},{10,... | collective-permute-start | bytes 393224 | tf_op jit(solution)/shard_map/ppermute | solution.py:16
  244.1 14.3 %collective-permute-start.44 = (bf16[2,128,256]{2,1,0:T(8,128)(2,1)S(1)}, bf16[2,128,256]{2,1,0:T(8,128)(2,1)S(1)}, u32[]{:S(2)}, u32[]{:S(2)}) collective-permute-start(bf16[2,128,256]{2,1,0:T(8,128)(2,1)S(1)} %get-tuple-element.39), channel_id=1, source_target_pairs={{0,4},{1,5},{2,6},{3,7},{4,0},{5,1},{6,2},{7,3},{8,12},{9,13},{10,... | collective-permute-start | bytes 393224 | tf_op jit(solution)/shard_map/ppermute | solution.py:16
  244.3 14.1 %collective-permute-start.43 = (bf16[2,128,256]{2,1,0:T(8,128)(2,1)S(1)}, bf16[2,128,256]{2,1,0:T(8,128)(2,1)S(1)}, u32[]{:S(2)}, u32[]{:S(2)}) collective-permute-start(bf16[2,128,256]{2,1,0:T(8,128)(2,1)S(1)} %get-tuple-element.37), channel_id=1, source_target_pairs={{0,2},{1,3},{2,0},{3,1},{4,6},{5,7},{6,4},{7,5},{8,10},{9,11},{10,... | collective-permute-start | bytes 393224 | tf_op jit(solution)/shard_map/ppermute | solution.py:16
  253.0 5.5 %copy-start.7 = (bf16[128,2048]{1,0:T(8,128)(2,1)}, bf16[128,2048]{1,0:T(8,128)(2,1)S(1)}, u32[]{:S(2)}) copy-start(bf16[128,2048]{1,0:T(8,128)(2,1)S(1)} %fusion.62) | copy-start | bytes 1572868

commit v2 on v0

v2 whole, which is shorter than its diff:
```python
import functools

import jax
import jax.numpy as jnp
from jax import lax
from jax.experimental import pallas as pl
from jax.experimental.pallas import tpu as pltpu
from jax.sharding import PartitionSpec as P

EPS = 1e-05
LANES = 128
VMEM_LIMIT = 52 * 1024 * 1024


def exchange(value, axis, bit):
    size = lax.axis_size(axis)
    return lax.ppermute(value, axis, [(i, i ^ bit) for i in range(size)])


def after(value, *earlier):
    return lax.optimization_barrier((value, *earlier))[0]


def cut_kernel(places, lanes, at_ref, gate_ref, up_ref, out_ref, held, in_sems, out_sems):
    weights = (gate_ref, up_ref)

    def copy_in(n, i):
        offset, start = places[n]
        first = pl.multiple_of((at_ref[0] ^ offset) * at_ref[2] + at_ref[1] + start, LANES)
        return pltpu.make_async_copy(weights[i].at[:, pl.ds(first, lanes)], held.at[n, i], in_sems.at[n, i])

    def copy_out(n, i):
        return pltpu.make_async_copy(held.at[n, i], out_ref.at[n, i], out_sems.at[n, i])

    every = [(n, i) for n in range(len(places)) for i in range(2)]
    for n, i in every:
        copy_in(n, i).start()
    for n, i in every:
        copy_in(n, i).wait()
        copy_out(n, i).start()
    for n, i in every:
        copy_out(n, i).wait()


def cut(at, gate_weight, up_weight, places, lanes):
    depth = gate_weight.shape[0]
    count = len(places)
    hbm = pl.BlockSpec(memory_space=pltpu.HBM)
    return pl.pallas_call(
        functools.partial(cut_kernel, places, lanes),
        in_specs=[pl.BlockSpec(memory_space=pltpu.SMEM), hbm, hbm],
        out_specs=hbm,
        out_shape=jax.ShapeDtypeStruct((count, 2, depth, lanes), jnp.bfloat16),
        scratch_shapes=[
            pltpu.VMEM((count, 2, depth, lanes), jnp.bfloat16),
            pltpu.SemaphoreType.DMA((count, 2)),
            pltpu.SemaphoreType.DMA((count, 2)),
        ],
        compiler_params=pltpu.CompilerParams(vmem_limit_bytes=VMEM_LIMIT),
        name="cut",
    )(at, gate_weight, up_weight)


def sums_kernel(places, lanes, side, stacked, at_ref, x_ref, gate_ref, up_ref, theirs_ref, masks_ref, *refs):
    out_refs, (kept, result, in_sems, out_sems) = refs[:-4], refs[-4:]
    depth = gate_ref.shape[0]
    weights = (gate_ref, up_ref)
    firsts = [
        pl.multiple_of((at_ref[0] ^ offset) * at_ref[2] + at_ref[1] + start, LANES) for offset, start, _ in places
    ]

    def copies_in(n, i):
        return (
            pltpu.make_async_copy(
                weights[i].at[:, pl.ds(firsts[n], lanes)], kept.at[n, i, pl.ds(0, depth)], in_sems.at[n, i, 0]
            ),
            pltpu.make_async_copy(
                theirs_ref.at[places[n][2], i], kept.at[n, i, pl.ds(depth, depth)], in_sems.at[n, i, 1]
            ),
        )

    def copy_out(n, i):
        out = out_refs[0].at[n, i] if stacked else out_refs[n].at[i]
        return pltpu.make_async_copy(result.at[n, i], out, out_sems.at[n, i])

    every = [(n, i) for n in range(len(places)) for i in range(2)]
    ahead = 3
    for one in every[:ahead]:
        for copy in copies_in(*one):
            copy.start()
    across = masks_ref.shape[1]
    blocks = 2 * depth // side
    for k, (n, i) in enumerate(every):
        if k + ahead < len(every):
            for copy in copies_in(*every[k + ahead]):
                copy.start()
        if i == 0:
            block = lax.broadcasted_iota(jnp.int32, (across, lanes), 0)
            column = firsts[n] + lax.broadcasted_iota(jnp.int32, (across, lanes), 1)
            spread = ((column >= block * side) & (column < (block + 1) * side)).astype(jnp.bfloat16)
            masks = jnp.dot(masks_ref[...], spread, preferred_element_type=jnp.float32).astype(jnp.bfloat16)
        for copy in copies_in(n, i):
            copy.wait()
        for b in range(blocks):
            rows = slice(b * side, (b + 1) * side)
            kept[n, i, rows, :] = kept[n, i, rows, :] * masks[i * blocks + b : i * blocks + b + 1, :]
        total = jnp.dot(x_ref[...], kept[n, i], preferred_element_type=jnp.float32)
        result[n, i] = total.astype(result.dtype)
        copy_out(n, i).start()
    for one in every:
        copy_out(*one).wait()


def sums(at, x, gate_weight, up_weight, theirs, masks, side, places, lanes, dtype, stacked):
    depth = gate_weight.shape[0]
    tokens = x.shape[0]
    count = len(places)
    vmem = pl.BlockSpec(memory_space=pltpu.VMEM)
    hbm = pl.BlockSpec(memory_space=pltpu.HBM)
    return pl.pallas_call(
        functools.partial(sums_kernel, places, lanes, side, stacked),
        in_specs=[pl.BlockSpec(memory_space=pltpu.SMEM), vmem, hbm, hbm, hbm, vmem],
        out_specs=[hbm] * (1 if stacked else count),
        out_shape=(
            [jax.ShapeDtypeStruct((count, 2, tokens, lanes), dtype)]
            if stacked
            else [jax.ShapeDtypeStruct((2, tokens, lanes), dtype)] * count
        ),
        scratch_shapes=[
            pltpu.VMEM((count, 2, 2 * depth, lanes), jnp.bfloat16),
            pltpu.VMEM((count, 2, tokens, lanes), dtype),
            pltpu.SemaphoreType.DMA((count, 2, 2)),
            pltpu.SemaphoreType.DMA((count, 2)),
        ],
        compiler_params=pltpu.CompilerParams(vmem_limit_bytes=VMEM_LIMIT),
        name="sums",
    )(at, x, gate_weight, up_weight, theirs, masks)


def local(tokens, gain, gate_weight, up_weight, gate_mask, up_mask):
    shards = lax.axis_size("tensor")
    shard = lax.axis_index("tensor")
    half = lax.axis_index("wide")
    depth, width = gate_weight.shape
    features = gain.shape[0]
    rows = tokens.shape[0]
    per_shard = width // shards
    per_core = per_shard // 2
    pairs = shards // 2

    mine = jnp.stack([shard, half * per_core, per_shard]).astype(jnp.int32)
    partners = jnp.stack([shard, (1 - half) * per_core, per_shard]).astype(jnp.int32)
    side = features // gate_mask.shape[0]
    first_rows = [half * (features // 2) + shard * depth, (1 - half) * (features // 2) + shard * depth]
    lanes = per_core // 2 if pairs == 4 else per_core
    theirs, pair, far = {}, {}, {}

    def place(unit):
        p, y, h = unit
        return (2 * p + y, h * lanes)

    latest = []

    def in_turn(value, *more):
        return after(value, *latest, *more)

    def emit(value):
        latest[:] = [value]
        return value

    def fetch(units, *earlier):
        value = emit(cut(in_turn(partners, *earlier), gate_weight, up_weight, tuple(map(place, units)), lanes))
        value = exchange(value, "wide", 1)
        for n, unit in enumerate(units):
            theirs[unit] = (value, n)

    raw = []
    for flip in range(2):
        moves = []
        for w in range(2):
            for t in range(shards):
                moves.append((((t % 2) ^ flip) * shards + w * pairs + t // 2, w * shards + t))
        piece = lax.dynamic_slice_in_dim(tokens, (half ^ flip) * depth, depth, 1)
        raw.append(lax.ppermute(piece, ("wide", "tensor"), moves))
    values = tokens.astype(jnp.float32)
    squares = jnp.sum(values * values, axis=-1).reshape(1, rows)
    emit(squares)
    if pairs == 4:
        fetch([(3, 1, 0), (3, 1, 1)])
    total = squares + exchange(squares, "tensor", 2)
    if pairs == 4:
        emit(total)
        fetch([(3, 0, 0), (3, 0, 1), (2, 1, 0), (1, 1, 0)])
    raw = after(jnp.where(shard % 2 == 1, jnp.concatenate(raw[::-1]), jnp.concatenate(raw)), total)
    raw_other = exchange(raw, "wide", 1)
    bit = 4
    while bit < shards:
        total = total + exchange(total, "tensor", bit)
        bit *= 2
    if pairs == 4:
        emit(total)
        fetch([(2, 1, 1), (1, 1, 1), (2, 0, 0), (1, 0, 0), (0, 0, 0), (0, 0, 1)])
    total = total + exchange(total, "tensor", 1)
    scale = lax.rsqrt(total / features + EPS)
    scale_other = exchange(scale, "wide", 1)
    scales = jnp.where(
        half == 0,
        jnp.concatenate([scale, scale_other], axis=1),
        jnp.concatenate([scale_other, scale], axis=1),
    ).reshape(2 * rows, 1)
    gains = [lax.dynamic_slice_in_dim(gain, r, depth, 0)[None, :] for r in first_rows]
    normed = jnp.concatenate(
        [(v.astype(jnp.float32) * scales * g).astype(jnp.bfloat16) for v, g in zip((raw, raw_other), gains)], axis=1
    )

    masks = jnp.concatenate(
        [
            lax.dynamic_slice_in_dim(mask, r // side, depth // side, 0)
            for mask in (gate_mask, up_mask)
            for r in first_rows
        ]
    ).astype(jnp.bfloat16)

    def chip_sums(units, *more, stacked=True):
        value = theirs[units[0]][0]
        places = tuple((*place(unit), theirs[unit][1]) for unit in units)
        dtype = jnp.bfloat16 if stacked else jnp.float32
        values = sums(
            mine, in_turn(normed, *more), gate_weight, up_weight, value, masks, side, places, lanes, dtype, stacked
        )
        emit(values[0])
        return values[0] if stacked else values

    def finish(own, *terms):
        total = in_turn(own)
        for term in terms:
            total = total + wide(term)
        return (jax.nn.silu(total[0]) * total[1]).astype(jnp.bfloat16)

    def add(own, *terms):
        total = in_turn(own)
        for term in terms:
            total = total + wide(term)
        return emit(total.astype(jnp.bfloat16))

    def give(hidden):
        keep = lax.dynamic_slice_in_dim(hidden, half * rows, rows, 0)
        got = exchange(lax.dynamic_slice_in_dim(hidden, (1 - half) * rows, rows, 0), "wide", 1)
        return jnp.where(half == 0, keep, got), jnp.where(half == 0, got, keep)

    wide = lambda value: value.astype(jnp.float32)

    if pairs == 4:
        tensor_pairs = lambda moves: [(2 * i + y, 2 * j + y) for i, j in moves for y in range(2)]
        by_neighbour = tensor_pairs(((0, 1), (3, 2)))
        middle = tensor_pairs(((1, 2), (2, 1)))

        pair3 = exchange(chip_sums([(3, 1, 0), (3, 1, 1)]), "tensor", 1)
        fetch([(2, 0, 1), (1, 0, 1)])
        fetch([(0, 1, 0), (0, 1, 1)])
        near3 = chip_sums([(3, 0, 0), (3, 0, 1)], stacked=False)
        far_a = chip_sums([(2, 1, 0), (1, 1, 0)])
        pair_a = exchange(in_turn(far_a, pair3), "tensor", 1)
        third = jnp.stack([add(near3[h], pair3[h]) for h in range(2)])
        relay = lax.ppermute(third, "tensor", by_neighbour)
        across = lax.ppermute(third, "tensor", middle)
        near_a = chip_sums([(2, 0, 0), (1, 0, 0)], stacked=False)
        far_b = chip_sums([(2, 1, 1), (1, 1, 1)])
        pair_b = exchange(in_turn(far_b, pair_a), "tensor", 1)
        second_a = exchange(add(after(near_a[0], across), pair_a[0], relay[0]), "tensor", 4)
        first_a = exchange(add(near_a[1], pair_a[1]), "tensor", 2)
        near_b = chip_sums([(2, 0, 1), (1, 0, 1)], stacked=False)
        far_0 = chip_sums([(0, 1, 0), (0, 1, 1)])
        pair_0 = exchange(in_turn(far_0, pair_b), "tensor", 1)
        second_b = exchange(add(near_b[0], pair_b[0], relay[1]), "tensor", 4)
        first_b = exchange(add(near_b[1], pair_b[1]), "tensor", 2)
        own = chip_sums([(0, 0, 0), (0, 0, 1)], stacked=False)
        left, right = [], []
        for h, second, first in ((0, second_a, first_a), (1, second_b, first_b)):
            one, other = give(finish(own[h], pair_0[h], first, second, across[h]))
            left.append(one)
            right.append(other)
        return jnp.concatenate(left + right, axis=1)
    received = []
    for p in range(pairs - 1, -1, -1):
        fetch([(p, 1, 0), (p, 0, 0)])
        from_pair = exchange(chip_sums([(p, 1, 0)])[0], "tensor", 1)
        own = chip_sums([(p, 0, 0)], stacked=False)[0]
        if p:
            received.append(exchange(add(own, from_pair), "tensor", 2 * p))
    return jnp.concatenate(give(finish(own, from_pair, *received)), axis=1)


def solution(mesh):
    in_specs = (
        P(("group", "wide"), "tensor"),
        P("group"),
        P(("group", "wide", "tensor"), None),
        P(("group", "wide", "tensor"), None),
        P("group", None),
        P("group", None),
    )
    out_specs = P(("group", "wide"), "tensor")
    return jax.shard_map(local, mesh=mesh, in_specs=in_specs, out_specs=out_specs, check_vma=False)
```

time: 884 us -> 162 us (0.18)
  waiting for transfers between devices: 533 us -> 47.8 us
  local copies, waits for them, and re-layouts: 250 us -> 5.05 us
  Pallas kernels: 0 us -> 54.9 us
  other arithmetic: 45.1 us -> 18.7 us
  starting transfers between devices: 11.7 us -> 34 us
  matrix products: 18.9 us -> 0 us
  between operations: 13.2 us -> 0.39 us
    all_to_all x2 -> x0, waiting for transfers between devices: 494 us -> none  [the longest x1 341 us: local(): lax.all_to_all(gate_weight, 'tensor', split_axis=1, concat_axis=0, tiled=...]
    mul x8 -> x0, local copies, waits for them, and re-layouts: 201 us -> none  [apply_mask(): blocks = blocks * mask.astype(jnp.bfloat16)[:, None, :, None]]
    pallas_call x0 -> x13, Pallas kernels: none -> 54.9 us  [the longest x8 35.3 us: sums(): pl.pallas_call(functools.partial(sums_kernel, places, lanes, side, stacke...]
    ppermute x0 -> x24, waiting for transfers between devices: none -> 47.8 us  [the longest x20 40.4 us: exchange(): return lax.ppermute(value, axis, [(i, i ^ bit) for i in range(size)])]
    unnamed x7 -> x14, local copies, waits for them, and re-layouts: 46.8 us -> 4.21 us
    mul x2 -> x0, other arithmetic: 34.3 us -> none  [apply_mask(): blocks = blocks * mask.astype(jnp.bfloat16)[:, None, :, None]]
    ppermute x0 -> x24, starting transfers between devices: none -> 34 us  [the longest x20 24.7 us: exchange(): return lax.ppermute(value, axis, [(i, i ^ bit) for i in range(size)])]
    all_gather x1 -> x0, waiting for transfers between devices: 30.6 us -> none  [local(): whole = lax.all_gather(tokens, 'tensor', axis=1, tiled=True)]
  transfers between devices with their start and end apart: 5 -> 24, of which waited for: 4 -> 13; matrix products, arithmetic and copies ran while one was open for 34% -> 9% of each run, Pallas kernels for 0% -> 30%
where the time goes in v2:
time: 162 us; the launch traced here: 161 us
  Pallas kernels  54.9 us (34%)
  waiting for transfers between devices  47.8 us (30%)
  starting transfers between devices  34 us (21%)
  other arithmetic  18.7 us (12%)
  local copies, waits for them, and re-layouts  5.05 us (3%)
    ppermute x20, waiting for transfers between devices, exchange(): return lax.ppermute(value, axis, [(i, i ^ bit) for i in range(size)])  40.4 us
    pallas_call x8, Pallas kernels, sums(): pl.pallas_call(functools.partial(sums_kernel, places, lanes, side, stacke...  35.3 us
    ppermute x20, starting transfers between devices, exchange(): return lax.ppermute(value, axis, [(i, i ^ bit) for i in range(size)])  24.7 us
    pallas_call x5, Pallas kernels, cut(): pl.pallas_call(functools.partial(cut_kernel, places, lanes), in_specs=[pl...  19.6 us
    convert_element_type x6, other arithmetic, add(): return emit(total.astype(jnp.bfloat16))  11 us
    ppermute x1, waiting for transfers between devices, local(): relay = lax.ppermute(third, 'tensor', by_neighbour)  7.24 us
    ppermute x1, starting transfers between devices, local(): relay = lax.ppermute(third, 'tensor', by_neighbour)  5.14 us
    unnamed x14, local copies, waits for them, and re-layouts  4.21 us
  transfers between devices with their start and end apart: 24, of which 13 were waited for; matrix products, arithmetic and copies ran while one was open for 9% of the time, Pallas kernels for 30%

profile of v2, /device:TPU:0, one launch (start us, length us, event | category | flops | bytes accessed | tf_op | source)
XLA Modules:
  0.0 160.9 jit_solution(3405687206959640519)
XLA Ops:
  0.0 1.1 multiply_reduce_fusion
  1.1 3.1 %collective-permute-start.2 = (f32[1,128]{1,0:T(1,128)S(1)}, f32[1,128]{1,0:T(1,128)S(1)}, u32[]{:S(2)}, u32[]{:S(2)}) collective-permute-start(f32[1,128]{1,0:T(1,128)S(1)} %bitcast.91), channel_id=1, source_target_pairs={{0,2},{1,3},{2,0},{3,1},{4,6},{5,7},{6,4},{7,5},{8,10},{9,11},{10,... | collective-permute-start | bytes 1544 | tf_op jit(solution)/shard_map/ppermute | solution.py:17
  4.2 1.5 collective-permute-done.2
  5.7 3.0 %collective-permute-start.3 = (f32[1,128]{1,0:T(1,128)S(1)}, f32[1,128]{1,0:T(1,128)S(1)}, u32[]{:S(2)}, u32[]{:S(2)}) collective-permute-start(f32[1,128]{1,0:T(1,128)S(1)} %bitcast_add_fusion), channel_id=1, source_target_pairs={{0,4},{1,5},{2,6},{3,7},{4,0},{5,1},{6,2},{7,3},{8,12},{9,13},{10,... | collective-permute-start | bytes 1544 | tf_op jit(solution)/shard_map/ppermute | solution.py:17
  8.8 1.4 collective-permute-done.3
  10.2 6.1 %cut.5 = bf16[6,2,512,512]{3,2,1,0:T(8,128)(2,1)} custom-call(s32[3]{0:T(128)S(1)} %pad_add_fusion.at_ref, bf16[512,16384]{1,0:T(8,128)(2,1)} %gate_ref.25, bf16[512,16384]{1,0:T(8,128)(2,1)} %up_ref.25), custom_call_target="tpu_custom_call" | custom-call | tf_op jit(solution)/shard_map/cut/pallas_call | solution.py:49
  16.4 4.3 %cut.9 = bf16[4,2,512,512]{3,2,1,0:T(8,128)(2,1)} custom-call(s32[3]{0:T(128)S(1)} %pad_add_fusion.at_ref, bf16[512,16384]{1,0:T(8,128)(2,1)} %gate_ref.25, bf16[512,16384]{1,0:T(8,128)(2,1)} %up_ref.25), custom_call_target="tpu_custom_call" | custom-call | tf_op jit(solution)/shard_map/cut/pallas_call | solution.py:49
  20.7 0.6 collective-permute-start.8
  21.3 3.0 %cut.6 = bf16[2,2,512,512]{3,2,1,0:T(8,128)(2,1)} custom-call(s32[3]{0:T(128)S(1)} %pad_add_fusion.at_ref, bf16[512,16384]{1,0:T(8,128)(2,1)} %gate_ref.25, bf16[512,16384]{1,0:T(8,128)(2,1)} %up_ref.25), custom_call_target="tpu_custom_call" | custom-call | tf_op jit(solution)/shard_map/cut/pallas_call | solution.py:49
  24.3 0.1 collective-permute-start.7
  24.4 1.9 %collective-permute-start = (bf16[128,512]{1,0:T(8,128)(2,1)S(1)}, bf16[128,512]{1,0:T(8,128)(2,1)S(1)}, u32[]{:S(2)}, u32[]{:S(2)}) collective-permute-start(bf16[128,512]{1,0:T(8,128)(2,1)S(1)} %get-tuple-element.79), channel_id=1, source_target_pairs={{8,0},{0,1},{9,2},{1,3},{10,4},{2,5},{11,6},{3,7},{12,8},{4,9},{13... | collective-permute-start | bytes 393224 | tf_op jit(solution)/shard_map/ppermute | solution.py:184
  26.3 0.7 collective-permute-start.1
  27.1 0.8 dynamic-slice_convert_fusion.1
  27.9 0.8 fusion.14
  28.6 0.2 collective-permute-done
  28.9 5.1 %collective-permute-start.4 = (f32[1,128]{1,0:T(1,128)S(1)}, f32[1,128]{1,0:T(1,128)S(1)}, u32[]{:S(2)}, u32[]{:S(2)}) collective-permute-start(f32[1,128]{1,0:T(1,128)S(1)} %add.114), channel_id=1, source_target_pairs={{0,1},{1,0},{2,3},{3,2},{4,5},{5,4},{6,7},{7,6},{8,9},{9,8},{10,11... | collective-permute-start | bytes 1544 | tf_op jit(solution)/shard_map/ppermute | solution.py:17
  34.1 0.4 collective-permute-start.6
  34.5 1.1 collective-permute-done.4
  35.5 0.1 pad_add_fusion.1.at_ref
  35.6 1.0 collective-permute-done.5
  36.7 0.2 multiply_convert_fusion.1
  36.9 1.4 copy-done
  38.3 4.0 %sums.8 = bf16[2,2,256,512]{3,2,1,0:T(8,128)(2,1)S(1)} custom-call(s32[3]{0:T(128)S(1)} %pad_add_fusion.1.at_ref, bf16[256,1024]{1,0:T(8,128)(2,1)S(1)} %pad_maximum_fusion.1.x_ref, bf16[512,16384]{1,0:T(8,128)(2,1)} %gate_ref.25, bf16[512,16384]{1,0:T(8,128)(2,1)} %up_ref.25, bf16[2,2,512,512]{3,2,1,0:T(8,128)(2,1)} %copy-done, ...), custom_call_target="tpu_custom_call" | custom-call | tf_op jit(solution)/shard_map/sums/pallas_call | solution.py:120
  42.3 2.1 %collective-permute-start.9 = (bf16[2,2,256,512]{3,2,1,0:T(8,128)(2,1)S(1)}, bf16[2,2,256,512]{3,2,1,0:T(8,128)(2,1)}, u32[]{:S(2)}, u32[]{:S(2)}) collective-permute-start(bf16[2,2,256,512]{3,2,1,0:T(8,128)(2,1)S(1)} %sums.8), channel_id=1, source_target_pairs={{0,1},{1,0},{2,3},{3,2},{4,5},{5,4},{6,7},{7,6},{8,9},{9,8},{10,11... | collective-permute-start | bytes 3145736 | tf_op jit(solution)/shard_map/ppermute | solution.py:17
  44.4 3.1 %cut.7 = bf16[2,2,512,512]{3,2,1,0:T(8,128)(2,1)} custom-call(s32[3]{0:T(128)S(1)} %pad_add_fusion.at_ref, bf16[512,16384]{1,0:T(8,128)(2,1)} %gate_ref.25, bf16[512,16384]{1,0:T(8,128)(2,1)} %up_ref.25), custom_call_target="tpu_custom_call" | custom-call | tf_op jit(solution)/shard_map/cut/pallas_call | solution.py:49
  47.5 3.1 %cut.8 = bf16[2,2,512,512]{3,2,1,0:T(8,128)(2,1)} custom-call(s32[3]{0:T(128)S(1)} %pad_add_fusion.at_ref, bf16[512,16384]{1,0:T(8,128)(2,1)} %gate_ref.25, bf16[512,16384]{1,0:T(8,128)(2,1)} %up_ref.25), custom_call_target="tpu_custom_call" | custom-call | tf_op jit(solution)/shard_map/cut/pallas_call | solution.py:49
  50.7 0.5 collective-permute-start.14
  51.2 4.8 %sums.9 = (f32[2,256,512]{2,1,0:T(8,128)S(1)}, f32[2,256,512]{2,1,0:T(8,128)}) custom-call(s32[3]{0:T(128)S(1)} %pad_add_fusion.1.at_ref, bf16[256,1024]{1,0:T(8,128)(2,1)S(1)} %pad_maximum_fusion.1.x_ref, bf16[512,16384]{1,0:T(8,128)(2,1)} %gate_ref.25, bf16[512,16384]{1,0:T(8,128)(2,1)} %up_ref.25, ...), custom_call_target="tpu_custom_call" | custom-call | tf_op jit(solution)/shard_map/sums/pallas_call | solution.py:120
  56.0 4.0 %sums.10 = bf16[2,2,256,512]{3,2,1,0:T(8,128)(2,1)S(1)} custom-call(s32[3]{0:T(128)S(1)} %pad_add_fusion.1.at_ref, bf16[256,1024]{1,0:T(8,128)(2,1)S(1)} %pad_maximum_fusion.1.x_ref, bf16[512,16384]{1,0:T(8,128)(2,1)} %gate_ref.25, bf16[512,16384]{1,0:T(8,128)(2,1)} %up_ref.25, bf16[4,2,512,512]{3,2,1,0:T(8,128)(2,1)} %collective-permute-done.8.theirs_ref, ...), custom_call_target="tpu_custom_call" | custom-call | tf_op jit(solution)/shard_map/sums/pallas_call | solution.py:120
  60.0 8.0 %collective-permute-done.9 = bf16[2,2,256,512]{3,2,1,0:T(8,128)(2,1)} collective-permute-done((bf16[2,2,256,512]{3,2,1,0:T(8,128)(2,1)S(1)}, bf16[2,2,256,512]{3,2,1,0:T(8,128)(2,1)}, u32[]{:S(2)}, u32[]{:S(2)}) %collective-permute-start.9) | collective-permute-done | bytes 1048608 | tf_op jit(solution)/shard_map/ppermute | solution.py:17
  68.1 1.7 %collective-permute-start.12 = (bf16[2,2,256,512]{3,2,1,0:T(8,128)(2,1)S(1)}, bf16[2,2,256,512]{3,2,1,0:T(8,128)(2,1)}, u32[]{:S(2)}, u32[]{:S(2)}) collective-permute-start(bf16[2,2,256,512]{3,2,1,0:T(8,128)(2,1)S(1)} %sums.10), channel_id=1, source_target_pairs={{0,1},{1,0},{2,3},{3,2},{4,5},{5,4},{6,7},{7,6},{8,9},{9,8},{10,11... | collective-permute-start | bytes 3145736 | tf_op jit(solution)/shard_map/ppermute | solution.py:17
  69.8 1.2 fusion.9
  71.1 1.2 fusion.8
  72.3 1.1 pad_maximum_fusion
  73.4 1.6 %collective-permute-start.11 = (bf16[2,2,256,512]{3,2,1,0:T(8,128)(2,1)}, bf16[2,2,256,512]{3,2,1,0:T(8,128)(2,1)}, u32[]{:S(2)}, u32[]{:S(2)}) collective-permute-start(bf16[2,2,256,512]{3,2,1,0:T(8,128)(2,1)} %pad_maximum_fusion), channel_id=1, source_target_pairs={{2,4},{3,5},{4,2},{5,3},{10,12},{11,13},{12,10},{13,11},{18,20},{1... | collective-permute-start | bytes 3145736 | tf_op jit(solution)/shard_map/ppermute | solution.py:266
  75.0 5.1 %collective-permute-start.13 = (bf16[2,2,256,512]{3,2,1,0:T(8,128)(2,1)}, bf16[2,2,256,512]{3,2,1,0:T(8,128)(2,1)S(1)}, u32[]{:S(2)}, u32[]{:S(2)}) collective-permute-start(bf16[2,2,256,512]{3,2,1,0:T(8,128)(2,1)} %pad_maximum_fusion), channel_id=1, source_target_pairs={{0,2},{1,3},{6,4},{7,5},{8,10},{9,11},{14,12},{15,13},{16,18},{17,... | collective-permute-start | bytes 3145736 | tf_op jit(solution)/shard_map/ppermute | solution.py:265
  80.1 4.8 %sums.11 = (f32[2,256,512]{2,1,0:T(8,128)S(1)}, f32[2,256,512]{2,1,0:T(8,128)}) custom-call(s32[3]{0:T(128)S(1)} %pad_add_fusion.1.at_ref, bf16[256,1024]{1,0:T(8,128)(2,1)S(1)} %pad_maximum_fusion.1.x_ref, bf16[512,16384]{1,0:T(8,128)(2,1)} %gate_ref.25, bf16[512,16384]{1,0:T(8,128)(2,1)} %up_ref.25, ...), custom_call_target="tpu_custom_call" | custom-call | tf_op jit(solution)/shard_map/sums/pallas_call | solution.py:120
  84.9 4.0 %sums.12 = bf16[2,2,256,512]{3,2,1,0:T(8,128)(2,1)S(1)} custom-call(s32[3]{0:T(128)S(1)} %pad_add_fusion.1.at_ref, bf16[256,1024]{1,0:T(8,128)(2,1)S(1)} %pad_maximum_fusion.1.x_ref, bf16[512,16384]{1,0:T(8,128)(2,1)} %gate_ref.25, bf16[512,16384]{1,0:T(8,128)(2,1)} %up_ref.25, bf16[6,2,512,512]{3,2,1,0:T(8,128)(2,1)} %collective-permute-done.10.theirs_ref, ...), custom_call_target="tpu_custom_call" | custom-call | tf_op jit(solution)/shard_map/sums/pallas_call | solution.py:120
  89.0 4.0 %collective-permute-done.12 = bf16[2,2,256,512]{3,2,1,0:T(8,128)(2,1)} collective-permute-done((bf16[2,2,256,512]{3,2,1,0:T(8,128)(2,1)S(1)}, bf16[2,2,256,512]{3,2,1,0:T(8,128)(2,1)}, u32[]{:S(2)}, u32[]{:S(2)}) %collective-permute-start.12) | collective-permute-done | bytes 1048608 | tf_op jit(solution)/shard_map/ppermute | solution.py:17
  92.9 1.4 collective-permute-start.16
  94.4 7.2 %collective-permute-done.13 = bf16[2,2,256,512]{3,2,1,0:T(8,128)(2,1)S(1)} collective-permute-done((bf16[2,2,256,512]{3,2,1,0:T(8,128)(2,1)}, bf16[2,2,256,512]{3,2,1,0:T(8,128)(2,1)S(1)}, u32[]{:S(2)}, u32[]{:S(2)}) %collective-permute-start.13) | collective-permute-done | bytes 1048608 | tf_op jit(solution)/shard_map/ppermute | solution.py:265
  101.6 2.1 %fusion.7 = bf16[2,256,512]{2,1,0:T(8,128)(2,1)} fusion(f32[2,256,512]{2,1,0:T(8,128)S(1)} %get-tuple-element.57, bf16[2,2,256,512]{3,2,1,0:T(8,128)(2,1)S(1)} %collective-permute-done.13, bf16[2,2,256,512]{3,2,1,0:T(8,128)(2,1)} %collective-permute-done.12), kind=kLoop, calls=%fused_computation.17 | loop fusion | flops 1310720 | bytes 2621440 | tf_op jit(solution)/shard_map/convert_element_type | solution.py:244
  103.7 2.3 %fusion.6 = bf16[2,256,512]{2,1,0:T(8,128)(2,1)} fusion(f32[2,256,512]{2,1,0:T(8,128)} %get-tuple-element.59, bf16[2,2,256,512]{3,2,1,0:T(8,128)(2,1)} %collective-permute-done.12), kind=kLoop, calls=%fused_computation.15 | loop fusion | flops 786432 | bytes 2097152 | tf_op jit(solution)/shard_map/convert_element_type | solution.py:244
  106.0 2.4 %collective-permute-start.18 = (bf16[2,256,512]{2,1,0:T(8,128)(2,1)}, bf16[2,256,512]{2,1,0:T(8,128)(2,1)S(1)}, u32[]{:S(2)}, u32[]{:S(2)}) collective-permute-start(bf16[2,256,512]{2,1,0:T(8,128)(2,1)} %fusion.6), channel_id=1, source_target_pairs={{0,2},{1,3},{2,0},{3,1},{4,6},{5,7},{6,4},{7,5},{8,10},{9,11},{10,... | collective-permute-start | bytes 1572872 | tf_op jit(solution)/shard_map/ppermute | solution.py:17
  108.4 0.3 collective-permute-start.19
  108.7 1.4 copy-done.3
  110.1 4.8 %sums.13 = (f32[2,256,512]{2,1,0:T(8,128)S(1)}, f32[2,256,512]{2,1,0:T(8,128)}) custom-call(s32[3]{0:T(128)S(1)} %pad_add_fusion.1.at_ref, bf16[256,1024]{1,0:T(8,128)(2,1)S(1)} %pad_maximum_fusion.1.x_ref, bf16[512,16384]{1,0:T(8,128)(2,1)} %gate_ref.25, bf16[512,16384]{1,0:T(8,128)(2,1)} %up_ref.25, bf16[2,2,512,512]{3,2,1,0:T(8,128)(2,1)} %copy-done.3, ...), custom_call_target="tpu_custom_call" | custom-call | tf_op jit(solution)/shard_map/sums/pallas_call | solution.py:120
  114.9 1.4 copy-done.1
  116.3 4.0 %sums.14 = bf16[2,2,256,512]{3,2,1,0:T(8,128)(2,1)S(1)} custom-call(s32[3]{0:T(128)S(1)} %pad_add_fusion.1.at_ref, bf16[256,1024]{1,0:T(8,128)(2,1)S(1)} %pad_maximum_fusion.1.x_ref, bf16[512,16384]{1,0:T(8,128)(2,1)} %gate_ref.25, bf16[512,16384]{1,0:T(8,128)(2,1)} %up_ref.25, bf16[2,2,512,512]{3,2,1,0:T(8,128)(2,1)} %copy-done.1, ...), custom_call_target="tpu_custom_call" | custom-call | tf_op jit(solution)/shard_map/sums/pallas_call | solution.py:120
  120.4 1.1 collective-permute-start.17
  121.5 2.1 %fusion.5 = bf16[2,256,512]{2,1,0:T(8,128)(2,1)} fusion(f32[2,256,512]{2,1,0:T(8,128)S(1)} %get-tuple-element.64, bf16[2,2,256,512]{3,2,1,0:T(8,128)(2,1)S(1)} %collective-permute-done.13, bf16[2,2,256,512]{3,2,1,0:T(8,128)(2,1)} %collective-permute-done.16), kind=kLoop, calls=%fused_computation.12 | loop fusion | flops 1310720 | bytes 2621440 | tf_op jit(solution)/shard_map/convert_element_type | solution.py:244
  123.6 2.0 %fusion.4 = bf16[2,256,512]{2,1,0:T(8,128)(2,1)} fusion(f32[2,256,512]{2,1,0:T(8,128)S(1)} %copy-done.4, bf16[2,2,256,512]{3,2,1,0:T(8,128)(2,1)} %collective-permute-done.16), kind=kLoop, calls=%fused_computation.10 | loop fusion | flops 786432 | bytes 2097152 | tf_op jit(solution)/shard_map/convert_element_type | solution.py:244
  125.6 2.0 %collective-permute-start.21 = (bf16[2,256,512]{2,1,0:T(8,128)(2,1)}, bf16[2,256,512]{2,1,0:T(8,128)(2,1)}, u32[]{:S(2)}, u32[]{:S(2)}) collective-permute-start(bf16[2,256,512]{2,1,0:T(8,128)(2,1)} %fusion.4), channel_id=1, source_target_pairs={{0,2},{1,3},{2,0},{3,1},{4,6},{5,7},{6,4},{7,5},{8,10},{9,11},{10,... | collective-permute-start | bytes 1572872 | tf_op jit(solution)/shard_map/ppermute | solution.py:17
  127.7 4.8 %sums.15 = (f32[2,256,512]{2,1,0:T(8,128)S(1)}, f32[2,256,512]{2,1,0:T(8,128)}) custom-call(s32[3]{0:T(128)S(1)} %pad_add_fusion.1.at_ref, bf16[256,1024]{1,0:T(8,128)(2,1)S(1)} %pad_maximum_fusion.1.x_ref, bf16[512,16384]{1,0:T(8,128)(2,1)} %gate_ref.25, bf16[512,16384]{1,0:T(8,128)(2,1)} %up_ref.25, ...), custom_call_target="tpu_custom_call" | custom-call | tf_op jit(solution)/shard_map/sums/pallas_call | solution.py:120
  132.6 7.2 %collective-permute-done.18 = bf16[2,256,512]{2,1,0:T(8,128)(2,1)S(1)} collective-permute-done((bf16[2,256,512]{2,1,0:T(8,128)(2,1)}, bf16[2,256,512]{2,1,0:T(8,128)(2,1)S(1)}, u32[]{:S(2)}, u32[]{:S(2)}) %collective-permute-start.18) | collective-permute-done | bytes 524320 | tf_op jit(solution)/shard_map/ppermute | solution.py:17
  139.8 11.9 %collective-permute-done.21 = bf16[2,256,512]{2,1,0:T(8,128)(2,1)} collective-permute-done((bf16[2,256,512]{2,1,0:T(8,128)(2,1)}, bf16[2,256,512]{2,1,0:T(8,128)(2,1)}, u32[]{:S(2)}, u32[]{:S(2)}) %collective-permute-start.21) | collective-permute-done | bytes 524320 | tf_op jit(solution)/shard_map/ppermute | solution.py:17
  151.6 3.3 %collective-permute-done.22 = bf16[2,256,512]{2,1,0:T(8,128)(2,1)} collective-permute-done((bf16[2,256,512]{2,1,0:T(8,128)(2,1)}, bf16[2,256,512]{2,1,0:T(8,128)(2,1)}, u32[]{:S(2)}, u32[]{:S(2)}) %collective-permute-start.22) | collective-permute-done | bytes 524320 | tf_op jit(solution)/shard_map/ppermute | solution.py:17
  154.9 3.0 %convert_add_fusion.2 = (f32[2,256,512]{2,1,0:T(8,128)S(1)}, f32[2,256,512]{2,1,0:T(8,128)S(1)}) fusion(f32[2,256,512]{2,1,0:T(8,128)S(1)} %get-tuple-element.69, bf16[2,256,512]{2,1,0:T(8,128)(2,1)} %collective-permute-done.19, bf16[2,256,512]{2,1,0:T(8,128)(2,1)S(1)} %collective-permute-done.18, bf16[2,2,256,512]{3,2,1,0:T(8,128)(2,1)} %collective-permute-done.11, ...), kind=kLoop, calls=%fused_computation.5 | loop fusion | flops 4194304 | bytes 8388608 | tf_op jit(solution)/shard_map/add | solution.py:237
  158.0 0.2 fusion.13
  158.3 0.2 fusion.11
  158.4 0.6 collective-permute-start.23
  159.0 0.6 collective-permute-done.20
  159.7 0.3 collective-permute-done.23
  160.1 0.8 pad_maximum_fusion.2
  (40 shorter events, 0.7 us)
Async XLA Ops:
  1.1 4.6 %collective-permute-start.2 = (f32[1,128]{1,0:T(1,128)S(1)}, f32[1,128]{1,0:T(1,128)S(1)}, u32[]{:S(2)}, u32[]{:S(2)}) collective-permute-start(f32[1,128]{1,0:T(1,128)S(1)} %bitcast.91), channel_id=1, source_target_pairs={{0,2},{1,3},{2,0},{3,1},{4,6},{5,7},{6,4},{7,5},{8,10},{9,11},{10,... | collective-permute-start | bytes 1544 | tf_op jit(solution)/shard_map/ppermute | solution.py:17
  5.7 4.6 %collective-permute-start.3 = (f32[1,128]{1,0:T(1,128)S(1)}, f32[1,128]{1,0:T(1,128)S(1)}, u32[]{:S(2)}, u32[]{:S(2)}) collective-permute-start(f32[1,128]{1,0:T(1,128)S(1)} %bitcast_add_fusion), channel_id=1, source_target_pairs={{0,4},{1,5},{2,6},{3,7},{4,0},{5,1},{6,2},{7,3},{8,12},{9,13},{10,... | collective-permute-start | bytes 1544 | tf_op jit(solution)/shard_map/ppermute | solution.py:17
  16.3 58.7 %collective-permute-start.10 = (bf16[6,2,512,512]{3,2,1,0:T(8,128)(2,1)}, bf16[6,2,512,512]{3,2,1,0:T(8,128)(2,1)}, u32[]{:S(2)}, u32[]{:S(2)}) collective-permute-start(bf16[6,2,512,512]{3,2,1,0:T(8,128)(2,1)} %cut.5), channel_id=1, source_target_pairs={{0,8},{8,0},{1,9},{9,1},{2,10},{10,2},{3,11},{11,3},{4,12},{12,4},... | collective-permute-start | bytes 18874376 | tf_op jit(solution)/shard_map/ppermute | solution.py:17
  20.7 3.7 %copy-start.6 = (bf16[128,1024]{1,0:T(8,128)(2,1)S(1)}, bf16[128,1024]{1,0:T(8,128)(2,1)}, u32[]{:S(2)}) copy-start(bf16[128,1024]{1,0:T(8,128)(2,1)} %param.6) | copy-start | bytes 786436
  20.7 30.5 %collective-permute-start.8 = (bf16[4,2,512,512]{3,2,1,0:T(8,128)(2,1)}, bf16[4,2,512,512]{3,2,1,0:T(8,128)(2,1)}, u32[]{:S(2)}, u32[]{:S(2)}) collective-permute-start(bf16[4,2,512,512]{3,2,1,0:T(8,128)(2,1)} %cut.9), channel_id=1, source_target_pairs={{0,8},{8,0},{1,9},{9,1},{2,10},{10,2},{3,11},{11,3},{4,12},{12,4},... | collective-permute-start | bytes 12582920 | tf_op jit(solution)/shard_map/ppermute | solution.py:17
  24.3 12.6 %collective-permute-start.7 = (bf16[2,2,512,512]{3,2,1,0:T(8,128)(2,1)}, bf16[2,2,512,512]{3,2,1,0:T(8,128)(2,1)S(1)}, u32[]{:S(2)}, u32[]{:S(2)}) collective-permute-start(bf16[2,2,512,512]{3,2,1,0:T(8,128)(2,1)} %cut.6), channel_id=1, source_target_pairs={{0,8},{8,0},{1,9},{9,1},{2,10},{10,2},{3,11},{11,3},{4,12},{12,4},... | collective-permute-start | bytes 6291464 | tf_op jit(solution)/shard_map/ppermute | solution.py:17
  24.4 4.4 %collective-permute-start = (bf16[128,512]{1,0:T(8,128)(2,1)S(1)}, bf16[128,512]{1,0:T(8,128)(2,1)S(1)}, u32[]{:S(2)}, u32[]{:S(2)}) collective-permute-start(bf16[128,512]{1,0:T(8,128)(2,1)S(1)} %get-tuple-element.79), channel_id=1, source_target_pairs={{8,0},{0,1},{9,2},{1,3},{10,4},{2,5},{11,6},{3,7},{12,8},{4,9},{13... | collective-permute-start | bytes 393224 | tf_op jit(solution)/shard_map/ppermute | solution.py:184
  26.3 7.7 %collective-permute-start.1 = (bf16[128,512]{1,0:T(8,128)(2,1)S(1)}, bf16[128,512]{1,0:T(8,128)(2,1)S(1)}, u32[]{:S(2)}, u32[]{:S(2)}) collective-permute-start(bf16[128,512]{1,0:T(8,128)(2,1)S(1)} %get-tuple-element.80), channel_id=1, source_target_pairs={{0,0},{8,1},{1,2},{9,3},{2,4},{10,5},{3,6},{11,7},{4,8},{12,9},{5,... | collective-permute-start | bytes 393224 | tf_op jit(solution)/shard_map/ppermute | solution.py:184
  28.9 6.6 %collective-permute-start.4 = (f32[1,128]{1,0:T(1,128)S(1)}, f32[1,128]{1,0:T(1,128)S(1)}, u32[]{:S(2)}, u32[]{:S(2)}) collective-permute-start(f32[1,128]{1,0:T(1,128)S(1)} %add.114), channel_id=1, source_target_pairs={{0,1},{1,0},{2,3},{3,2},{4,5},{5,4},{6,7},{7,6},{8,9},{9,8},{10,11... | collective-permute-start | bytes 1544 | tf_op jit(solution)/shard_map/ppermute | solution.py:17
  34.1 2.6 %collective-permute-start.6 = (bf16[256,512]{1,0:T(8,128)(2,1)S(1)}, bf16[256,512]{1,0:T(8,128)(2,1)S(1)}, u32[]{:S(2)}, u32[]{:S(2)}) collective-permute-start(bf16[256,512]{1,0:T(8,128)(2,1)S(1)} %maximum_select_fusion), channel_id=1, source_target_pairs={{0,8},{8,0},{1,9},{9,1},{2,10},{10,2},{3,11},{11,3},{4,12},{12,4},... | collective-permute-start | bytes 786440 | tf_op jit(solution)/shard_map/ppermute | solution.py:17
  35.5 1.1 collective-permute-start.5
  36.9 1.4 copy-start
  42.3 25.7 %collective-permute-start.9 = (bf16[2,2,256,512]{3,2,1,0:T(8,128)(2,1)S(1)}, bf16[2,2,256,512]{3,2,1,0:T(8,128)(2,1)}, u32[]{:S(2)}, u32[]{:S(2)}) collective-permute-start(bf16[2,2,256,512]{3,2,1,0:T(8,128)(2,1)S(1)} %sums.8), channel_id=1, source_target_pairs={{0,1},{1,0},{2,3},{3,2},{4,5},{5,4},{6,7},{7,6},{8,9},{9,8},{10,11... | collective-permute-start | bytes 3145736 | tf_op jit(solution)/shard_map/ppermute | solution.py:17
  47.5 3.2 %copy-start.2 = (bf16[2,2,512,512]{3,2,1,0:T(8,128)(2,1)S(1)}, bf16[2,2,512,512]{3,2,1,0:T(8,128)(2,1)}, u32[]{:S(2)}) copy-start(bf16[2,2,512,512]{3,2,1,0:T(8,128)(2,1)} %cut.7) | copy-start | bytes 6291460
  50.6 64.3 %collective-permute-start.15 = (bf16[2,2,512,512]{3,2,1,0:T(8,128)(2,1)}, bf16[2,2,512,512]{3,2,1,0:T(8,128)(2,1)S(1)}, u32[]{:S(2)}, u32[]{:S(2)}) collective-permute-start(bf16[2,2,512,512]{3,2,1,0:T(8,128)(2,1)} %cut.8), channel_id=1, source_target_pairs={{0,8},{8,0},{1,9},{9,1},{2,10},{10,2},{3,11},{11,3},{4,12},{12,4},... | collective-permute-start | bytes 6291464 | tf_op jit(solution)/shard_map/ppermute | solution.py:17
  50.7 57.9 %collective-permute-start.14 = (bf16[2,2,512,512]{3,2,1,0:T(8,128)(2,1)S(1)}, bf16[2,2,512,512]{3,2,1,0:T(8,128)(2,1)S(1)}, u32[]{:S(2)}, u32[]{:S(2)}) collective-permute-start(bf16[2,2,512,512]{3,2,1,0:T(8,128)(2,1)S(1)} %copy-done.2), channel_id=1, source_target_pairs={{0,8},{8,0},{1,9},{9,1},{2,10},{10,2},{3,11},{11,3},{4,12},{12,4},... | collective-permute-start | bytes 6291464 | tf_op jit(solution)/shard_map/ppermute | solution.py:17
  56.0 15.0 %copy-start.5 = (f32[2,256,512]{2,1,0:T(8,128)S(1)}, f32[2,256,512]{2,1,0:T(8,128)}, u32[]{:S(2)}) copy-start(f32[2,256,512]{2,1,0:T(8,128)} %get-tuple-element.51) | copy-start | bytes 3145732
  68.1 24.9 %collective-permute-start.12 = (bf16[2,2,256,512]{3,2,1,0:T(8,128)(2,1)S(1)}, bf16[2,2,256,512]{3,2,1,0:T(8,128)(2,1)}, u32[]{:S(2)}, u32[]{:S(2)}) collective-permute-start(bf16[2,2,256,512]{3,2,1,0:T(8,128)(2,1)S(1)} %sums.10), channel_id=1, source_target_pairs={{0,1},{1,0},{2,3},{3,2},{4,5},{5,4},{6,7},{7,6},{8,9},{9,8},{10,11... | collective-permute-start | bytes 3145736 | tf_op jit(solution)/shard_map/ppermute | solution.py:17
  73.4 21.0 %collective-permute-start.11 = (bf16[2,2,256,512]{3,2,1,0:T(8,128)(2,1)}, bf16[2,2,256,512]{3,2,1,0:T(8,128)(2,1)}, u32[]{:S(2)}, u32[]{:S(2)}) collective-permute-start(bf16[2,2,256,512]{3,2,1,0:T(8,128)(2,1)} %pad_maximum_fusion), channel_id=1, source_target_pairs={{2,4},{3,5},{4,2},{5,3},{10,12},{11,13},{12,10},{13,11},{18,20},{1... | collective-permute-start | bytes 3145736 | tf_op jit(solution)/shard_map/ppermute | solution.py:266
  75.0 26.6 %collective-permute-start.13 = (bf16[2,2,256,512]{3,2,1,0:T(8,128)(2,1)}, bf16[2,2,256,512]{3,2,1,0:T(8,128)(2,1)S(1)}, u32[]{:S(2)}, u32[]{:S(2)}) collective-permute-start(bf16[2,2,256,512]{3,2,1,0:T(8,128)(2,1)} %pad_maximum_fusion), channel_id=1, source_target_pairs={{0,2},{1,3},{6,4},{7,5},{8,10},{9,11},{14,12},{15,13},{16,18},{17,... | collective-permute-start | bytes 3145736 | tf_op jit(solution)/shard_map/ppermute | solution.py:265
  92.9 27.4 %collective-permute-start.16 = (bf16[2,2,256,512]{3,2,1,0:T(8,128)(2,1)S(1)}, bf16[2,2,256,512]{3,2,1,0:T(8,128)(2,1)}, u32[]{:S(2)}, u32[]{:S(2)}) collective-permute-start(bf16[2,2,256,512]{3,2,1,0:T(8,128)(2,1)S(1)} %sums.12), channel_id=1, source_target_pairs={{0,1},{1,0},{2,3},{3,2},{4,5},{5,4},{6,7},{7,6},{8,9},{9,8},{10,11... | collective-permute-start | bytes 3145736 | tf_op jit(solution)/shard_map/ppermute | solution.py:17
  106.0 33.8 %collective-permute-start.18 = (bf16[2,256,512]{2,1,0:T(8,128)(2,1)}, bf16[2,256,512]{2,1,0:T(8,128)(2,1)S(1)}, u32[]{:S(2)}, u32[]{:S(2)}) collective-permute-start(bf16[2,256,512]{2,1,0:T(8,128)(2,1)} %fusion.6), channel_id=1, source_target_pairs={{0,2},{1,3},{2,0},{3,1},{4,6},{5,7},{6,4},{7,5},{8,10},{9,11},{10,... | collective-permute-start | bytes 1572872 | tf_op jit(solution)/shard_map/ppermute | solution.py:17
  108.4 31.4 %collective-permute-start.19 = (bf16[2,256,512]{2,1,0:T(8,128)(2,1)}, bf16[2,256,512]{2,1,0:T(8,128)(2,1)}, u32[]{:S(2)}, u32[]{:S(2)}) collective-permute-start(bf16[2,256,512]{2,1,0:T(8,128)(2,1)} %fusion.7), channel_id=1, source_target_pairs={{0,4},{1,5},{2,6},{3,7},{4,0},{5,1},{6,2},{7,3},{8,12},{9,13},{10,... | collective-permute-start | bytes 1572872 | tf_op jit(solution)/shard_map/ppermute | solution.py:17
  108.7 1.4 copy-start.3
  114.9 8.7 %copy-start.4 = (f32[2,256,512]{2,1,0:T(8,128)S(1)}, f32[2,256,512]{2,1,0:T(8,128)}, u32[]{:S(2)}) copy-start(f32[2,256,512]{2,1,0:T(8,128)} %get-tuple-element.66) | copy-start | bytes 3145732
  114.9 1.4 copy-start.1
  120.4 34.6 %collective-permute-start.17 = (bf16[2,2,256,512]{3,2,1,0:T(8,128)(2,1)S(1)}, bf16[2,2,256,512]{3,2,1,0:T(8,128)(2,1)}, u32[]{:S(2)}, u32[]{:S(2)}) collective-permute-start(bf16[2,2,256,512]{3,2,1,0:T(8,128)(2,1)S(1)} %sums.14), channel_id=1, source_target_pairs={{0,1},{1,0},{2,3},{3,2},{4,5},{5,4},{6,7},{7,6},{8,9},{9,8},{10,11... | collective-permute-start | bytes 3145736 | tf_op jit(solution)/shard_map/ppermute | solution.py:17
  125.6 26.0 %collective-permute-start.21 = (bf16[2,256,512]{2,1,0:T(8,128)(2,1)}, bf16[2,256,512]{2,1,0:T(8,128)(2,1)}, u32[]{:S(2)}, u32[]{:S(2)}) collective-permute-start(bf16[2,256,512]{2,1,0:T(8,128)(2,1)} %fusion.4), channel_id=1, source_target_pairs={{0,2},{1,3},{2,0},{3,1},{4,6},{5,7},{6,4},{7,5},{8,10},{9,11},{10,... | collective-permute-start | bytes 1572872 | tf_op jit(solution)/shard_map/ppermute | solution.py:17
  127.6 27.3 %collective-permute-start.22 = (bf16[2,256,512]{2,1,0:T(8,128)(2,1)}, bf16[2,256,512]{2,1,0:T(8,128)(2,1)}, u32[]{:S(2)}, u32[]{:S(2)}) collective-permute-start(bf16[2,256,512]{2,1,0:T(8,128)(2,1)} %fusion.5), channel_id=1, source_target_pairs={{0,4},{1,5},{2,6},{3,7},{4,0},{5,1},{6,2},{7,3},{8,12},{9,13},{10,... | collective-permute-start | bytes 1572872 | tf_op jit(solution)/shard_map/ppermute | solution.py:17
  158.2 1.4 collective-permute-start.20
  158.4 1.5 collective-permute-start.23

commit v3 on v2

--- a/solution.py
+++ b/solution.py
@@ -21,40 +21,46 @@
     return lax.optimization_barrier((value, *earlier))[0]
 
 
-def cut_kernel(places, lanes, at_ref, gate_ref, up_ref, out_ref, held, in_sems, out_sems):
+def cut_kernel(groups, lanes, at_ref, gate_ref, up_ref, *refs):
+    out_refs, (held, in_sems, out_sems) = refs[:-3], refs[-3:]
     weights = (gate_ref, up_ref)
-
-    def copy_in(n, i):
-        offset, start = places[n]
-        first = pl.multiple_of((at_ref[0] ^ offset) * at_ref[2] + at_ref[1] + start, LANES)
-        return pltpu.make_async_copy(weights[i].at[:, pl.ds(first, lanes)], held.at[n, i], in_sems.at[n, i])
-
-    def copy_out(n, i):
-        return pltpu.make_async_copy(held.at[n, i], out_ref.at[n, i], out_sems.at[n, i])
-
-    every = [(n, i) for n in range(len(places)) for i in range(2)]
-    for n, i in every:
-        copy_in(n, i).start()
-    for n, i in every:
-        copy_in(n, i).wait()
-        copy_out(n, i).start()
-    for n, i in every:
-        copy_out(n, i).wait()
-
-
-def cut(at, gate_weight, up_weight, places, lanes):
+    every = []
+    for places, out_ref in zip(groups, out_refs):
+        for n, (offset, start) in enumerate(places):
+            first = pl.multiple_of((at_ref[0] ^ offset) * at_ref[2] + at_ref[1] + start, LANES)
+            for i in range(2):
+                k = len(every)
+                every.append(
+                    (
+                        pltpu.make_async_copy(weights[i].at[:, pl.ds(first, lanes)], held.at[k], in_sems.at[k]),
+                        pltpu.make_async_copy(held.at[k], out_ref.at[n, i], out_sems.at[k]),
+                    )
+                )
+    ahead = 6
+    for copy_in, _ in every[:ahead]:
+        copy_in.start()
+    for k, (copy_in, copy_out) in enumerate(every):
+        copy_in.wait()
+        copy_out.start()
+        if k + ahead < len(every):
+            every[k + ahead][0].start()
+    for _, copy_out in every:
+        copy_out.wait()
+
+
+def cut(at, gate_weight, up_weight, groups, lanes):
     depth = gate_weight.shape[0]
-    count = len(places)
+    count = 2 * sum(map(len, groups))
     hbm = pl.BlockSpec(memory_space=pltpu.HBM)
     return pl.pallas_call(
-        functools.partial(cut_kernel, places, lanes),
+        functools.partial(cut_kernel, groups, lanes),
         in_specs=[pl.BlockSpec(memory_space=pltpu.SMEM), hbm, hbm],
-        out_specs=hbm,
-        out_shape=jax.ShapeDtypeStruct((count, 2, depth, lanes), jnp.bfloat16),
+        out_specs=[hbm] * len(groups),
+        out_shape=[jax.ShapeDtypeStruct((len(places), 2, depth, lanes), jnp.bfloat16) for places in groups],
         scratch_shapes=[
-            pltpu.VMEM((count, 2, depth, lanes), jnp.bfloat16),
-            pltpu.SemaphoreType.DMA((count, 2)),
-            pltpu.SemaphoreType.DMA((count, 2)),
+            pltpu.VMEM((count, depth, lanes), jnp.bfloat16),
+            pltpu.SemaphoreType.DMA((count,)),
+            pltpu.SemaphoreType.DMA((count,)),
         ],
         compiler_params=pltpu.CompilerParams(vmem_limit_bytes=VMEM_LIMIT),
         name="cut",
@@ -168,11 +174,15 @@
         latest[:] = [value]
         return value
 
-    def fetch(units, *earlier):
-        value = emit(cut(in_turn(partners, *earlier), gate_weight, up_weight, tuple(map(place, units)), lanes))
-        value = exchange(value, "wide", 1)
-        for n, unit in enumerate(units):
-            theirs[unit] = (value, n)
+    def fetch(*groups):
+        values = cut(
+            in_turn(partners), gate_weight, up_weight, tuple(tuple(map(place, units)) for units in groups), lanes
+        )
+        emit(values[0])
+        for units, value in zip(groups, values):
+            value = exchange(value, "wide", 1)
+            for n, unit in enumerate(units):
+                theirs[unit] = (value, n)
 
     raw = []
     for flip in range(2):
@@ -187,20 +197,12 @@
     emit(squares)
     if pairs == 4:
         fetch([(3, 1, 0), (3, 1, 1)])
-    total = squares + exchange(squares, "tensor", 2)
-    if pairs == 4:
-        emit(total)
-        fetch([(3, 0, 0), (3, 0, 1), (2, 1, 0), (1, 1, 0)])
-    raw = after(jnp.where(shard % 2 == 1, jnp.concatenate(raw[::-1]), jnp.concatenate(raw)), total)
-    raw_other = exchange(raw, "wide", 1)
-    bit = 4
-    while bit < shards:
-        total = total + exchange(total, "tensor", bit)
-        bit *= 2
-    if pairs == 4:
-        emit(total)
-        fetch([(2, 1, 1), (1, 1, 1), (2, 0, 0), (1, 0, 0), (0, 0, 0), (0, 0, 1)])
-    total = total + exchange(total, "tensor", 1)
+    total = squares
+    for p in range(1, pairs):
+        total = total + exchange(squares, "tensor", 2 * p)
+    raw = jnp.where(shard % 2 == 1, jnp.concatenate(raw[::-1]), jnp.concatenate(raw))
+    raw_other = exchange(after(raw, total), "wide", 1)
+    total = total + exchange(after(total, raw), "tensor", 1)
     scale = lax.rsqrt(total / features + EPS)
     scale_other = exchange(scale, "wide", 1)
     scales = jnp.where(
@@ -213,6 +215,14 @@
         [(v.astype(jnp.float32) * scales * g).astype(jnp.bfloat16) for v, g in zip((raw, raw_other), gains)], axis=1
     )
 
+    emit(normed)
+    if pairs == 4:
+        latest.append(theirs[3, 1, 0][0])
+        fetch(
+            [(3, 0, 0), (3, 0, 1), (2, 1, 0), (1, 1, 0)],
+            [(2, 1, 1), (1, 1, 1), (2, 0, 0), (1, 0, 0), (0, 0, 0), (0, 0, 1)],
+        )
+
     masks = jnp.concatenate(
         [
             lax.dynamic_slice_in_dim(mask, r // side, depth // side, 0)
@@ -256,8 +266,7 @@
         middle = tensor_pairs(((1, 2), (2, 1)))
 
         pair3 = exchange(chip_sums([(3, 1, 0), (3, 1, 1)]), "tensor", 1)
-        fetch([(2, 0, 1), (1, 0, 1)])
-        fetch([(0, 1, 0), (0, 1, 1)])
+        fetch([(2, 0, 1), (1, 0, 1)], [(0, 1, 0), (0, 1, 1)])
         near3 = chip_sums([(3, 0, 0), (3, 0, 1)], stacked=False)
         far_a = chip_sums([(2, 1, 0), (1, 1, 0)])
         pair_a = exchange(in_turn(far_a, pair3), "tensor", 1)
@@ -275,12 +284,9 @@
         second_b = exchange(add(near_b[0], pair_b[0], relay[1]), "tensor", 4)
         first_b = exchange(add(near_b[1], pair_b[1]), "tensor", 2)
         own = chip_sums([(0, 0, 0), (0, 0, 1)], stacked=False)
-        left, right = [], []
-        for h, second, first in ((0, second_a, first_a), (1, second_b, first_b)):
-            one, other = give(finish(own[h], pair_0[h], first, second, across[h]))
-            left.append(one)
-            right.append(other)
-        return jnp.concatenate(left + right, axis=1)
+        one, other = give(finish(own[0], pair_0[0], first_a, second_a, across[0]))
+        two, another = give(finish(own[1], pair_0[1], first_b, second_b, across[1]))
+        return jnp.concatenate([one, two, other, another], axis=1)
     received = []
     for p in range(pairs - 1, -1, -1):
         fetch([(p, 1, 0), (p, 0, 0)])

time: 162 us -> 153 us (0.944)
  other arithmetic: 18.7 us -> 11.9 us
  Pallas kernels: 54.9 us -> 51.9 us
  starting transfers between devices: 34 us -> 36.4 us
    convert_element_type x6, other arithmetic: 11 us -> 4.5 us  [add(): return emit(total.astype(jnp.bfloat16))]
    pallas_call x5 -> x3, Pallas kernels: 19.6 us -> 16.5 us  [cut(): pl.pallas_call(functools.partial(cut_kernel, groups, lanes), in_specs=[pl...]
    ppermute x20 -> x21, starting transfers between devices: 24.7 us -> 27 us  [exchange(): return lax.ppermute(value, axis, [(i, i ^ bit) for i in range(size)])]
    ppermute x1, waiting for transfers between devices: 7.24 us -> 5.44 us  [local(): relay = lax.ppermute(third, 'tensor', by_neighbour)]
    ppermute x2, waiting for transfers between devices: 0.22 us -> 1.87 us  [local(): raw.append(lax.ppermute(piece, ('wide', 'tensor'), moves))]
    ppermute x20 -> x21, waiting for transfers between devices: 40.4 us -> 41 us  [exchange(): return lax.ppermute(value, axis, [(i, i ^ bit) for i in range(size)])]
  transfers between devices with their start and end apart: 24 -> 25, of which waited for: 13 -> 13; matrix products, arithmetic and copies ran while one was open for 9% -> 5% of each run, Pallas kernels for 30% -> 26%
where the time goes in v3:
time: 153 us; the launch traced here: 152 us
  Pallas kernels  51.9 us (34%)
  waiting for transfers between devices  48.4 us (32%)
  starting transfers between devices  36.4 us (24%)
  other arithmetic  11.9 us (8%)
  local copies, waits for them, and re-layouts  3.67 us (2%)
    ppermute x21, waiting for transfers between devices, exchange(): return lax.ppermute(value, axis, [(i, i ^ bit) for i in range(size)])  41 us
    pallas_call x8, Pallas kernels, sums(): pl.pallas_call(functools.partial(sums_kernel, places, lanes, side, stacke...  35.3 us
    ppermute x21, starting transfers between devices, exchange(): return lax.ppermute(value, axis, [(i, i ^ bit) for i in range(size)])  27 us
    pallas_call x3, Pallas kernels, cut(): pl.pallas_call(functools.partial(cut_kernel, groups, lanes), in_specs=[pl...  16.5 us
    ppermute x1, waiting for transfers between devices, local(): relay = lax.ppermute(third, 'tensor', by_neighbour)  5.44 us
    ppermute x1, starting transfers between devices, local(): relay = lax.ppermute(third, 'tensor', by_neighbour)  5.32 us
    convert_element_type x6, other arithmetic, add(): return emit(total.astype(jnp.bfloat16))  4.5 us
  transfers between devices with their start and end apart: 25, of which 13 were waited for; matrix products, arithmetic and copies ran while one was open for 5% of the time, Pallas kernels for 26%

profile of v3, /device:TPU:0, one launch (start us, length us, event | category | flops | bytes accessed | tf_op | source)
XLA Modules:
  0.0 152.5 jit_solution(17175538713401843402)
XLA Ops:
  0.0 1.1 multiply_reduce_fusion
  1.1 0.1 pad_add_fusion.at_ref
  1.2 3.0 %cut.3 = bf16[2,2,512,512]{3,2,1,0:T(8,128)(2,1)} custom-call(s32[3]{0:T(128)S(1)} %pad_add_fusion.at_ref, bf16[512,16384]{1,0:T(8,128)(2,1)} %gate_ref.21, bf16[512,16384]{1,0:T(8,128)(2,1)} %up_ref.21), custom_call_target="tpu_custom_call" | custom-call | tf_op jit(solution)/shard_map/cut/pallas_call | solution.py:55
  4.2 0.5 collective-permute-start.8
  4.7 4.7 %collective-permute-start.4 = (f32[1,128]{1,0:T(1,128)S(1)}, f32[1,128]{1,0:T(1,128)S(1)}, u32[]{:S(2)}, u32[]{:S(2)}) collective-permute-start(f32[1,128]{1,0:T(1,128)S(1)} %bitcast.91), channel_id=1, source_target_pairs={{0,6},{1,7},{2,4},{3,5},{4,2},{5,3},{6,0},{7,1},{8,14},{9,15},{10,... | collective-permute-start | bytes 1544 | tf_op jit(solution)/shard_map/ppermute | solution.py:17
  9.4 0.7 collective-permute-start.2
  10.1 1.7 %collective-permute-start = (bf16[128,512]{1,0:T(8,128)(2,1)S(1)}, bf16[128,512]{1,0:T(8,128)(2,1)S(1)}, u32[]{:S(2)}, u32[]{:S(2)}) collective-permute-start(bf16[128,512]{1,0:T(8,128)(2,1)S(1)} %get-tuple-element.85), channel_id=1, source_target_pairs={{8,0},{0,1},{9,2},{1,3},{10,4},{2,5},{11,6},{3,7},{12,8},{4,9},{13... | collective-permute-start | bytes 393224 | tf_op jit(solution)/shard_map/ppermute | solution.py:194
  11.8 0.7 collective-permute-start.1
  12.4 1.4 collective-permute-done.3
  13.8 1.9 %collective-permute-done = bf16[128,512]{1,0:T(8,128)(2,1)S(1)} collective-permute-done((bf16[128,512]{1,0:T(8,128)(2,1)S(1)}, bf16[128,512]{1,0:T(8,128)(2,1)S(1)}, u32[]{:S(2)}, u32[]{:S(2)}) %collective-permute-start) | collective-permute-done | bytes 131104 | tf_op jit(solution)/shard_map/ppermute | solution.py:194
  15.8 5.5 %collective-permute-start.5 = (f32[1,128]{1,0:T(1,128)S(1)}, f32[1,128]{1,0:T(1,128)S(1)}, u32[]{:S(2)}, u32[]{:S(2)}) collective-permute-start(f32[1,128]{1,0:T(1,128)S(1)} %add_add_fusion), channel_id=1, source_target_pairs={{0,1},{1,0},{2,3},{3,2},{4,5},{5,4},{6,7},{7,6},{8,9},{9,8},{10,11... | collective-permute-start | bytes 1544 | tf_op jit(solution)/shard_map/ppermute | solution.py:17
  21.3 1.5 collective-permute-done.5
  22.8 0.8 fusion.14
  23.6 0.3 collective-permute-done.6
  23.9 0.2 multiply_convert_fusion.1
  24.2 8.9 %cut.4 = (bf16[4,2,512,512]{3,2,1,0:T(8,128)(2,1)}, bf16[6,2,512,512]{3,2,1,0:T(8,128)(2,1)}) custom-call(s32[3]{0:T(128)S(1)} %pad_add_fusion.at_ref, bf16[512,16384]{1,0:T(8,128)(2,1)} %gate_ref.21, bf16[512,16384]{1,0:T(8,128)(2,1)} %up_ref.21), custom_call_target="tpu_custom_call" | custom-call | tf_op jit(solution)/shard_map/cut/pallas_call | solution.py:55
  33.1 0.3 collective-permute-start.11
  33.4 0.3 collective-permute-start.9
  33.7 0.1 pad_add_fusion.1.at_ref
  33.8 0.8 dynamic-slice_convert_fusion.1
  34.6 4.0 %sums.8 = bf16[2,2,256,512]{3,2,1,0:T(8,128)(2,1)S(1)} custom-call(s32[3]{0:T(128)S(1)} %pad_add_fusion.1.at_ref, bf16[256,1024]{1,0:T(8,128)(2,1)S(1)} %pad_maximum_fusion.1.x_ref, bf16[512,16384]{1,0:T(8,128)(2,1)} %gate_ref.21, bf16[512,16384]{1,0:T(8,128)(2,1)} %up_ref.21, bf16[2,2,512,512]{3,2,1,0:T(8,128)(2,1)} %copy-done, ...), custom_call_target="tpu_custom_call" | custom-call | tf_op jit(solution)/shard_map/sums/pallas_call | solution.py:126
  38.6 2.1 %collective-permute-start.10 = (bf16[2,2,256,512]{3,2,1,0:T(8,128)(2,1)S(1)}, bf16[2,2,256,512]{3,2,1,0:T(8,128)(2,1)S(1)}, u32[]{:S(2)}, u32[]{:S(2)}) collective-permute-start(bf16[2,2,256,512]{3,2,1,0:T(8,128)(2,1)S(1)} %sums.8), channel_id=1, source_target_pairs={{0,1},{1,0},{2,3},{3,2},{4,5},{5,4},{6,7},{7,6},{8,9},{9,8},{10,11... | collective-permute-start | bytes 3145736 | tf_op jit(solution)/shard_map/ppermute | solution.py:17
  40.7 4.7 %cut.5 = (bf16[2,2,512,512]{3,2,1,0:T(8,128)(2,1)}, bf16[2,2,512,512]{3,2,1,0:T(8,128)(2,1)}) custom-call(s32[3]{0:T(128)S(1)} %pad_add_fusion.at_ref, bf16[512,16384]{1,0:T(8,128)(2,1)} %gate_ref.21, bf16[512,16384]{1,0:T(8,128)(2,1)} %up_ref.21), custom_call_target="tpu_custom_call" | custom-call | tf_op jit(solution)/shard_map/cut/pallas_call | solution.py:55
  45.4 0.5 collective-permute-start.16
  45.9 3.8 %collective-permute-done.9.theirs_ref = bf16[4,2,512,512]{3,2,1,0:T(8,128)(2,1)} collective-permute-done((bf16[4,2,512,512]{3,2,1,0:T(8,128)(2,1)}, bf16[4,2,512,512]{3,2,1,0:T(8,128)(2,1)}, u32[]{:S(2)}, u32[]{:S(2)}) %collective-permute-start.9) | collective-permute-done | bytes 4194336 | tf_op jit(solution)/shard_map/ppermute | solution.py:17
  49.7 4.8 %sums.9 = (f32[2,256,512]{2,1,0:T(8,128)S(1)}, f32[2,256,512]{2,1,0:T(8,128)}) custom-call(s32[3]{0:T(128)S(1)} %pad_add_fusion.1.at_ref, bf16[256,1024]{1,0:T(8,128)(2,1)S(1)} %pad_maximum_fusion.1.x_ref, bf16[512,16384]{1,0:T(8,128)(2,1)} %gate_ref.21, bf16[512,16384]{1,0:T(8,128)(2,1)} %up_ref.21, ...), custom_call_target="tpu_custom_call" | custom-call | tf_op jit(solution)/shard_map/sums/pallas_call | solution.py:126
  54.5 4.0 %sums.10 = bf16[2,2,256,512]{3,2,1,0:T(8,128)(2,1)S(1)} custom-call(s32[3]{0:T(128)S(1)} %pad_add_fusion.1.at_ref, bf16[256,1024]{1,0:T(8,128)(2,1)S(1)} %pad_maximum_fusion.1.x_ref, bf16[512,16384]{1,0:T(8,128)(2,1)} %gate_ref.21, bf16[512,16384]{1,0:T(8,128)(2,1)} %up_ref.21, bf16[4,2,512,512]{3,2,1,0:T(8,128)(2,1)} %collective-permute-done.9.theirs_ref, ...), custom_call_target="tpu_custom_call" | custom-call | tf_op jit(solution)/shard_map/sums/pallas_call | solution.py:126
  58.5 5.7 %collective-permute-done.10 = bf16[2,2,256,512]{3,2,1,0:T(8,128)(2,1)S(1)} collective-permute-done((bf16[2,2,256,512]{3,2,1,0:T(8,128)(2,1)S(1)}, bf16[2,2,256,512]{3,2,1,0:T(8,128)(2,1)S(1)}, u32[]{:S(2)}, u32[]{:S(2)}) %collective-permute-start.10) | collective-permute-done | bytes 1048608 | tf_op jit(solution)/shard_map/ppermute | solution.py:17
  64.2 1.7 %collective-permute-start.13 = (bf16[2,2,256,512]{3,2,1,0:T(8,128)(2,1)S(1)}, bf16[2,2,256,512]{3,2,1,0:T(8,128)(2,1)S(1)}, u32[]{:S(2)}, u32[]{:S(2)}) collective-permute-start(bf16[2,2,256,512]{3,2,1,0:T(8,128)(2,1)S(1)} %sums.10), channel_id=1, source_target_pairs={{0,1},{1,0},{2,3},{3,2},{4,5},{5,4},{6,7},{7,6},{8,9},{9,8},{10,11... | collective-permute-start | bytes 3145736 | tf_op jit(solution)/shard_map/ppermute | solution.py:17
  66.0 0.2 fusion.9
  66.2 0.2 fusion.8
  66.3 1.1 pad_maximum_fusion
  67.4 1.6 %collective-permute-start.12 = (bf16[2,2,256,512]{3,2,1,0:T(8,128)(2,1)}, bf16[2,2,256,512]{3,2,1,0:T(8,128)(2,1)}, u32[]{:S(2)}, u32[]{:S(2)}) collective-permute-start(bf16[2,2,256,512]{3,2,1,0:T(8,128)(2,1)} %pad_maximum_fusion), channel_id=1, source_target_pairs={{2,4},{3,5},{4,2},{5,3},{10,12},{11,13},{12,10},{13,11},{18,20},{1... | collective-permute-start | bytes 3145736 | tf_op jit(solution)/shard_map/ppermute | solution.py:275
  69.1 5.3 %collective-permute-start.14 = (bf16[2,2,256,512]{3,2,1,0:T(8,128)(2,1)}, bf16[2,2,256,512]{3,2,1,0:T(8,128)(2,1)S(1)}, u32[]{:S(2)}, u32[]{:S(2)}) collective-permute-start(bf16[2,2,256,512]{3,2,1,0:T(8,128)(2,1)} %pad_maximum_fusion), channel_id=1, source_target_pairs={{0,2},{1,3},{6,4},{7,5},{8,10},{9,11},{14,12},{15,13},{16,18},{17,... | collective-permute-start | bytes 3145736 | tf_op jit(solution)/shard_map/ppermute | solution.py:274
  74.4 4.8 %sums.11 = (f32[2,256,512]{2,1,0:T(8,128)S(1)}, f32[2,256,512]{2,1,0:T(8,128)}) custom-call(s32[3]{0:T(128)S(1)} %pad_add_fusion.1.at_ref, bf16[256,1024]{1,0:T(8,128)(2,1)S(1)} %pad_maximum_fusion.1.x_ref, bf16[512,16384]{1,0:T(8,128)(2,1)} %gate_ref.21, bf16[512,16384]{1,0:T(8,128)(2,1)} %up_ref.21, ...), custom_call_target="tpu_custom_call" | custom-call | tf_op jit(solution)/shard_map/sums/pallas_call | solution.py:126
  79.2 4.0 %sums.12 = bf16[2,2,256,512]{3,2,1,0:T(8,128)(2,1)S(1)} custom-call(s32[3]{0:T(128)S(1)} %pad_add_fusion.1.at_ref, bf16[256,1024]{1,0:T(8,128)(2,1)S(1)} %pad_maximum_fusion.1.x_ref, bf16[512,16384]{1,0:T(8,128)(2,1)} %gate_ref.21, bf16[512,16384]{1,0:T(8,128)(2,1)} %up_ref.21, bf16[6,2,512,512]{3,2,1,0:T(8,128)(2,1)} %collective-permute-done.11.theirs_ref, ...), custom_call_target="tpu_custom_call" | custom-call | tf_op jit(solution)/shard_map/sums/pallas_call | solution.py:126
  83.3 5.7 %collective-permute-done.13 = bf16[2,2,256,512]{3,2,1,0:T(8,128)(2,1)S(1)} collective-permute-done((bf16[2,2,256,512]{3,2,1,0:T(8,128)(2,1)S(1)}, bf16[2,2,256,512]{3,2,1,0:T(8,128)(2,1)S(1)}, u32[]{:S(2)}, u32[]{:S(2)}) %collective-permute-start.13) | collective-permute-done | bytes 1048608 | tf_op jit(solution)/shard_map/ppermute | solution.py:17
  89.0 1.4 collective-permute-start.17
  90.4 5.4 %collective-permute-done.14 = bf16[2,2,256,512]{3,2,1,0:T(8,128)(2,1)S(1)} collective-permute-done((bf16[2,2,256,512]{3,2,1,0:T(8,128)(2,1)}, bf16[2,2,256,512]{3,2,1,0:T(8,128)(2,1)S(1)}, u32[]{:S(2)}, u32[]{:S(2)}) %collective-permute-start.14) | collective-permute-done | bytes 1048608 | tf_op jit(solution)/shard_map/ppermute | solution.py:274
  95.8 1.1 fusion.7
  96.9 1.0 fusion.6
  97.9 2.4 %collective-permute-start.19 = (bf16[2,256,512]{2,1,0:T(8,128)(2,1)}, bf16[2,256,512]{2,1,0:T(8,128)(2,1)S(1)}, u32[]{:S(2)}, u32[]{:S(2)}) collective-permute-start(bf16[2,256,512]{2,1,0:T(8,128)(2,1)} %fusion.6), channel_id=1, source_target_pairs={{0,2},{1,3},{2,0},{3,1},{4,6},{5,7},{6,4},{7,5},{8,10},{9,11},{10,... | collective-permute-start | bytes 1572872 | tf_op jit(solution)/shard_map/ppermute | solution.py:17
  100.3 1.0 collective-permute-start.20
  101.3 1.4 copy-done.2
  102.8 4.8 %sums.13 = (f32[2,256,512]{2,1,0:T(8,128)S(1)}, f32[2,256,512]{2,1,0:T(8,128)}) custom-call(s32[3]{0:T(128)S(1)} %pad_add_fusion.1.at_ref, bf16[256,1024]{1,0:T(8,128)(2,1)S(1)} %pad_maximum_fusion.1.x_ref, bf16[512,16384]{1,0:T(8,128)(2,1)} %gate_ref.21, bf16[512,16384]{1,0:T(8,128)(2,1)} %up_ref.21, bf16[2,2,512,512]{3,2,1,0:T(8,128)(2,1)} %copy-done.2, ...), custom_call_target="tpu_custom_call" | custom-call | tf_op jit(solution)/shard_map/sums/pallas_call | solution.py:126
  107.6 1.4 copy-done.1
  109.0 4.0 %sums.14 = bf16[2,2,256,512]{3,2,1,0:T(8,128)(2,1)S(1)} custom-call(s32[3]{0:T(128)S(1)} %pad_add_fusion.1.at_ref, bf16[256,1024]{1,0:T(8,128)(2,1)S(1)} %pad_maximum_fusion.1.x_ref, bf16[512,16384]{1,0:T(8,128)(2,1)} %gate_ref.21, bf16[512,16384]{1,0:T(8,128)(2,1)} %up_ref.21, bf16[2,2,512,512]{3,2,1,0:T(8,128)(2,1)} %copy-done.1, ...), custom_call_target="tpu_custom_call" | custom-call | tf_op jit(solution)/shard_map/sums/pallas_call | solution.py:126
  113.0 1.6 %collective-permute-start.18 = (bf16[2,2,256,512]{3,2,1,0:T(8,128)(2,1)S(1)}, bf16[2,2,256,512]{3,2,1,0:T(8,128)(2,1)S(1)}, u32[]{:S(2)}, u32[]{:S(2)}) collective-permute-start(bf16[2,2,256,512]{3,2,1,0:T(8,128)(2,1)S(1)} %sums.14), channel_id=1, source_target_pairs={{0,1},{1,0},{2,3},{3,2},{4,5},{5,4},{6,7},{7,6},{8,9},{9,8},{10,11... | collective-permute-start | bytes 3145736 | tf_op jit(solution)/shard_map/ppermute | solution.py:17
  114.6 1.1 fusion.5
  115.7 1.0 fusion.4
  116.7 2.0 %collective-permute-start.22 = (bf16[2,256,512]{2,1,0:T(8,128)(2,1)}, bf16[2,256,512]{2,1,0:T(8,128)(2,1)}, u32[]{:S(2)}, u32[]{:S(2)}) collective-permute-start(bf16[2,256,512]{2,1,0:T(8,128)(2,1)} %fusion.4), channel_id=1, source_target_pairs={{0,2},{1,3},{2,0},{3,1},{4,6},{5,7},{6,4},{7,5},{8,10},{9,11},{10,... | collective-permute-start | bytes 1572872 | tf_op jit(solution)/shard_map/ppermute | solution.py:17
  118.7 1.7 %collective-permute-start.23 = (bf16[2,256,512]{2,1,0:T(8,128)(2,1)}, bf16[2,256,512]{2,1,0:T(8,128)(2,1)}, u32[]{:S(2)}, u32[]{:S(2)}) collective-permute-start(bf16[2,256,512]{2,1,0:T(8,128)(2,1)} %fusion.5), channel_id=1, source_target_pairs={{0,4},{1,5},{2,6},{3,7},{4,0},{5,1},{6,2},{7,3},{8,12},{9,13},{10,... | collective-permute-start | bytes 1572872 | tf_op jit(solution)/shard_map/ppermute | solution.py:17
  120.3 4.8 %sums.15 = (f32[2,256,512]{2,1,0:T(8,128)S(1)}, f32[2,256,512]{2,1,0:T(8,128)}) custom-call(s32[3]{0:T(128)S(1)} %pad_add_fusion.1.at_ref, bf16[256,1024]{1,0:T(8,128)(2,1)S(1)} %pad_maximum_fusion.1.x_ref, bf16[512,16384]{1,0:T(8,128)(2,1)} %gate_ref.21, bf16[512,16384]{1,0:T(8,128)(2,1)} %up_ref.21, ...), custom_call_target="tpu_custom_call" | custom-call | tf_op jit(solution)/shard_map/sums/pallas_call | solution.py:126
  125.1 7.1 %collective-permute-done.19 = bf16[2,256,512]{2,1,0:T(8,128)(2,1)S(1)} collective-permute-done((bf16[2,256,512]{2,1,0:T(8,128)(2,1)}, bf16[2,256,512]{2,1,0:T(8,128)(2,1)S(1)}, u32[]{:S(2)}, u32[]{:S(2)}) %collective-permute-start.19) | collective-permute-done | bytes 524320 | tf_op jit(solution)/shard_map/ppermute | solution.py:17
  132.2 12.0 %collective-permute-done.22 = bf16[2,256,512]{2,1,0:T(8,128)(2,1)} collective-permute-done((bf16[2,256,512]{2,1,0:T(8,128)(2,1)}, bf16[2,256,512]{2,1,0:T(8,128)(2,1)}, u32[]{:S(2)}, u32[]{:S(2)}) %collective-permute-start.22) | collective-permute-done | bytes 524320 | tf_op jit(solution)/shard_map/ppermute | solution.py:17
  144.2 2.7 %collective-permute-done.23 = bf16[2,256,512]{2,1,0:T(8,128)(2,1)} collective-permute-done((bf16[2,256,512]{2,1,0:T(8,128)(2,1)}, bf16[2,256,512]{2,1,0:T(8,128)(2,1)}, u32[]{:S(2)}, u32[]{:S(2)}) %collective-permute-start.23) | collective-permute-done | bytes 524320 | tf_op jit(solution)/shard_map/ppermute | solution.py:17
  146.9 2.7 %convert_add_fusion.2 = (f32[2,256,512]{2,1,0:T(8,128)S(1)}, f32[2,256,512]{2,1,0:T(8,128)S(1)}) fusion(f32[2,256,512]{2,1,0:T(8,128)S(1)} %get-tuple-element.75, bf16[2,256,512]{2,1,0:T(8,128)(2,1)} %collective-permute-done.20, bf16[2,256,512]{2,1,0:T(8,128)(2,1)S(1)} %collective-permute-done.19, bf16[2,2,256,512]{3,2,1,0:T(8,128)(2,1)} %collective-permute-done.12, ...), kind=kLoop, calls=%fused_computation.5 | loop fusion | flops 4194304 | bytes 8388608 | tf_op jit(solution)/shard_map/add | solution.py:247
  149.6 0.2 fusion.13
  149.7 0.1 collective-permute-start.21
  149.8 0.2 fusion.11
  150.0 0.6 collective-permute-start.24
  150.6 0.6 collective-permute-done.21
  151.2 0.3 collective-permute-done.24
  151.6 0.8 pad_maximum_fusion.2
  (39 shorter events, 0.4 us)
Async XLA Ops:
  1.2 8.9 %copy-start.6 = (bf16[128,1024]{1,0:T(8,128)(2,1)S(1)}, bf16[128,1024]{1,0:T(8,128)(2,1)}, u32[]{:S(2)}) copy-start(bf16[128,1024]{1,0:T(8,128)(2,1)} %param.6) | copy-start | bytes 786436
  4.2 20.0 %collective-permute-start.8 = (bf16[2,2,512,512]{3,2,1,0:T(8,128)(2,1)}, bf16[2,2,512,512]{3,2,1,0:T(8,128)(2,1)S(1)}, u32[]{:S(2)}, u32[]{:S(2)}) collective-permute-start(bf16[2,2,512,512]{3,2,1,0:T(8,128)(2,1)} %cut.3), channel_id=1, source_target_pairs={{0,8},{8,0},{1,9},{9,1},{2,10},{10,2},{3,11},{11,3},{4,12},{12,4},... | collective-permute-start | bytes 6291464 | tf_op jit(solution)/shard_map/ppermute | solution.py:17
  4.7 7.1 %collective-permute-start.4 = (f32[1,128]{1,0:T(1,128)S(1)}, f32[1,128]{1,0:T(1,128)S(1)}, u32[]{:S(2)}, u32[]{:S(2)}) collective-permute-start(f32[1,128]{1,0:T(1,128)S(1)} %bitcast.91), channel_id=1, source_target_pairs={{0,6},{1,7},{2,4},{3,5},{4,2},{5,3},{6,0},{7,1},{8,14},{9,15},{10,... | collective-permute-start | bytes 1544 | tf_op jit(solution)/shard_map/ppermute | solution.py:17
  9.4 4.4 %collective-permute-start.3 = (f32[1,128]{1,0:T(1,128)S(1)}, f32[1,128]{1,0:T(1,128)S(1)}, u32[]{:S(2)}, u32[]{:S(2)}) collective-permute-start(f32[1,128]{1,0:T(1,128)S(1)} %bitcast.92), channel_id=1, source_target_pairs={{0,4},{1,5},{2,6},{3,7},{4,0},{5,1},{6,2},{7,3},{8,12},{9,13},{10,... | collective-permute-start | bytes 1544 | tf_op jit(solution)/shard_map/ppermute | solution.py:17
  9.4 4.4 %collective-permute-start.2 = (f32[1,128]{1,0:T(1,128)S(1)}, f32[1,128]{1,0:T(1,128)S(1)}, u32[]{:S(2)}, u32[]{:S(2)}) collective-permute-start(f32[1,128]{1,0:T(1,128)S(1)} %bitcast.93), channel_id=1, source_target_pairs={{0,2},{1,3},{2,0},{3,1},{4,6},{5,7},{6,4},{7,5},{8,10},{9,11},{10,... | collective-permute-start | bytes 1544 | tf_op jit(solution)/shard_map/ppermute | solution.py:17
  10.1 5.6 %collective-permute-start = (bf16[128,512]{1,0:T(8,128)(2,1)S(1)}, bf16[128,512]{1,0:T(8,128)(2,1)S(1)}, u32[]{:S(2)}, u32[]{:S(2)}) collective-permute-start(bf16[128,512]{1,0:T(8,128)(2,1)S(1)} %get-tuple-element.85), channel_id=1, source_target_pairs={{8,0},{0,1},{9,2},{1,3},{10,4},{2,5},{11,6},{3,7},{12,8},{4,9},{13... | collective-permute-start | bytes 393224 | tf_op jit(solution)/shard_map/ppermute | solution.py:194
  11.8 3.9 %collective-permute-start.1 = (bf16[128,512]{1,0:T(8,128)(2,1)S(1)}, bf16[128,512]{1,0:T(8,128)(2,1)S(1)}, u32[]{:S(2)}, u32[]{:S(2)}) collective-permute-start(bf16[128,512]{1,0:T(8,128)(2,1)S(1)} %get-tuple-element.86), channel_id=1, source_target_pairs={{0,0},{8,1},{1,2},{9,3},{2,4},{10,5},{3,6},{11,7},{4,8},{12,9},{5,... | collective-permute-start | bytes 393224 | tf_op jit(solution)/shard_map/ppermute | solution.py:194
  15.8 7.0 %collective-permute-start.5 = (f32[1,128]{1,0:T(1,128)S(1)}, f32[1,128]{1,0:T(1,128)S(1)}, u32[]{:S(2)}, u32[]{:S(2)}) collective-permute-start(f32[1,128]{1,0:T(1,128)S(1)} %add_add_fusion), channel_id=1, source_target_pairs={{0,1},{1,0},{2,3},{3,2},{4,5},{5,4},{6,7},{7,6},{8,9},{9,8},{10,11... | collective-permute-start | bytes 1544 | tf_op jit(solution)/shard_map/ppermute | solution.py:17
  21.3 2.7 %collective-permute-start.7 = (bf16[256,512]{1,0:T(8,128)(2,1)S(1)}, bf16[256,512]{1,0:T(8,128)(2,1)S(1)}, u32[]{:S(2)}, u32[]{:S(2)}) collective-permute-start(bf16[256,512]{1,0:T(8,128)(2,1)S(1)} %maximum_select_fusion), channel_id=1, source_target_pairs={{0,8},{8,0},{1,9},{9,1},{2,10},{10,2},{3,11},{11,3},{4,12},{12,4},... | collective-permute-start | bytes 786440 | tf_op jit(solution)/shard_map/ppermute | solution.py:17
  22.8 1.1 collective-permute-start.6
  24.2 8.9 %copy-start = (bf16[2,2,512,512]{3,2,1,0:T(8,128)(2,1)}, bf16[2,2,512,512]{3,2,1,0:T(8,128)(2,1)S(1)}, u32[]{:S(2)}) copy-start(bf16[2,2,512,512]{3,2,1,0:T(8,128)(2,1)S(1)} %collective-permute-done.8.theirs_ref) | copy-start | bytes 6291460
  33.1 36.0 %collective-permute-start.11 = (bf16[6,2,512,512]{3,2,1,0:T(8,128)(2,1)}, bf16[6,2,512,512]{3,2,1,0:T(8,128)(2,1)}, u32[]{:S(2)}, u32[]{:S(2)}) collective-permute-start(bf16[6,2,512,512]{3,2,1,0:T(8,128)(2,1)} %get-tuple-element.57), channel_id=1, source_target_pairs={{0,8},{8,0},{1,9},{9,1},{2,10},{10,2},{3,11},{11,3},{4,12},{12,4},... | collective-permute-start | bytes 18874376 | tf_op jit(solution)/shard_map/ppermute | solution.py:17
  33.4 16.3 %collective-permute-start.9 = (bf16[4,2,512,512]{3,2,1,0:T(8,128)(2,1)}, bf16[4,2,512,512]{3,2,1,0:T(8,128)(2,1)}, u32[]{:S(2)}, u32[]{:S(2)}) collective-permute-start(bf16[4,2,512,512]{3,2,1,0:T(8,128)(2,1)} %get-tuple-element.46), channel_id=1, source_target_pairs={{0,8},{8,0},{1,9},{9,1},{2,10},{10,2},{3,11},{11,3},{4,12},{12,4},... | collective-permute-start | bytes 12582920 | tf_op jit(solution)/shard_map/ppermute | solution.py:17
  38.6 25.6 %collective-permute-start.10 = (bf16[2,2,256,512]{3,2,1,0:T(8,128)(2,1)S(1)}, bf16[2,2,256,512]{3,2,1,0:T(8,128)(2,1)S(1)}, u32[]{:S(2)}, u32[]{:S(2)}) collective-permute-start(bf16[2,2,256,512]{3,2,1,0:T(8,128)(2,1)S(1)} %sums.8), channel_id=1, source_target_pairs={{0,1},{1,0},{2,3},{3,2},{4,5},{5,4},{6,7},{7,6},{8,9},{9,8},{10,11... | collective-permute-start | bytes 3145736 | tf_op jit(solution)/shard_map/ppermute | solution.py:17
  45.3 56.0 %collective-permute-start.15 = (bf16[2,2,512,512]{3,2,1,0:T(8,128)(2,1)}, bf16[2,2,512,512]{3,2,1,0:T(8,128)(2,1)S(1)}, u32[]{:S(2)}, u32[]{:S(2)}) collective-permute-start(bf16[2,2,512,512]{3,2,1,0:T(8,128)(2,1)} %get-tuple-element.49), channel_id=1, source_target_pairs={{0,8},{8,0},{1,9},{9,1},{2,10},{10,2},{3,11},{11,3},{4,12},{12,4},... | collective-permute-start | bytes 6291464 | tf_op jit(solution)/shard_map/ppermute | solution.py:17
  45.4 62.2 %collective-permute-start.16 = (bf16[2,2,512,512]{3,2,1,0:T(8,128)(2,1)}, bf16[2,2,512,512]{3,2,1,0:T(8,128)(2,1)S(1)}, u32[]{:S(2)}, u32[]{:S(2)}) collective-permute-start(bf16[2,2,512,512]{3,2,1,0:T(8,128)(2,1)} %get-tuple-element.69), channel_id=1, source_target_pairs={{0,8},{8,0},{1,9},{9,1},{2,10},{10,2},{3,11},{11,3},{4,12},{12,4},... | collective-permute-start | bytes 6291464 | tf_op jit(solution)/shard_map/ppermute | solution.py:17
  54.5 11.7 %copy-start.5 = (f32[2,256,512]{2,1,0:T(8,128)S(1)}, f32[2,256,512]{2,1,0:T(8,128)}, u32[]{:S(2)}) copy-start(f32[2,256,512]{2,1,0:T(8,128)} %get-tuple-element.55) | copy-start | bytes 3145732
  64.2 24.8 %collective-permute-start.13 = (bf16[2,2,256,512]{3,2,1,0:T(8,128)(2,1)S(1)}, bf16[2,2,256,512]{3,2,1,0:T(8,128)(2,1)S(1)}, u32[]{:S(2)}, u32[]{:S(2)}) collective-permute-start(bf16[2,2,256,512]{3,2,1,0:T(8,128)(2,1)S(1)} %sums.10), channel_id=1, source_target_pairs={{0,1},{1,0},{2,3},{3,2},{4,5},{5,4},{6,7},{7,6},{8,9},{9,8},{10,11... | collective-permute-start | bytes 3145736 | tf_op jit(solution)/shard_map/ppermute | solution.py:17
  67.4 23.0 %collective-permute-start.12 = (bf16[2,2,256,512]{3,2,1,0:T(8,128)(2,1)}, bf16[2,2,256,512]{3,2,1,0:T(8,128)(2,1)}, u32[]{:S(2)}, u32[]{:S(2)}) collective-permute-start(bf16[2,2,256,512]{3,2,1,0:T(8,128)(2,1)} %pad_maximum_fusion), channel_id=1, source_target_pairs={{2,4},{3,5},{4,2},{5,3},{10,12},{11,13},{12,10},{13,11},{18,20},{1... | collective-permute-start | bytes 3145736 | tf_op jit(solution)/shard_map/ppermute | solution.py:275
  69.1 26.8 %collective-permute-start.14 = (bf16[2,2,256,512]{3,2,1,0:T(8,128)(2,1)}, bf16[2,2,256,512]{3,2,1,0:T(8,128)(2,1)S(1)}, u32[]{:S(2)}, u32[]{:S(2)}) collective-permute-start(bf16[2,2,256,512]{3,2,1,0:T(8,128)(2,1)} %pad_maximum_fusion), channel_id=1, source_target_pairs={{0,2},{1,3},{6,4},{7,5},{8,10},{9,11},{14,12},{15,13},{16,18},{17,... | collective-permute-start | bytes 3145736 | tf_op jit(solution)/shard_map/ppermute | solution.py:274
  79.2 17.7 %copy-start.3 = (f32[2,256,512]{2,1,0:T(8,128)S(1)}, f32[2,256,512]{2,1,0:T(8,128)}, u32[]{:S(2)}) copy-start(f32[2,256,512]{2,1,0:T(8,128)} %get-tuple-element.64) | copy-start | bytes 3145732
  89.0 24.1 %collective-permute-start.17 = (bf16[2,2,256,512]{3,2,1,0:T(8,128)(2,1)S(1)}, bf16[2,2,256,512]{3,2,1,0:T(8,128)(2,1)S(1)}, u32[]{:S(2)}, u32[]{:S(2)}) collective-permute-start(bf16[2,2,256,512]{3,2,1,0:T(8,128)(2,1)S(1)} %sums.12), channel_id=1, source_target_pairs={{0,1},{1,0},{2,3},{3,2},{4,5},{5,4},{6,7},{7,6},{8,9},{9,8},{10,11... | collective-permute-start | bytes 3145736 | tf_op jit(solution)/shard_map/ppermute | solution.py:17
  97.9 34.3 %collective-permute-start.19 = (bf16[2,256,512]{2,1,0:T(8,128)(2,1)}, bf16[2,256,512]{2,1,0:T(8,128)(2,1)S(1)}, u32[]{:S(2)}, u32[]{:S(2)}) collective-permute-start(bf16[2,256,512]{2,1,0:T(8,128)(2,1)} %fusion.6), channel_id=1, source_target_pairs={{0,2},{1,3},{2,0},{3,1},{4,6},{5,7},{6,4},{7,5},{8,10},{9,11},{10,... | collective-permute-start | bytes 1572872 | tf_op jit(solution)/shard_map/ppermute | solution.py:17
  100.3 31.9 %collective-permute-start.20 = (bf16[2,256,512]{2,1,0:T(8,128)(2,1)}, bf16[2,256,512]{2,1,0:T(8,128)(2,1)}, u32[]{:S(2)}, u32[]{:S(2)}) collective-permute-start(bf16[2,256,512]{2,1,0:T(8,128)(2,1)} %fusion.7), channel_id=1, source_target_pairs={{0,4},{1,5},{2,6},{3,7},{4,0},{5,1},{6,2},{7,3},{8,12},{9,13},{10,... | collective-permute-start | bytes 1572872 | tf_op jit(solution)/shard_map/ppermute | solution.py:17
  101.3 1.4 copy-start.2
  107.6 8.1 %copy-start.4 = (f32[2,256,512]{2,1,0:T(8,128)S(1)}, f32[2,256,512]{2,1,0:T(8,128)}, u32[]{:S(2)}) copy-start(f32[2,256,512]{2,1,0:T(8,128)} %get-tuple-element.72) | copy-start | bytes 3145732
  107.6 1.4 copy-start.1
  113.0 33.8 %collective-permute-start.18 = (bf16[2,2,256,512]{3,2,1,0:T(8,128)(2,1)S(1)}, bf16[2,2,256,512]{3,2,1,0:T(8,128)(2,1)S(1)}, u32[]{:S(2)}, u32[]{:S(2)}) collective-permute-start(bf16[2,2,256,512]{3,2,1,0:T(8,128)(2,1)S(1)} %sums.14), channel_id=1, source_target_pairs={{0,1},{1,0},{2,3},{3,2},{4,5},{5,4},{6,7},{7,6},{8,9},{9,8},{10,11... | collective-permute-start | bytes 3145736 | tf_op jit(solution)/shard_map/ppermute | solution.py:17
  116.7 27.6 %collective-permute-start.22 = (bf16[2,256,512]{2,1,0:T(8,128)(2,1)}, bf16[2,256,512]{2,1,0:T(8,128)(2,1)}, u32[]{:S(2)}, u32[]{:S(2)}) collective-permute-start(bf16[2,256,512]{2,1,0:T(8,128)(2,1)} %fusion.4), channel_id=1, source_target_pairs={{0,2},{1,3},{2,0},{3,1},{4,6},{5,7},{6,4},{7,5},{8,10},{9,11},{10,... | collective-permute-start | bytes 1572872 | tf_op jit(solution)/shard_map/ppermute | solution.py:17
  118.7 28.2 %collective-permute-start.23 = (bf16[2,256,512]{2,1,0:T(8,128)(2,1)}, bf16[2,256,512]{2,1,0:T(8,128)(2,1)}, u32[]{:S(2)}, u32[]{:S(2)}) collective-permute-start(bf16[2,256,512]{2,1,0:T(8,128)(2,1)} %fusion.5), channel_id=1, source_target_pairs={{0,4},{1,5},{2,6},{3,7},{4,0},{5,1},{6,2},{7,3},{8,12},{9,13},{10,... | collective-permute-start | bytes 1572872 | tf_op jit(solution)/shard_map/ppermute | solution.py:17
  149.7 1.4 collective-permute-start.21
  150.0 1.5 %collective-permute-start.24 = (bf16[128,512]{1,0:T(8,128)(2,1)S(1)}, bf16[128,512]{1,0:T(8,128)(2,1)S(1)}, u32[]{:S(2)}, u32[]{:S(2)}) collective-permute-start(bf16[128,512]{1,0:T(8,128)(2,1)S(1)} %constant_dynamic-slice_fusion), channel_id=1, source_target_pairs={{0,8},{8,0},{1,9},{9,1},{2,10},{10,2},{3,11},{11,3},{4,12},{12,4},... | collective-permute-start | bytes 393224 | tf_op jit(solution)/shard_map/ppermute | solution.py:17

commit v4 on v3

--- a/solution.py
+++ b/solution.py
@@ -21,8 +21,7 @@
     return lax.optimization_barrier((value, *earlier))[0]
 
 
-def cut_kernel(groups, lanes, at_ref, gate_ref, up_ref, *refs):
-    out_refs, (held, in_sems, out_sems) = refs[:-3], refs[-3:]
+def cut_copies(groups, lanes, at_ref, gate_ref, up_ref, out_refs, held, in_sems, out_sems):
     weights = (gate_ref, up_ref)
     every = []
     for places, out_ref in zip(groups, out_refs):
@@ -36,43 +35,55 @@
                         pltpu.make_async_copy(held.at[k], out_ref.at[n, i], out_sems.at[k]),
                     )
                 )
-    ahead = 6
-    for copy_in, _ in every[:ahead]:
+    return every
+
+
+def cut_scratch(groups, depth, lanes):
+    count = 2 * sum(map(len, groups))
+    return [
+        pltpu.VMEM((count, depth, lanes), jnp.bfloat16),
+        pltpu.SemaphoreType.DMA((count,)),
+        pltpu.SemaphoreType.DMA((count,)),
+    ]
+
+
+def cut_kernel(groups, lanes, at_ref, gate_ref, up_ref, *refs):
+    every = cut_copies(groups, lanes, at_ref, gate_ref, up_ref, refs[:-3], *refs[-3:])
+    for copy_in, _ in every:
         copy_in.start()
-    for k, (copy_in, copy_out) in enumerate(every):
+    for copy_in, copy_out in every:
         copy_in.wait()
         copy_out.start()
-        if k + ahead < len(every):
-            every[k + ahead][0].start()
     for _, copy_out in every:
         copy_out.wait()
 
 
 def cut(at, gate_weight, up_weight, groups, lanes):
     depth = gate_weight.shape[0]
-    count = 2 * sum(map(len, groups))
     hbm = pl.BlockSpec(memory_space=pltpu.HBM)
     return pl.pallas_call(
         functools.partial(cut_kernel, groups, lanes),
         in_specs=[pl.BlockSpec(memory_space=pltpu.SMEM), hbm, hbm],
         out_specs=[hbm] * len(groups),
         out_shape=[jax.ShapeDtypeStruct((len(places), 2, depth, lanes), jnp.bfloat16) for places in groups],
-        scratch_shapes=[
-            pltpu.VMEM((count, depth, lanes), jnp.bfloat16),
-            pltpu.SemaphoreType.DMA((count,)),
-            pltpu.SemaphoreType.DMA((count,)),
-        ],
+        scratch_shapes=cut_scratch(groups, depth, lanes),
         compiler_params=pltpu.CompilerParams(vmem_limit_bytes=VMEM_LIMIT),
         name="cut",
     )(at, gate_weight, up_weight)
 
 
-def sums_kernel(places, lanes, side, stacked, at_ref, x_ref, gate_ref, up_ref, theirs_ref, masks_ref, *refs):
-    out_refs, (kept, result, in_sems, out_sems) = refs[:-4], refs[-4:]
+def sums_kernel(
+    places, lanes, side, stacked, groups, messages, at_ref, partner_ref, x_ref, gate_ref, up_ref, masks_ref, *refs
+):
+    theirs_refs, refs = refs[:messages], refs[messages:]
+    outs = 1 if stacked else len(places)
+    out_refs, refs = refs[:outs], refs[outs:]
+    cut_refs, refs = refs[: len(groups)], refs[len(groups) :]
+    kept, result, in_sems, out_sems = refs[:4]
     depth = gate_ref.shape[0]
     weights = (gate_ref, up_ref)
     firsts = [
-        pl.multiple_of((at_ref[0] ^ offset) * at_ref[2] + at_ref[1] + start, LANES) for offset, start, _ in places
+        pl.multiple_of((at_ref[0] ^ offset) * at_ref[2] + at_ref[1] + start, LANES) for offset, start, *_ in places
     ]
 
     def copies_in(n, i):
@@ -81,7 +92,7 @@
                 weights[i].at[:, pl.ds(firsts[n], lanes)], kept.at[n, i, pl.ds(0, depth)], in_sems.at[n, i, 0]
             ),
             pltpu.make_async_copy(
-                theirs_ref.at[places[n][2], i], kept.at[n, i, pl.ds(depth, depth)], in_sems.at[n, i, 1]
+                theirs_refs[places[n][2]].at[places[n][3], i], kept.at[n, i, pl.ds(depth, depth)], in_sems.at[n, i, 1]
             ),
         )
 
@@ -94,6 +105,9 @@
     for one in every[:ahead]:
         for copy in copies_in(*one):
             copy.start()
+    cuts = cut_copies(groups, lanes, partner_ref, gate_ref, up_ref, cut_refs, *refs[4:]) if groups else []
+    for copy_in, _ in cuts:
+        copy_in.start()
     across = masks_ref.shape[1]
     blocks = 2 * depth // side
     for k, (n, i) in enumerate(every):
@@ -113,34 +127,41 @@
         total = jnp.dot(x_ref[...], kept[n, i], preferred_element_type=jnp.float32)
         result[n, i] = total.astype(result.dtype)
         copy_out(n, i).start()
+    for copy_in, copy_out_cut in cuts:
+        copy_in.wait()
+        copy_out_cut.start()
     for one in every:
         copy_out(*one).wait()
-
-
-def sums(at, x, gate_weight, up_weight, theirs, masks, side, places, lanes, dtype, stacked):
+    for _, copy_out_cut in cuts:
+        copy_out_cut.wait()
+
+
+def sums(at, x, gate_weight, up_weight, theirs, masks, side, places, lanes, dtype, stacked, partner, groups):
     depth = gate_weight.shape[0]
     tokens = x.shape[0]
     count = len(places)
     vmem = pl.BlockSpec(memory_space=pltpu.VMEM)
     hbm = pl.BlockSpec(memory_space=pltpu.HBM)
     return pl.pallas_call(
-        functools.partial(sums_kernel, places, lanes, side, stacked),
-        in_specs=[pl.BlockSpec(memory_space=pltpu.SMEM), vmem, hbm, hbm, hbm, vmem],
-        out_specs=[hbm] * (1 if stacked else count),
+        functools.partial(sums_kernel, places, lanes, side, stacked, groups, len(theirs)),
+        in_specs=[pl.BlockSpec(memory_space=pltpu.SMEM)] * 2 + [vmem, hbm, hbm, vmem] + [hbm] * len(theirs),
+        out_specs=[hbm] * ((1 if stacked else count) + len(groups)),
         out_shape=(
             [jax.ShapeDtypeStruct((count, 2, tokens, lanes), dtype)]
             if stacked
             else [jax.ShapeDtypeStruct((2, tokens, lanes), dtype)] * count
-        ),
+        )
+        + [jax.ShapeDtypeStruct((len(units), 2, depth, lanes), jnp.bfloat16) for units in groups],
         scratch_shapes=[
             pltpu.VMEM((count, 2, 2 * depth, lanes), jnp.bfloat16),
             pltpu.VMEM((count, 2, tokens, lanes), dtype),
             pltpu.SemaphoreType.DMA((count, 2, 2)),
             pltpu.SemaphoreType.DMA((count, 2)),
-        ],
+        ]
+        + (cut_scratch(groups, depth, lanes) if groups else []),
         compiler_params=pltpu.CompilerParams(vmem_limit_bytes=VMEM_LIMIT),
         name="sums",
-    )(at, x, gate_weight, up_weight, theirs, masks)
+    )(at, partner, x, gate_weight, up_weight, masks, *theirs)
 
 
 def local(tokens, gain, gate_weight, up_weight, gate_mask, up_mask):
@@ -174,15 +195,19 @@
         latest[:] = [value]
         return value
 
-    def fetch(*groups):
-        values = cut(
-            in_turn(partners), gate_weight, up_weight, tuple(tuple(map(place, units)) for units in groups), lanes
-        )
-        emit(values[0])
+    def in_place(groups):
+        return tuple(tuple(map(place, units)) for units in groups)
+
+    def swap(groups, values):
         for units, value in zip(groups, values):
             value = exchange(value, "wide", 1)
             for n, unit in enumerate(units):
                 theirs[unit] = (value, n)
+
+    def fetch(*groups):
+        values = cut(in_turn(partners), gate_weight, up_weight, in_place(groups), lanes)
+        emit(values[0])
+        swap(groups, values)
 
     raw = []
     for flip in range(2):
@@ -194,13 +219,21 @@
         raw.append(lax.ppermute(piece, ("wide", "tensor"), moves))
     values = tokens.astype(jnp.float32)
     squares = jnp.sum(values * values, axis=-1).reshape(1, rows)
-    emit(squares)
-    if pairs == 4:
-        fetch([(3, 1, 0), (3, 1, 1)])
     total = squares
     for p in range(1, pairs):
         total = total + exchange(squares, "tensor", 2 * p)
     raw = jnp.where(shard % 2 == 1, jnp.concatenate(raw[::-1]), jnp.concatenate(raw))
+    masks = jnp.concatenate(
+        [
+            lax.dynamic_slice_in_dim(mask, r // side, depth // side, 0)
+            for mask in (gate_mask, up_mask)
+            for r in first_rows
+        ]
+    ).astype(jnp.bfloat16)
+    gains = jnp.stack([lax.dynamic_slice_in_dim(gain, r, depth, 0) for r in first_rows])
+    latest[:] = [total, raw, masks, gains]
+    if pairs == 4:
+        fetch([(3, 1, 0), (3, 1, 1)])
     raw_other = exchange(after(raw, total), "wide", 1)
     total = total + exchange(after(total, raw), "tensor", 1)
     scale = lax.rsqrt(total / features + EPS)
@@ -210,35 +243,28 @@
         jnp.concatenate([scale, scale_other], axis=1),
         jnp.concatenate([scale_other, scale], axis=1),
     ).reshape(2 * rows, 1)
-    gains = [lax.dynamic_slice_in_dim(gain, r, depth, 0)[None, :] for r in first_rows]
     normed = jnp.concatenate(
-        [(v.astype(jnp.float32) * scales * g).astype(jnp.bfloat16) for v, g in zip((raw, raw_other), gains)], axis=1
+        [(v.astype(jnp.float32) * scales * gains[i : i + 1]).astype(jnp.bfloat16) for i, v in enumerate((raw, raw_other))], axis=1
     )
 
     emit(normed)
-    if pairs == 4:
-        latest.append(theirs[3, 1, 0][0])
-        fetch(
-            [(3, 0, 0), (3, 0, 1), (2, 1, 0), (1, 1, 0)],
-            [(2, 1, 1), (1, 1, 1), (2, 0, 0), (1, 0, 0), (0, 0, 0), (0, 0, 1)],
-        )
-
-    masks = jnp.concatenate(
-        [
-            lax.dynamic_slice_in_dim(mask, r // side, depth // side, 0)
-            for mask in (gate_mask, up_mask)
-            for r in first_rows
-        ]
-    ).astype(jnp.bfloat16)
-
-    def chip_sums(units, *more, stacked=True):
-        value = theirs[units[0]][0]
-        places = tuple((*place(unit), theirs[unit][1]) for unit in units)
+
+    def chip_sums(units, stacked=True, groups=()):
+        messages = []
+        for unit in units:
+            if not any(theirs[unit][0] is message for message in messages):
+                messages.append(theirs[unit][0])
+        places = tuple(
+            (*place(unit), [theirs[unit][0] is m for m in messages].index(True), theirs[unit][1]) for unit in units
+        )
         dtype = jnp.bfloat16 if stacked else jnp.float32
         values = sums(
-            mine, in_turn(normed, *more), gate_weight, up_weight, value, masks, side, places, lanes, dtype, stacked
+            mine, in_turn(normed), gate_weight, up_weight, messages, masks, side, places, lanes, dtype, stacked,
+            partners, in_place(groups)
         )
         emit(values[0])
+        outs = 1 if stacked else len(units)
+        swap(groups, values[outs:])
         return values[0] if stacked else values
 
     def finish(own, *terms):
@@ -265,8 +291,15 @@
         by_neighbour = tensor_pairs(((0, 1), (3, 2)))
         middle = tensor_pairs(((1, 2), (2, 1)))
 
-        pair3 = exchange(chip_sums([(3, 1, 0), (3, 1, 1)]), "tensor", 1)
-        fetch([(2, 0, 1), (1, 0, 1)], [(0, 1, 0), (0, 1, 1)])
+        far_3 = chip_sums(
+            [(3, 1, 0), (3, 1, 1)],
+            groups=[
+                [(3, 0, 0), (3, 0, 1), (2, 1, 0), (1, 1, 0)],
+                [(2, 1, 1), (1, 1, 1), (2, 0, 0), (1, 0, 0)],
+            ],
+        )
+        pair3 = exchange(far_3, "tensor", 1)
+        fetch([(2, 0, 1), (1, 0, 1), (0, 0, 0)], [(0, 1, 0), (0, 1, 1), (0, 0, 1)])
         near3 = chip_sums([(3, 0, 0), (3, 0, 1)], stacked=False)
         far_a = chip_sums([(2, 1, 0), (1, 1, 0)])
         pair_a = exchange(in_turn(far_a, pair3), "tensor", 1)
@@ -276,17 +309,17 @@
         near_a = chip_sums([(2, 0, 0), (1, 0, 0)], stacked=False)
         far_b = chip_sums([(2, 1, 1), (1, 1, 1)])
         pair_b = exchange(in_turn(far_b, pair_a), "tensor", 1)
-        second_a = exchange(add(after(near_a[0], across), pair_a[0], relay[0]), "tensor", 4)
-        first_a = exchange(add(near_a[1], pair_a[1]), "tensor", 2)
+        second_a = exchange(add(near_a[0], pair_a[0], relay[0]), "tensor", 4)
+        first_a = exchange(add(after(near_a[1], across), pair_a[1]), "tensor", 2)
         near_b = chip_sums([(2, 0, 1), (1, 0, 1)], stacked=False)
         far_0 = chip_sums([(0, 1, 0), (0, 1, 1)])
         pair_0 = exchange(in_turn(far_0, pair_b), "tensor", 1)
         second_b = exchange(add(near_b[0], pair_b[0], relay[1]), "tensor", 4)
         first_b = exchange(add(near_b[1], pair_b[1]), "tensor", 2)
         own = chip_sums([(0, 0, 0), (0, 0, 1)], stacked=False)
-        one, other = give(finish(own[0], pair_0[0], first_a, second_a, across[0]))
-        two, another = give(finish(own[1], pair_0[1], first_b, second_b, across[1]))
-        return jnp.concatenate([one, two, other, another], axis=1)
+        early = emit(in_turn(own[0]) + wide(first_a) + wide(second_a) + wide(across[0]))
+        hidden = [finish(early, pair_0[0]), finish(own[1], pair_0[1], first_b, second_b, across[1])]
+        return jnp.concatenate(give(jnp.concatenate(hidden, axis=1)), axis=1)
     received = []
     for p in range(pairs - 1, -1, -1):
         fetch([(p, 1, 0), (p, 0, 0)])

time: 153 us -> 147 us (0.961)
  Pallas kernels: 51.9 us -> 49.7 us
  local copies, waits for them, and re-layouts: 3.67 us -> 1.78 us
    pallas_call x3 -> x2, Pallas kernels: 16.5 us -> 9.09 us  [cut(): pl.pallas_call(functools.partial(cut_kernel, groups, lanes), in_specs=[pl...]
    pallas_call x8, Pallas kernels: 35.3 us -> 40.6 us  [sums(): pl.pallas_call(functools.partial(sums_kernel, places, lanes, side, stacke...]
    unnamed x14 -> x10, local copies, waits for them, and re-layouts: 2.83 us -> 0.02 us
    add x0 -> x1, other arithmetic: none -> 1.56 us  [local(): in_turn(own[0]) + wide(first_a) + wide(second_a) + wide(across[0])]
    ppermute x21 -> x20, starting transfers between devices: 27 us -> 26.2 us  [exchange(): return lax.ppermute(value, axis, [(i, i ^ bit) for i in range(size)])]
    ppermute x21 -> x20, waiting for transfers between devices: 41 us -> 41.4 us  [exchange(): return lax.ppermute(value, axis, [(i, i ^ bit) for i in range(size)])]
  transfers between devices with their start and end apart: 25 -> 24, of which waited for: 13 -> 11; matrix products, arithmetic and copies ran while one was open for 5% -> 6% of each run, Pallas kernels for 26% -> 25%
where the time goes in v4:
time: 147 us; the launch traced here: 146 us
  Pallas kernels  49.7 us (34%)
  waiting for transfers between devices  48 us (33%)
  starting transfers between devices  35.5 us (24%)
  other arithmetic  10.9 us (7%)
  local copies, waits for them, and re-layouts  1.78 us (1%)
    ppermute x20, waiting for transfers between devices, exchange(): return lax.ppermute(value, axis, [(i, i ^ bit) for i in range(size)])  41.4 us
    pallas_call x8, Pallas kernels, sums(): pl.pallas_call(functools.partial(sums_kernel, places, lanes, side, stacke...  40.6 us
    ppermute x20, starting transfers between devices, exchange(): return lax.ppermute(value, axis, [(i, i ^ bit) for i in range(size)])  26.2 us
    pallas_call x2, Pallas kernels, cut(): pl.pallas_call(functools.partial(cut_kernel, groups, lanes), in_specs=[pl...  9.09 us
    ppermute x1, starting transfers between devices, local(): relay = lax.ppermute(third, 'tensor', by_neighbour)  6.36 us
    ppermute x1, waiting for transfers between devices, local(): relay = lax.ppermute(third, 'tensor', by_neighbour)  4.27 us
    convert_element_type x6, other arithmetic, add(): return emit(total.astype(jnp.bfloat16))  3.47 us
  transfers between devices with their start and end apart: 24, of which 11 were waited for; matrix products, arithmetic and copies ran while one was open for 6% of the time, Pallas kernels for 25%

profile of v4, /device:TPU:0, one launch (start us, length us, event | category | flops | bytes accessed | tf_op | source)
XLA Modules:
  0.0 146.3 jit_solution(13728312424247394448)
XLA Ops:
  0.0 1.1 multiply_reduce_fusion
  1.1 4.1 %collective-permute-start.3 = (f32[1,128]{1,0:T(1,128)S(1)}, f32[1,128]{1,0:T(1,128)S(1)}, u32[]{:S(2)}, u32[]{:S(2)}) collective-permute-start(f32[1,128]{1,0:T(1,128)S(1)} %bitcast.91), channel_id=1, source_target_pairs={{0,4},{1,5},{2,6},{3,7},{4,0},{5,1},{6,2},{7,3},{8,12},{9,13},{10,... | collective-permute-start | bytes 1544 | tf_op jit(solution)/shard_map/ppermute | solution.py:17
  5.2 1.3 collective-permute-start.4
  6.5 0.2 collective-permute-start.2
  6.8 1.0 constant_dynamic-slice_fusion.1
  7.7 1.6 %collective-permute-start = (bf16[128,512]{1,0:T(8,128)(2,1)S(1)}, bf16[128,512]{1,0:T(8,128)(2,1)S(1)}, u32[]{:S(2)}, u32[]{:S(2)}) collective-permute-start(bf16[128,512]{1,0:T(8,128)(2,1)S(1)} %get-tuple-element.83), channel_id=1, source_target_pairs={{8,0},{0,1},{9,2},{1,3},{10,4},{2,5},{11,6},{3,7},{12,8},{4,9},{13... | collective-permute-start | bytes 393224 | tf_op jit(solution)/shard_map/ppermute | solution.py:219
  9.3 0.7 collective-permute-start.1
  10.0 0.1 pad_add_fusion.at_ref.partner_ref
  10.1 0.8 dynamic-slice_convert_fusion.1
  11.0 2.3 %collective-permute-done = bf16[128,512]{1,0:T(8,128)(2,1)S(1)} collective-permute-done((bf16[128,512]{1,0:T(8,128)(2,1)S(1)}, bf16[128,512]{1,0:T(8,128)(2,1)S(1)}, u32[]{:S(2)}, u32[]{:S(2)}) %collective-permute-start) | collective-permute-done | bytes 131104 | tf_op jit(solution)/shard_map/ppermute | solution.py:219
  13.3 0.1 maximum_select_fusion
  13.3 3.0 %cut.2 = bf16[2,2,512,512]{3,2,1,0:T(8,128)(2,1)} custom-call(s32[3]{0:T(128)S(1)} %pad_add_fusion.at_ref.partner_ref, bf16[512,16384]{1,0:T(8,128)(2,1)} %gate_ref.19, bf16[512,16384]{1,0:T(8,128)(2,1)} %up_ref.19), custom_call_target="tpu_custom_call" | custom-call | tf_op jit(solution)/shard_map/cut/pallas_call | solution.py:64
  16.3 2.3 %collective-permute-start.8 = (bf16[2,2,512,512]{3,2,1,0:T(8,128)(2,1)}, bf16[2,2,512,512]{3,2,1,0:T(8,128)(2,1)}, u32[]{:S(2)}, u32[]{:S(2)}) collective-permute-start(bf16[2,2,512,512]{3,2,1,0:T(8,128)(2,1)} %cut.2), channel_id=1, source_target_pairs={{0,8},{8,0},{1,9},{9,1},{2,10},{10,2},{3,11},{11,3},{4,12},{12,4},... | collective-permute-start | bytes 6291464 | tf_op jit(solution)/shard_map/ppermute | solution.py:17
  18.7 3.2 %collective-permute-start.5 = (f32[1,128]{1,0:T(1,128)S(1)}, f32[1,128]{1,0:T(1,128)S(1)}, u32[]{:S(2)}, u32[]{:S(2)}) collective-permute-start(f32[1,128]{1,0:T(1,128)S(1)} %add_add_fusion), channel_id=1, source_target_pairs={{0,1},{1,0},{2,3},{3,2},{4,5},{5,4},{6,7},{7,6},{8,9},{9,8},{10,11... | collective-permute-start | bytes 1544 | tf_op jit(solution)/shard_map/ppermute | solution.py:17
  21.8 0.8 fusion.14
  22.6 0.7 collective-permute-done.5
  23.4 0.1 pad_add_fusion.1.at_ref
  23.4 1.0 collective-permute-done.6
  24.5 0.2 multiply_convert_fusion.1
  24.8 9.4 %sums.8 = (bf16[2,2,256,512]{3,2,1,0:T(8,128)(2,1)S(1)}, bf16[4,2,512,512]{3,2,1,0:T(8,128)(2,1)}, bf16[4,2,512,512]{3,2,1,0:T(8,128)(2,1)}) custom-call(s32[3]{0:T(128)S(1)} %pad_add_fusion.1.at_ref, s32[3]{0:T(128)S(1)} %pad_add_fusion.at_ref.partner_ref, bf16[256,1024]{1,0:T(8,128)(2,1)S(1)} %pad_maximum_fusion.1.x_ref, bf16[512,16384]{1,0:T(8,128)(2,1)} %gate_ref.19, ...), custom_call_target="tpu_custom_call" | custom-call | tf_op jit(solution)/shard_map/sums/pallas_call | solution.py:145
  34.2 0.3 collective-permute-start.9
  34.5 0.3 collective-permute-start.11
  34.8 2.0 %collective-permute-start.10 = (bf16[2,2,256,512]{3,2,1,0:T(8,128)(2,1)S(1)}, bf16[2,2,256,512]{3,2,1,0:T(8,128)(2,1)S(1)}, u32[]{:S(2)}, u32[]{:S(2)}) collective-permute-start(bf16[2,2,256,512]{3,2,1,0:T(8,128)(2,1)S(1)} %get-tuple-element.46), channel_id=1, source_target_pairs={{0,1},{1,0},{2,3},{3,2},{4,5},{5,4},{6,7},{7,6},{8,9},{9,8},{10,11... | collective-permute-start | bytes 3145736 | tf_op jit(solution)/shard_map/ppermute | solution.py:17
  36.8 6.1 %cut.3 = (bf16[3,2,512,512]{3,2,1,0:T(8,128)(2,1)}, bf16[3,2,512,512]{3,2,1,0:T(8,128)(2,1)}) custom-call(s32[3]{0:T(128)S(1)} %pad_add_fusion.at_ref.partner_ref, bf16[512,16384]{1,0:T(8,128)(2,1)} %gate_ref.19, bf16[512,16384]{1,0:T(8,128)(2,1)} %up_ref.19), custom_call_target="tpu_custom_call" | custom-call | tf_op jit(solution)/shard_map/cut/pallas_call | solution.py:64
  42.9 0.1 collective-permute-start.15
  42.9 0.5 collective-permute-start.16
  43.4 2.3 %collective-permute-done.9.refs_0_ = bf16[4,2,512,512]{3,2,1,0:T(8,128)(2,1)} collective-permute-done((bf16[4,2,512,512]{3,2,1,0:T(8,128)(2,1)}, bf16[4,2,512,512]{3,2,1,0:T(8,128)(2,1)}, u32[]{:S(2)}, u32[]{:S(2)}) %collective-permute-start.9) | collective-permute-done | bytes 4194336 | tf_op jit(solution)/shard_map/ppermute | solution.py:17
  45.7 4.8 %sums.9 = (f32[2,256,512]{2,1,0:T(8,128)S(1)}, f32[2,256,512]{2,1,0:T(8,128)}) custom-call(s32[3]{0:T(128)S(1)} %pad_add_fusion.1.at_ref, s32[3]{0:T(128)S(1)} %pad_add_fusion.at_ref.partner_ref, bf16[256,1024]{1,0:T(8,128)(2,1)S(1)} %pad_maximum_fusion.1.x_ref, bf16[512,16384]{1,0:T(8,128)(2,1)} %gate_ref.19, bf16[512,16384]{1,0:T(8,128)(2,1)} %up_ref.19, ...), custom_call_target="tpu_custom_call" | custom-call | tf_op jit(solution)/shard_map/sums/pallas_call | solution.py:145
  50.5 4.0 %sums.10 = bf16[2,2,256,512]{3,2,1,0:T(8,128)(2,1)S(1)} custom-call(s32[3]{0:T(128)S(1)} %pad_add_fusion.1.at_ref, s32[3]{0:T(128)S(1)} %pad_add_fusion.at_ref.partner_ref, bf16[256,1024]{1,0:T(8,128)(2,1)S(1)} %pad_maximum_fusion.1.x_ref, bf16[512,16384]{1,0:T(8,128)(2,1)} %gate_ref.19, bf16[512,16384]{1,0:T(8,128)(2,1)} %up_ref.19, ...), custom_call_target="tpu_custom_call" | custom-call | tf_op jit(solution)/shard_map/sums/pallas_call | solution.py:145
  54.5 5.8 %collective-permute-done.10 = bf16[2,2,256,512]{3,2,1,0:T(8,128)(2,1)S(1)} collective-permute-done((bf16[2,2,256,512]{3,2,1,0:T(8,128)(2,1)S(1)}, bf16[2,2,256,512]{3,2,1,0:T(8,128)(2,1)S(1)}, u32[]{:S(2)}, u32[]{:S(2)}) %collective-permute-start.10) | collective-permute-done | bytes 1048608 | tf_op jit(solution)/shard_map/ppermute | solution.py:17
  60.3 1.7 %collective-permute-start.13 = (bf16[2,2,256,512]{3,2,1,0:T(8,128)(2,1)S(1)}, bf16[2,2,256,512]{3,2,1,0:T(8,128)(2,1)S(1)}, u32[]{:S(2)}, u32[]{:S(2)}) collective-permute-start(bf16[2,2,256,512]{3,2,1,0:T(8,128)(2,1)S(1)} %sums.10), channel_id=1, source_target_pairs={{0,1},{1,0},{2,3},{3,2},{4,5},{5,4},{6,7},{7,6},{8,9},{9,8},{10,11... | collective-permute-start | bytes 3145736 | tf_op jit(solution)/shard_map/ppermute | solution.py:17
  62.1 0.2 fusion.7
  62.2 0.2 fusion.6
  62.4 0.1 pad_maximum_fusion
  62.5 0.7 collective-permute-start.12
  63.3 6.4 %collective-permute-start.14 = (bf16[2,2,256,512]{3,2,1,0:T(8,128)(2,1)S(1)}, bf16[2,2,256,512]{3,2,1,0:T(8,128)(2,1)S(1)}, u32[]{:S(2)}, u32[]{:S(2)}) collective-permute-start(bf16[2,2,256,512]{3,2,1,0:T(8,128)(2,1)S(1)} %pad_maximum_fusion), channel_id=1, source_target_pairs={{0,2},{1,3},{6,4},{7,5},{8,10},{9,11},{14,12},{15,13},{16,18},{17,... | collective-permute-start | bytes 3145736 | tf_op jit(solution)/shard_map/ppermute | solution.py:307
  69.7 4.8 %sums.11 = (f32[2,256,512]{2,1,0:T(8,128)S(1)}, f32[2,256,512]{2,1,0:T(8,128)}) custom-call(s32[3]{0:T(128)S(1)} %pad_add_fusion.1.at_ref, s32[3]{0:T(128)S(1)} %pad_add_fusion.at_ref.partner_ref, bf16[256,1024]{1,0:T(8,128)(2,1)S(1)} %pad_maximum_fusion.1.x_ref, bf16[512,16384]{1,0:T(8,128)(2,1)} %gate_ref.19, bf16[512,16384]{1,0:T(8,128)(2,1)} %up_ref.19, ...), custom_call_target="tpu_custom_call" | custom-call | tf_op jit(solution)/shard_map/sums/pallas_call | solution.py:145
  74.5 4.0 %sums.12 = bf16[2,2,256,512]{3,2,1,0:T(8,128)(2,1)S(1)} custom-call(s32[3]{0:T(128)S(1)} %pad_add_fusion.1.at_ref, s32[3]{0:T(128)S(1)} %pad_add_fusion.at_ref.partner_ref, bf16[256,1024]{1,0:T(8,128)(2,1)S(1)} %pad_maximum_fusion.1.x_ref, bf16[512,16384]{1,0:T(8,128)(2,1)} %gate_ref.19, bf16[512,16384]{1,0:T(8,128)(2,1)} %up_ref.19, ...), custom_call_target="tpu_custom_call" | custom-call | tf_op jit(solution)/shard_map/sums/pallas_call | solution.py:145
  78.5 6.6 %collective-permute-done.13 = bf16[2,2,256,512]{3,2,1,0:T(8,128)(2,1)S(1)} collective-permute-done((bf16[2,2,256,512]{3,2,1,0:T(8,128)(2,1)S(1)}, bf16[2,2,256,512]{3,2,1,0:T(8,128)(2,1)S(1)}, u32[]{:S(2)}, u32[]{:S(2)}) %collective-permute-start.13) | collective-permute-done | bytes 1048608 | tf_op jit(solution)/shard_map/ppermute | solution.py:17
  85.1 1.4 collective-permute-start.17
  86.5 4.3 %collective-permute-done.14 = bf16[2,2,256,512]{3,2,1,0:T(8,128)(2,1)S(1)} collective-permute-done((bf16[2,2,256,512]{3,2,1,0:T(8,128)(2,1)S(1)}, bf16[2,2,256,512]{3,2,1,0:T(8,128)(2,1)S(1)}, u32[]{:S(2)}, u32[]{:S(2)}) %collective-permute-start.14) | collective-permute-done | bytes 1048608 | tf_op jit(solution)/shard_map/ppermute | solution.py:307
  90.8 0.2 fusion.5
  91.0 1.0 fusion.4
  92.0 2.5 %collective-permute-start.18 = (bf16[2,256,512]{2,1,0:T(8,128)(2,1)}, bf16[2,256,512]{2,1,0:T(8,128)(2,1)}, u32[]{:S(2)}, u32[]{:S(2)}) collective-permute-start(bf16[2,256,512]{2,1,0:T(8,128)(2,1)} %fusion.4), channel_id=1, source_target_pairs={{0,2},{1,3},{2,0},{3,1},{4,6},{5,7},{6,4},{7,5},{8,10},{9,11},{10,... | collective-permute-start | bytes 1572872 | tf_op jit(solution)/shard_map/ppermute | solution.py:17
  94.4 1.1 collective-permute-start.19
  95.5 4.8 %sums.13 = (f32[2,256,512]{2,1,0:T(8,128)S(1)}, f32[2,256,512]{2,1,0:T(8,128)}) custom-call(s32[3]{0:T(128)S(1)} %pad_add_fusion.1.at_ref, s32[3]{0:T(128)S(1)} %pad_add_fusion.at_ref.partner_ref, bf16[256,1024]{1,0:T(8,128)(2,1)S(1)} %pad_maximum_fusion.1.x_ref, bf16[512,16384]{1,0:T(8,128)(2,1)} %gate_ref.19, bf16[512,16384]{1,0:T(8,128)(2,1)} %up_ref.19, ...), custom_call_target="tpu_custom_call" | custom-call | tf_op jit(solution)/shard_map/sums/pallas_call | solution.py:145
  100.4 4.0 %sums.14 = bf16[2,2,256,512]{3,2,1,0:T(8,128)(2,1)S(1)} custom-call(s32[3]{0:T(128)S(1)} %pad_add_fusion.1.at_ref, s32[3]{0:T(128)S(1)} %pad_add_fusion.at_ref.partner_ref, bf16[256,1024]{1,0:T(8,128)(2,1)S(1)} %pad_maximum_fusion.1.x_ref, bf16[512,16384]{1,0:T(8,128)(2,1)} %gate_ref.19, bf16[512,16384]{1,0:T(8,128)(2,1)} %up_ref.19, ...), custom_call_target="tpu_custom_call" | custom-call | tf_op jit(solution)/shard_map/sums/pallas_call | solution.py:145
  104.4 4.6 %collective-permute-done.17 = bf16[2,2,256,512]{3,2,1,0:T(8,128)(2,1)S(1)} collective-permute-done((bf16[2,2,256,512]{3,2,1,0:T(8,128)(2,1)S(1)}, bf16[2,2,256,512]{3,2,1,0:T(8,128)(2,1)S(1)}, u32[]{:S(2)}, u32[]{:S(2)}) %collective-permute-start.17) | collective-permute-done | bytes 1048608 | tf_op jit(solution)/shard_map/ppermute | solution.py:17
  109.0 1.1 collective-permute-start.20
  110.0 1.0 fusion.3
  111.0 1.0 fusion.2
  112.0 3.0 %collective-permute-start.21 = (bf16[2,256,512]{2,1,0:T(8,128)(2,1)}, bf16[2,256,512]{2,1,0:T(8,128)(2,1)}, u32[]{:S(2)}, u32[]{:S(2)}) collective-permute-start(bf16[2,256,512]{2,1,0:T(8,128)(2,1)} %fusion.2), channel_id=1, source_target_pairs={{0,2},{1,3},{2,0},{3,1},{4,6},{5,7},{6,4},{7,5},{8,10},{9,11},{10,... | collective-permute-start | bytes 1572872 | tf_op jit(solution)/shard_map/ppermute | solution.py:17
  115.0 1.0 collective-permute-start.22
  116.0 4.8 %sums.15 = (f32[2,256,512]{2,1,0:T(8,128)S(1)}, f32[2,256,512]{2,1,0:T(8,128)}) custom-call(s32[3]{0:T(128)S(1)} %pad_add_fusion.1.at_ref, s32[3]{0:T(128)S(1)} %pad_add_fusion.at_ref.partner_ref, bf16[256,1024]{1,0:T(8,128)(2,1)S(1)} %pad_maximum_fusion.1.x_ref, bf16[512,16384]{1,0:T(8,128)(2,1)} %gate_ref.19, bf16[512,16384]{1,0:T(8,128)(2,1)} %up_ref.19, ...), custom_call_target="tpu_custom_call" | custom-call | tf_op jit(solution)/shard_map/sums/pallas_call | solution.py:145
  120.9 1.6 %convert_add_fusion.3 = f32[2,256,512]{2,1,0:T(8,128)S(1)} fusion(bf16[2,256,512]{2,1,0:T(8,128)(2,1)} %collective-permute-done.19, f32[2,256,512]{2,1,0:T(8,128)S(1)} %get-tuple-element.74, bf16[2,256,512]{2,1,0:T(8,128)(2,1)} %collective-permute-done.18, bf16[2,2,256,512]{3,2,1,0:T(8,128)(2,1)S(1)} %collective-permute-done.12), kind=kLoop, calls=%fused_computation.6 | loop fusion | flops 1572864 | bytes 3670016 | tf_op jit(solution)/shard_map/add | solution.py:320
  122.4 15.8 %collective-permute-done.21 = bf16[2,256,512]{2,1,0:T(8,128)(2,1)} collective-permute-done((bf16[2,256,512]{2,1,0:T(8,128)(2,1)}, bf16[2,256,512]{2,1,0:T(8,128)(2,1)}, u32[]{:S(2)}, u32[]{:S(2)}) %collective-permute-start.21) | collective-permute-done | bytes 524320 | tf_op jit(solution)/shard_map/ppermute | solution.py:17
  138.3 3.0 %collective-permute-done.22 = bf16[2,256,512]{2,1,0:T(8,128)(2,1)} collective-permute-done((bf16[2,256,512]{2,1,0:T(8,128)(2,1)}, bf16[2,256,512]{2,1,0:T(8,128)(2,1)}, u32[]{:S(2)}, u32[]{:S(2)}) %collective-permute-start.22) | collective-permute-done | bytes 524320 | tf_op jit(solution)/shard_map/ppermute | solution.py:17
  141.3 2.1 %convert_add_fusion = (f32[2,256,512]{2,1,0:T(8,128)S(1)}, f32[2,256,512]{2,1,0:T(8,128)S(1)}) fusion(f32[2,256,512]{2,1,0:T(8,128)S(1)} %copy-done.4, bf16[2,256,512]{2,1,0:T(8,128)(2,1)} %collective-permute-done.22, bf16[2,256,512]{2,1,0:T(8,128)(2,1)} %collective-permute-done.21, bf16[2,2,256,512]{3,2,1,0:T(8,128)(2,1)S(1)} %collective-permute-done.12, ...), kind=kLoop, calls=%fused_computation.1 | loop fusion | flops 2621440 | bytes 6815744 | tf_op jit(solution)/shard_map/add | solution.py:273
  143.4 0.2 fusion.9
  143.6 0.2 fusion.11
  143.8 0.1 collective-permute-start.23
  143.8 1.5 %collective-permute-done.23 = bf16[128,1024]{1,0:T(8,128)(2,1)S(1)} collective-permute-done((bf16[128,1024]{1,0:T(8,128)(2,1)S(1)}, bf16[128,1024]{1,0:T(8,128)(2,1)S(1)}, u32[]{:S(2)}, u32[]{:S(2)}) %collective-permute-start.23) | collective-permute-done | bytes 262176 | tf_op jit(solution)/shard_map/ppermute | solution.py:17
  145.4 0.1 broadcast_select_fusion.1
  145.5 0.8 pad_maximum_fusion.2
  (31 shorter events, 0.2 us)
Async XLA Ops:
  1.1 9.9 %collective-permute-start.3 = (f32[1,128]{1,0:T(1,128)S(1)}, f32[1,128]{1,0:T(1,128)S(1)}, u32[]{:S(2)}, u32[]{:S(2)}) collective-permute-start(f32[1,128]{1,0:T(1,128)S(1)} %bitcast.91), channel_id=1, source_target_pairs={{0,4},{1,5},{2,6},{3,7},{4,0},{5,1},{6,2},{7,3},{8,12},{9,13},{10,... | collective-permute-start | bytes 1544 | tf_op jit(solution)/shard_map/ppermute | solution.py:17
  5.2 5.8 %collective-permute-start.4 = (f32[1,128]{1,0:T(1,128)S(1)}, f32[1,128]{1,0:T(1,128)S(1)}, u32[]{:S(2)}, u32[]{:S(2)}) collective-permute-start(f32[1,128]{1,0:T(1,128)S(1)} %bitcast.92), channel_id=1, source_target_pairs={{0,6},{1,7},{2,4},{3,5},{4,2},{5,3},{6,0},{7,1},{8,14},{9,15},{10,... | collective-permute-start | bytes 1544 | tf_op jit(solution)/shard_map/ppermute | solution.py:17
  6.5 4.4 %collective-permute-start.2 = (f32[1,128]{1,0:T(1,128)S(1)}, f32[1,128]{1,0:T(1,128)S(1)}, u32[]{:S(2)}, u32[]{:S(2)}) collective-permute-start(f32[1,128]{1,0:T(1,128)S(1)} %bitcast.93), channel_id=1, source_target_pairs={{0,2},{1,3},{2,0},{3,1},{4,6},{5,7},{6,4},{7,5},{8,10},{9,11},{10,... | collective-permute-start | bytes 1544 | tf_op jit(solution)/shard_map/ppermute | solution.py:17
  7.7 5.5 %collective-permute-start = (bf16[128,512]{1,0:T(8,128)(2,1)S(1)}, bf16[128,512]{1,0:T(8,128)(2,1)S(1)}, u32[]{:S(2)}, u32[]{:S(2)}) collective-permute-start(bf16[128,512]{1,0:T(8,128)(2,1)S(1)} %get-tuple-element.83), channel_id=1, source_target_pairs={{8,0},{0,1},{9,2},{1,3},{10,4},{2,5},{11,6},{3,7},{12,8},{4,9},{13... | collective-permute-start | bytes 393224 | tf_op jit(solution)/shard_map/ppermute | solution.py:219
  9.3 3.9 %collective-permute-start.1 = (bf16[128,512]{1,0:T(8,128)(2,1)S(1)}, bf16[128,512]{1,0:T(8,128)(2,1)S(1)}, u32[]{:S(2)}, u32[]{:S(2)}) collective-permute-start(bf16[128,512]{1,0:T(8,128)(2,1)S(1)} %get-tuple-element.84), channel_id=1, source_target_pairs={{0,0},{8,1},{1,2},{9,3},{2,4},{10,5},{3,6},{11,7},{4,8},{12,9},{5,... | collective-permute-start | bytes 393224 | tf_op jit(solution)/shard_map/ppermute | solution.py:219
  16.3 8.4 %collective-permute-start.8 = (bf16[2,2,512,512]{3,2,1,0:T(8,128)(2,1)}, bf16[2,2,512,512]{3,2,1,0:T(8,128)(2,1)}, u32[]{:S(2)}, u32[]{:S(2)}) collective-permute-start(bf16[2,2,512,512]{3,2,1,0:T(8,128)(2,1)} %cut.2), channel_id=1, source_target_pairs={{0,8},{8,0},{1,9},{9,1},{2,10},{10,2},{3,11},{11,3},{4,12},{12,4},... | collective-permute-start | bytes 6291464 | tf_op jit(solution)/shard_map/ppermute | solution.py:17
  18.7 4.7 %collective-permute-start.5 = (f32[1,128]{1,0:T(1,128)S(1)}, f32[1,128]{1,0:T(1,128)S(1)}, u32[]{:S(2)}, u32[]{:S(2)}) collective-permute-start(f32[1,128]{1,0:T(1,128)S(1)} %add_add_fusion), channel_id=1, source_target_pairs={{0,1},{1,0},{2,3},{3,2},{4,5},{5,4},{6,7},{7,6},{8,9},{9,8},{10,11... | collective-permute-start | bytes 1544 | tf_op jit(solution)/shard_map/ppermute | solution.py:17
  22.6 1.9 %collective-permute-start.7 = (bf16[256,512]{1,0:T(8,128)(2,1)S(1)}, bf16[256,512]{1,0:T(8,128)(2,1)S(1)}, u32[]{:S(2)}, u32[]{:S(2)}) collective-permute-start(bf16[256,512]{1,0:T(8,128)(2,1)S(1)} %maximum_select_fusion), channel_id=1, source_target_pairs={{0,8},{8,0},{1,9},{9,1},{2,10},{10,2},{3,11},{11,3},{4,12},{12,4},... | collective-permute-start | bytes 786440 | tf_op jit(solution)/shard_map/ppermute | solution.py:17
  23.4 1.1 collective-permute-start.6
  34.2 11.5 %collective-permute-start.9 = (bf16[4,2,512,512]{3,2,1,0:T(8,128)(2,1)}, bf16[4,2,512,512]{3,2,1,0:T(8,128)(2,1)}, u32[]{:S(2)}, u32[]{:S(2)}) collective-permute-start(bf16[4,2,512,512]{3,2,1,0:T(8,128)(2,1)} %get-tuple-element.50), channel_id=1, source_target_pairs={{0,8},{8,0},{1,9},{9,1},{2,10},{10,2},{3,11},{11,3},{4,12},{12,4},... | collective-permute-start | bytes 12582920 | tf_op jit(solution)/shard_map/ppermute | solution.py:17
  34.5 28.8 %collective-permute-start.11 = (bf16[4,2,512,512]{3,2,1,0:T(8,128)(2,1)}, bf16[4,2,512,512]{3,2,1,0:T(8,128)(2,1)S(1)}, u32[]{:S(2)}, u32[]{:S(2)}) collective-permute-start(bf16[4,2,512,512]{3,2,1,0:T(8,128)(2,1)} %get-tuple-element.57), channel_id=1, source_target_pairs={{0,8},{8,0},{1,9},{9,1},{2,10},{10,2},{3,11},{11,3},{4,12},{12,4},... | collective-permute-start | bytes 12582920 | tf_op jit(solution)/shard_map/ppermute | solution.py:17
  34.8 25.6 %collective-permute-start.10 = (bf16[2,2,256,512]{3,2,1,0:T(8,128)(2,1)S(1)}, bf16[2,2,256,512]{3,2,1,0:T(8,128)(2,1)S(1)}, u32[]{:S(2)}, u32[]{:S(2)}) collective-permute-start(bf16[2,2,256,512]{3,2,1,0:T(8,128)(2,1)S(1)} %get-tuple-element.46), channel_id=1, source_target_pairs={{0,1},{1,0},{2,3},{3,2},{4,5},{5,4},{6,7},{7,6},{8,9},{9,8},{10,11... | collective-permute-start | bytes 3145736 | tf_op jit(solution)/shard_map/ppermute | solution.py:17
  42.9 52.7 %collective-permute-start.15 = (bf16[3,2,512,512]{3,2,1,0:T(8,128)(2,1)}, bf16[3,2,512,512]{3,2,1,0:T(8,128)(2,1)}, u32[]{:S(2)}, u32[]{:S(2)}) collective-permute-start(bf16[3,2,512,512]{3,2,1,0:T(8,128)(2,1)} %get-tuple-element.48), channel_id=1, source_target_pairs={{0,8},{8,0},{1,9},{9,1},{2,10},{10,2},{3,11},{11,3},{4,12},{12,4},... | collective-permute-start | bytes 9437192 | tf_op jit(solution)/shard_map/ppermute | solution.py:17
  42.9 57.4 %collective-permute-start.16 = (bf16[3,2,512,512]{3,2,1,0:T(8,128)(2,1)}, bf16[3,2,512,512]{3,2,1,0:T(8,128)(2,1)}, u32[]{:S(2)}, u32[]{:S(2)}) collective-permute-start(bf16[3,2,512,512]{3,2,1,0:T(8,128)(2,1)} %get-tuple-element.69), channel_id=1, source_target_pairs={{0,8},{8,0},{1,9},{9,1},{2,10},{10,2},{3,11},{11,3},{4,12},{12,4},... | collective-permute-start | bytes 9437192 | tf_op jit(solution)/shard_map/ppermute | solution.py:17
  50.5 11.7 %copy-start.3 = (f32[2,256,512]{2,1,0:T(8,128)S(1)}, f32[2,256,512]{2,1,0:T(8,128)}, u32[]{:S(2)}) copy-start(f32[2,256,512]{2,1,0:T(8,128)} %get-tuple-element.55) | copy-start | bytes 3145732
  60.3 24.8 %collective-permute-start.13 = (bf16[2,2,256,512]{3,2,1,0:T(8,128)(2,1)S(1)}, bf16[2,2,256,512]{3,2,1,0:T(8,128)(2,1)S(1)}, u32[]{:S(2)}, u32[]{:S(2)}) collective-permute-start(bf16[2,2,256,512]{3,2,1,0:T(8,128)(2,1)S(1)} %sums.10), channel_id=1, source_target_pairs={{0,1},{1,0},{2,3},{3,2},{4,5},{5,4},{6,7},{7,6},{8,9},{9,8},{10,11... | collective-permute-start | bytes 3145736 | tf_op jit(solution)/shard_map/ppermute | solution.py:17
  62.5 24.0 %collective-permute-start.12 = (bf16[2,2,256,512]{3,2,1,0:T(8,128)(2,1)S(1)}, bf16[2,2,256,512]{3,2,1,0:T(8,128)(2,1)S(1)}, u32[]{:S(2)}, u32[]{:S(2)}) collective-permute-start(bf16[2,2,256,512]{3,2,1,0:T(8,128)(2,1)S(1)} %pad_maximum_fusion), channel_id=1, source_target_pairs={{2,4},{3,5},{4,2},{5,3},{10,12},{11,13},{12,10},{13,11},{18,20},{1... | collective-permute-start | bytes 3145736 | tf_op jit(solution)/shard_map/ppermute | solution.py:308
  63.3 6.4 %copy-start = (bf16[4,2,512,512]{3,2,1,0:T(8,128)(2,1)}, bf16[4,2,512,512]{3,2,1,0:T(8,128)(2,1)S(1)}, u32[]{:S(2)}) copy-start(bf16[4,2,512,512]{3,2,1,0:T(8,128)(2,1)S(1)} %collective-permute-done.11.refs_0_) | copy-start | bytes 12582916
  63.3 27.5 %collective-permute-start.14 = (bf16[2,2,256,512]{3,2,1,0:T(8,128)(2,1)S(1)}, bf16[2,2,256,512]{3,2,1,0:T(8,128)(2,1)S(1)}, u32[]{:S(2)}, u32[]{:S(2)}) collective-permute-start(bf16[2,2,256,512]{3,2,1,0:T(8,128)(2,1)S(1)} %pad_maximum_fusion), channel_id=1, source_target_pairs={{0,2},{1,3},{6,4},{7,5},{8,10},{9,11},{14,12},{15,13},{16,18},{17,... | collective-permute-start | bytes 3145736 | tf_op jit(solution)/shard_map/ppermute | solution.py:307
  74.5 16.5 %copy-start.1 = (f32[2,256,512]{2,1,0:T(8,128)S(1)}, f32[2,256,512]{2,1,0:T(8,128)}, u32[]{:S(2)}) copy-start(f32[2,256,512]{2,1,0:T(8,128)} %get-tuple-element.64) | copy-start | bytes 3145732
  85.1 23.9 %collective-permute-start.17 = (bf16[2,2,256,512]{3,2,1,0:T(8,128)(2,1)S(1)}, bf16[2,2,256,512]{3,2,1,0:T(8,128)(2,1)S(1)}, u32[]{:S(2)}, u32[]{:S(2)}) collective-permute-start(bf16[2,2,256,512]{3,2,1,0:T(8,128)(2,1)S(1)} %sums.12), channel_id=1, source_target_pairs={{0,1},{1,0},{2,3},{3,2},{4,5},{5,4},{6,7},{7,6},{8,9},{9,8},{10,11... | collective-permute-start | bytes 3145736 | tf_op jit(solution)/shard_map/ppermute | solution.py:17
  92.0 28.9 %collective-permute-start.18 = (bf16[2,256,512]{2,1,0:T(8,128)(2,1)}, bf16[2,256,512]{2,1,0:T(8,128)(2,1)}, u32[]{:S(2)}, u32[]{:S(2)}) collective-permute-start(bf16[2,256,512]{2,1,0:T(8,128)(2,1)} %fusion.4), channel_id=1, source_target_pairs={{0,2},{1,3},{2,0},{3,1},{4,6},{5,7},{6,4},{7,5},{8,10},{9,11},{10,... | collective-permute-start | bytes 1572872 | tf_op jit(solution)/shard_map/ppermute | solution.py:17
  94.4 26.4 %collective-permute-start.19 = (bf16[2,256,512]{2,1,0:T(8,128)(2,1)S(1)}, bf16[2,256,512]{2,1,0:T(8,128)(2,1)}, u32[]{:S(2)}, u32[]{:S(2)}) collective-permute-start(bf16[2,256,512]{2,1,0:T(8,128)(2,1)S(1)} %fusion.5), channel_id=1, source_target_pairs={{0,4},{1,5},{2,6},{3,7},{4,0},{5,1},{6,2},{7,3},{8,12},{9,13},{10,... | collective-permute-start | bytes 1572872 | tf_op jit(solution)/shard_map/ppermute | solution.py:17
  100.3 10.7 %copy-start.2 = (f32[2,256,512]{2,1,0:T(8,128)S(1)}, f32[2,256,512]{2,1,0:T(8,128)}, u32[]{:S(2)}) copy-start(f32[2,256,512]{2,1,0:T(8,128)} %get-tuple-element.72) | copy-start | bytes 3145732
  109.0 32.3 %collective-permute-start.20 = (bf16[2,2,256,512]{3,2,1,0:T(8,128)(2,1)S(1)}, bf16[2,2,256,512]{3,2,1,0:T(8,128)(2,1)}, u32[]{:S(2)}, u32[]{:S(2)}) collective-permute-start(bf16[2,2,256,512]{3,2,1,0:T(8,128)(2,1)S(1)} %sums.14), channel_id=1, source_target_pairs={{0,1},{1,0},{2,3},{3,2},{4,5},{5,4},{6,7},{7,6},{8,9},{9,8},{10,11... | collective-permute-start | bytes 3145736 | tf_op jit(solution)/shard_map/ppermute | solution.py:17
  112.0 26.3 %collective-permute-start.21 = (bf16[2,256,512]{2,1,0:T(8,128)(2,1)}, bf16[2,256,512]{2,1,0:T(8,128)(2,1)}, u32[]{:S(2)}, u32[]{:S(2)}) collective-permute-start(bf16[2,256,512]{2,1,0:T(8,128)(2,1)} %fusion.2), channel_id=1, source_target_pairs={{0,2},{1,3},{2,0},{3,1},{4,6},{5,7},{6,4},{7,5},{8,10},{9,11},{10,... | collective-permute-start | bytes 1572872 | tf_op jit(solution)/shard_map/ppermute | solution.py:17
  115.0 26.3 %collective-permute-start.22 = (bf16[2,256,512]{2,1,0:T(8,128)(2,1)}, bf16[2,256,512]{2,1,0:T(8,128)(2,1)}, u32[]{:S(2)}, u32[]{:S(2)}) collective-permute-start(bf16[2,256,512]{2,1,0:T(8,128)(2,1)} %fusion.3), channel_id=1, source_target_pairs={{0,4},{1,5},{2,6},{3,7},{4,0},{5,1},{6,2},{7,3},{8,12},{9,13},{10,... | collective-permute-start | bytes 1572872 | tf_op jit(solution)/shard_map/ppermute | solution.py:17
  120.8 20.5 %copy-start.4 = (f32[2,256,512]{2,1,0:T(8,128)S(1)}, f32[2,256,512]{2,1,0:T(8,128)}, u32[]{:S(2)}) copy-start(f32[2,256,512]{2,1,0:T(8,128)} %get-tuple-element.78) | copy-start | bytes 3145732
  143.8 1.6 %collective-permute-start.23 = (bf16[128,1024]{1,0:T(8,128)(2,1)S(1)}, bf16[128,1024]{1,0:T(8,128)(2,1)S(1)}, u32[]{:S(2)}, u32[]{:S(2)}) collective-permute-start(bf16[128,1024]{1,0:T(8,128)(2,1)S(1)} %fusion.12), channel_id=1, source_target_pairs={{0,8},{8,0},{1,9},{9,1},{2,10},{10,2},{3,11},{11,3},{4,12},{12,4},... | collective-permute-start | bytes 786440 | tf_op jit(solution)/shard_map/ppermute | solution.py:17

commit v5 on v4

--- a/solution.py
+++ b/solution.py
@@ -19,6 +19,25 @@
 
 def after(value, *earlier):
     return lax.optimization_barrier((value, *earlier))[0]
+
+
+def split_kernel(own_ref, other_ref, gains_ref, out_ref):
+    rows, depth = own_ref.shape
+    for i, ref in enumerate((own_ref, other_ref)):
+        value = ref[...].astype(jnp.float32) * gains_ref[i : i + 1, :]
+        high = value.astype(jnp.bfloat16)
+        columns = slice(i * depth, (i + 1) * depth)
+        out_ref[:rows, columns] = high
+        out_ref[rows:, columns] = (value - high.astype(jnp.float32)).astype(jnp.bfloat16)
+
+
+def split(own, other, gains):
+    rows, depth = own.shape
+    return pl.pallas_call(
+        split_kernel,
+        out_shape=jax.ShapeDtypeStruct((2 * rows, 2 * depth), jnp.bfloat16),
+        name="split",
+    )(own, other, gains)
 
 
 def cut_copies(groups, lanes, at_ref, gate_ref, up_ref, out_refs, held, in_sems, out_sems):
@@ -125,6 +144,9 @@
             rows = slice(b * side, (b + 1) * side)
             kept[n, i, rows, :] = kept[n, i, rows, :] * masks[i * blocks + b : i * blocks + b + 1, :]
         total = jnp.dot(x_ref[...], kept[n, i], preferred_element_type=jnp.float32)
+        tokens = result.shape[2]
+        if total.shape[0] > tokens:
+            total = total[:tokens] + total[tokens:]
         result[n, i] = total.astype(result.dtype)
         copy_out(n, i).start()
     for copy_in, copy_out_cut in cuts:
@@ -136,9 +158,8 @@
         copy_out_cut.wait()
 
 
-def sums(at, x, gate_weight, up_weight, theirs, masks, side, places, lanes, dtype, stacked, partner, groups):
+def sums(at, x, gate_weight, up_weight, theirs, masks, side, places, lanes, dtype, stacked, partner, groups, tokens):
     depth = gate_weight.shape[0]
-    tokens = x.shape[0]
     count = len(places)
     vmem = pl.BlockSpec(memory_space=pltpu.VMEM)
     hbm = pl.BlockSpec(memory_space=pltpu.HBM)
@@ -209,6 +230,8 @@
         emit(values[0])
         swap(groups, values)
 
+    if pairs == 4:
+        fetch([(3, 1, 0), (3, 1, 1)])
     raw = []
     for flip in range(2):
         moves = []
@@ -219,9 +242,13 @@
         raw.append(lax.ppermute(piece, ("wide", "tensor"), moves))
     values = tokens.astype(jnp.float32)
     squares = jnp.sum(values * values, axis=-1).reshape(1, rows)
-    total = squares
-    for p in range(1, pairs):
-        total = total + exchange(squares, "tensor", 2 * p)
+    squares_other = exchange(squares, "wide", 1)
+    squares = jnp.where(
+        half == 0,
+        jnp.concatenate([squares, squares_other], axis=0),
+        jnp.concatenate([squares_other, squares], axis=0),
+    )
+    squares = squares + exchange(squares, "tensor", 1)
     raw = jnp.where(shard % 2 == 1, jnp.concatenate(raw[::-1]), jnp.concatenate(raw))
     masks = jnp.concatenate(
         [
@@ -231,25 +258,21 @@
         ]
     ).astype(jnp.bfloat16)
     gains = jnp.stack([lax.dynamic_slice_in_dim(gain, r, depth, 0) for r in first_rows])
-    latest[:] = [total, raw, masks, gains]
-    if pairs == 4:
-        fetch([(3, 1, 0), (3, 1, 1)])
-    raw_other = exchange(after(raw, total), "wide", 1)
-    total = total + exchange(after(total, raw), "tensor", 1)
-    scale = lax.rsqrt(total / features + EPS)
-    scale_other = exchange(scale, "wide", 1)
-    scales = jnp.where(
-        half == 0,
-        jnp.concatenate([scale, scale_other], axis=1),
-        jnp.concatenate([scale_other, scale], axis=1),
-    ).reshape(2 * rows, 1)
-    normed = jnp.concatenate(
-        [(v.astype(jnp.float32) * scales * gains[i : i + 1]).astype(jnp.bfloat16) for i, v in enumerate((raw, raw_other))], axis=1
-    )
-
-    emit(normed)
-
-    def chip_sums(units, stacked=True, groups=()):
+    raw_other = exchange(raw, "wide", 1)
+
+    def normalise(start):
+        total, bit = after(squares, start), 2
+        while bit < shards:
+            total = total + exchange(total, "tensor", bit)
+            bit *= 2
+        scales = lax.rsqrt(total / features + EPS).reshape(2 * rows, 1)
+        parts = [
+            (part.astype(jnp.float32) * scales * gains[i : i + 1]).astype(jnp.bfloat16)
+            for i, part in enumerate((raw, raw_other))
+        ]
+        return jnp.concatenate(parts, axis=1), scales
+
+    def chip_sums(x, units, stacked=True, groups=()):
         messages = []
         for unit in units:
             if not any(theirs[unit][0] is message for message in messages):
@@ -259,8 +282,8 @@
         )
         dtype = jnp.bfloat16 if stacked else jnp.float32
         values = sums(
-            mine, in_turn(normed), gate_weight, up_weight, messages, masks, side, places, lanes, dtype, stacked,
-            partners, in_place(groups)
+            mine, in_turn(x), gate_weight, up_weight, messages, masks, side, places, lanes, dtype, stacked,
+            partners, in_place(groups), 2 * rows
         )
         emit(values[0])
         outs = 1 if stacked else len(units)
@@ -291,7 +314,10 @@
         by_neighbour = tensor_pairs(((0, 1), (3, 2)))
         middle = tensor_pairs(((1, 2), (2, 1)))
 
+        latest.extend([masks, gains])
+        unscaled = split(after(raw, squares), raw_other, gains)
         far_3 = chip_sums(
+            unscaled,
             [(3, 1, 0), (3, 1, 1)],
             groups=[
                 [(3, 0, 0), (3, 0, 1), (2, 1, 0), (1, 1, 0)],
@@ -299,32 +325,34 @@
             ],
         )
         pair3 = exchange(far_3, "tensor", 1)
+        normed, scales = normalise(far_3)
         fetch([(2, 0, 1), (1, 0, 1), (0, 0, 0)], [(0, 1, 0), (0, 1, 1), (0, 0, 1)])
-        near3 = chip_sums([(3, 0, 0), (3, 0, 1)], stacked=False)
-        far_a = chip_sums([(2, 1, 0), (1, 1, 0)])
+        near3 = chip_sums(unscaled, [(3, 0, 0), (3, 0, 1)], stacked=False)
+        far_a = chip_sums(unscaled, [(2, 1, 0), (1, 1, 0)])
         pair_a = exchange(in_turn(far_a, pair3), "tensor", 1)
         third = jnp.stack([add(near3[h], pair3[h]) for h in range(2)])
         relay = lax.ppermute(third, "tensor", by_neighbour)
         across = lax.ppermute(third, "tensor", middle)
-        near_a = chip_sums([(2, 0, 0), (1, 0, 0)], stacked=False)
-        far_b = chip_sums([(2, 1, 1), (1, 1, 1)])
+        near_a = chip_sums(normed, [(2, 0, 0), (1, 0, 0)], stacked=False)
+        far_b = chip_sums(normed, [(2, 1, 1), (1, 1, 1)])
         pair_b = exchange(in_turn(far_b, pair_a), "tensor", 1)
-        second_a = exchange(add(near_a[0], pair_a[0], relay[0]), "tensor", 4)
-        first_a = exchange(add(after(near_a[1], across), pair_a[1]), "tensor", 2)
-        near_b = chip_sums([(2, 0, 1), (1, 0, 1)], stacked=False)
-        far_0 = chip_sums([(0, 1, 0), (0, 1, 1)])
+        second_a = exchange(add(near_a[0], (wide(pair_a[0]) + wide(relay[0])) * scales), "tensor", 4)
+        first_a = exchange(add(after(near_a[1], across), wide(pair_a[1]) * scales), "tensor", 2)
+        near_b = chip_sums(normed, [(2, 0, 1), (1, 0, 1)], stacked=False)
+        far_0 = chip_sums(normed, [(0, 1, 0), (0, 1, 1)])
         pair_0 = exchange(in_turn(far_0, pair_b), "tensor", 1)
-        second_b = exchange(add(near_b[0], pair_b[0], relay[1]), "tensor", 4)
+        second_b = exchange(add(near_b[0], pair_b[0], wide(relay[1]) * scales), "tensor", 4)
         first_b = exchange(add(near_b[1], pair_b[1]), "tensor", 2)
-        own = chip_sums([(0, 0, 0), (0, 0, 1)], stacked=False)
-        early = emit(in_turn(own[0]) + wide(first_a) + wide(second_a) + wide(across[0]))
-        hidden = [finish(early, pair_0[0]), finish(own[1], pair_0[1], first_b, second_b, across[1])]
+        own = chip_sums(normed, [(0, 0, 0), (0, 0, 1)], stacked=False)
+        early = emit(in_turn(own[0]) + wide(first_a) + wide(second_a) + wide(across[0]) * scales)
+        hidden = [finish(early, pair_0[0]), finish(own[1], pair_0[1], first_b, second_b, wide(across[1]) * scales)]
         return jnp.concatenate(give(jnp.concatenate(hidden, axis=1)), axis=1)
     received = []
+    normed, _ = normalise(squares)
     for p in range(pairs - 1, -1, -1):
         fetch([(p, 1, 0), (p, 0, 0)])
-        from_pair = exchange(chip_sums([(p, 1, 0)])[0], "tensor", 1)
-        own = chip_sums([(p, 0, 0)], stacked=False)[0]
+        from_pair = exchange(chip_sums(normed, [(p, 1, 0)])[0], "tensor", 1)
+        own = chip_sums(normed, [(p, 0, 0)], stacked=False)[0]
         if p:
             received.append(exchange(add(own, from_pair), "tensor", 2 * p))
     return jnp.concatenate(give(finish(own, from_pair, *received)), axis=1)

time: 147 us -> 142 us (0.966)
  waiting for transfers between devices: 48 us -> 35.4 us
  Pallas kernels: 49.7 us -> 56.5 us
  starting transfers between devices: 35.5 us -> 30.9 us
  local copies, waits for them, and re-layouts: 1.78 us -> 4.32 us
  other arithmetic: 10.9 us -> 12.7 us
    ppermute x20 -> x19, waiting for transfers between devices: 41.4 us -> 35.4 us  [exchange(): return lax.ppermute(value, axis, [(i, i ^ bit) for i in range(size)])]
    pallas_call x8, Pallas kernels: 40.6 us -> 45.2 us  [sums(): pl.pallas_call(functools.partial(sums_kernel, places, lanes, side, stacke...]
    ppermute x1, waiting for transfers between devices: 4.27 us -> 0.01 us  [local(): relay = lax.ppermute(third, 'tensor', by_neighbour)]
    ppermute x1, starting transfers between devices: 6.36 us -> 2.58 us  [local(): relay = lax.ppermute(third, 'tensor', by_neighbour)]
    unnamed x10 -> x26, local copies, waits for them, and re-layouts: 0.02 us -> 3.52 us
    convert_element_type x6, other arithmetic: 3.47 us -> 6.05 us  [add(): return emit(total.astype(jnp.bfloat16))]
    ppermute x20 -> x19, starting transfers between devices: 26.2 us -> 23.7 us  [exchange(): return lax.ppermute(value, axis, [(i, i ^ bit) for i in range(size)])]
    ppermute x2, waiting for transfers between devices: 2.27 us -> 0.01 us  [local(): raw.append(lax.ppermute(piece, ('wide', 'tensor'), moves))]
  transfers between devices with their start and end apart: 24 -> 23, of which waited for: 11 -> 7; matrix products, arithmetic and copies ran while one was open for 6% -> 7% of each run, Pallas kernels for 25% -> 30%
where the time goes in v5:
time: 142 us; the launch traced here: 140 us
  Pallas kernels  56.5 us (40%)
  waiting for transfers between devices  35.4 us (25%)
  starting transfers between devices  30.9 us (22%)
  other arithmetic  12.7 us (9%)
  local copies, waits for them, and re-layouts  4.32 us (3%)
    pallas_call x8, Pallas kernels, sums(): pl.pallas_call(functools.partial(sums_kernel, places, lanes, side, stacke...  45.2 us
    ppermute x19, waiting for transfers between devices, exchange(): return lax.ppermute(value, axis, [(i, i ^ bit) for i in range(size)])  35.4 us
    ppermute x19, starting transfers between devices, exchange(): return lax.ppermute(value, axis, [(i, i ^ bit) for i in range(size)])  23.7 us
    pallas_call x2, Pallas kernels, cut(): pl.pallas_call(functools.partial(cut_kernel, groups, lanes), in_specs=[pl...  9.1 us
    convert_element_type x6, other arithmetic, add(): return emit(total.astype(jnp.bfloat16))  6.05 us
    ppermute x2, starting transfers between devices, local(): raw.append(lax.ppermute(piece, ('wide', 'tensor'), moves))  3.68 us
    unnamed x26, local copies, waits for them, and re-layouts  3.52 us
  transfers between devices with their start and end apart: 23, of which 7 were waited for; matrix products, arithmetic and copies ran while one was open for 7% of the time, Pallas kernels for 30%

profile of v5, /device:TPU:0, one launch (start us, length us, event | category | flops | bytes accessed | tf_op | source)
XLA Modules:
  0.0 140.2 jit_solution(6066838331612939974)
XLA Ops:
  0.0 0.1 pad_add_fusion.at_ref.partner_ref
  0.1 3.0 %cut.2 = bf16[2,2,512,512]{3,2,1,0:T(8,128)(2,1)} custom-call(s32[3]{0:T(128)S(1)} %pad_add_fusion.at_ref.partner_ref, bf16[512,16384]{1,0:T(8,128)(2,1)} %gate_ref.19, bf16[512,16384]{1,0:T(8,128)(2,1)} %up_ref.19), custom_call_target="tpu_custom_call" | custom-call | tf_op jit(solution)/shard_map/cut/pallas_call | solution.py:83
  3.1 0.5 collective-permute-start.5
  3.6 0.1 multiply_reduce_fusion
  3.8 0.1 collective-permute-start.2
  3.9 3.0 %collective-permute-start = (bf16[128,512]{1,0:T(8,128)(2,1)S(1)}, bf16[128,512]{1,0:T(8,128)(2,1)S(1)}, u32[]{:S(2)}, u32[]{:S(2)}) collective-permute-start(bf16[128,512]{1,0:T(8,128)(2,1)S(1)} %get-tuple-element.81), channel_id=1, source_target_pairs={{8,0},{0,1},{9,2},{1,3},{10,4},{2,5},{11,6},{3,7},{12,8},{4,9},{13... | collective-permute-start | bytes 393224 | tf_op jit(solution)/shard_map/ppermute | solution.py:242
  6.9 0.7 collective-permute-start.1
  7.6 0.8 fusion.19
  8.4 0.8 dynamic-slice_convert_fusion.1
  9.2 0.6 pad_maximum_fusion.4.gains_ref
  9.8 5.3 %collective-permute-start.3 = (f32[2,128]{1,0:T(2,128)S(1)}, f32[2,128]{1,0:T(2,128)S(1)}, u32[]{:S(2)}, u32[]{:S(2)}) collective-permute-start(f32[2,128]{1,0:T(2,128)S(1)} %maximum_select_fusion.1), channel_id=1, source_target_pairs={{0,1},{1,0},{2,3},{3,2},{4,5},{5,4},{6,7},{7,6},{8,9},{9,8},{10,11... | collective-permute-start | bytes 3080 | tf_op jit(solution)/shard_map/ppermute | solution.py:17
  15.2 0.1 collective-permute-start.4
  15.3 0.1 pad_add_fusion.1.at_ref
  15.4 1.3 collective-permute-done.3
  16.7 0.1 collective-permute-done.4.other_ref
  16.9 0.7 copy-done.9
  17.6 2.2 %split.1.x_ref = bf16[512,1024]{1,0:T(8,128)(2,1)} custom-call(bf16[256,512]{1,0:T(8,128)(2,1)} %copy-done.2, bf16[256,512]{1,0:T(8,128)(2,1)} %copy-done.9, f32[2,512]{1,0:T(2,128)} %pad_maximum_fusion.4.gains_ref), custom_call_target="tpu_custom_call" | custom-call | tf_op jit(solution)/shard_map/split/pallas_call | solution.py:36
  19.8 10.8 %sums.8 = (bf16[2,2,256,512]{3,2,1,0:T(8,128)(2,1)S(1)}, bf16[4,2,512,512]{3,2,1,0:T(8,128)(2,1)}, bf16[4,2,512,512]{3,2,1,0:T(8,128)(2,1)}) custom-call(s32[3]{0:T(128)S(1)} %pad_add_fusion.1.at_ref, s32[3]{0:T(128)S(1)} %pad_add_fusion.at_ref.partner_ref, bf16[512,1024]{1,0:T(8,128)(2,1)} %split.1.x_ref, bf16[512,16384]{1,0:T(8,128)(2,1)} %gate_ref.19, ...), custom_call_target="tpu_custom_call" | custom-call | tf_op jit(solution)/shard_map/sums/pallas_call | solution.py:166
  30.6 0.2 collective-permute-start.8
  30.8 0.4 collective-permute-start.10
  31.2 1.9 %collective-permute-start.9 = (bf16[2,2,256,512]{3,2,1,0:T(8,128)(2,1)S(1)}, bf16[2,2,256,512]{3,2,1,0:T(8,128)(2,1)S(1)}, u32[]{:S(2)}, u32[]{:S(2)}) collective-permute-start(bf16[2,2,256,512]{3,2,1,0:T(8,128)(2,1)S(1)} %get-tuple-element.43), channel_id=1, source_target_pairs={{0,1},{1,0},{2,3},{3,2},{4,5},{5,4},{6,7},{7,6},{8,9},{9,8},{10,11... | collective-permute-start | bytes 3145736 | tf_op jit(solution)/shard_map/ppermute | solution.py:17
  33.1 1.3 collective-permute-start.6
  34.4 6.1 %cut.3 = (bf16[3,2,512,512]{3,2,1,0:T(8,128)(2,1)}, bf16[3,2,512,512]{3,2,1,0:T(8,128)(2,1)}) custom-call(s32[3]{0:T(128)S(1)} %pad_add_fusion.at_ref.partner_ref, bf16[512,16384]{1,0:T(8,128)(2,1)} %gate_ref.19, bf16[512,16384]{1,0:T(8,128)(2,1)} %up_ref.19), custom_call_target="tpu_custom_call" | custom-call | tf_op jit(solution)/shard_map/cut/pallas_call | solution.py:83
  40.4 0.1 collective-permute-start.14
  40.5 0.5 collective-permute-start.15
  41.0 2.0 %copy-done.1 = bf16[4,2,512,512]{3,2,1,0:T(8,128)(2,1)} copy-done((bf16[4,2,512,512]{3,2,1,0:T(8,128)(2,1)}, bf16[4,2,512,512]{3,2,1,0:T(8,128)(2,1)S(1)}, u32[]{:S(2)}) %copy-start.1) | copy-done | bytes 4194328
  43.1 1.6 %collective-permute-start.7 = (f32[2,128]{1,0:T(2,128)S(1)}, f32[2,128]{1,0:T(2,128)S(1)}, u32[]{:S(2)}, u32[]{:S(2)}) collective-permute-start(f32[2,128]{1,0:T(2,128)S(1)} %add.121), channel_id=1, source_target_pairs={{0,4},{1,5},{2,6},{3,7},{4,0},{5,1},{6,2},{7,3},{8,12},{9,13},{10,... | collective-permute-start | bytes 3080 | tf_op jit(solution)/shard_map/ppermute | solution.py:17
  44.7 6.5 %sums.9 = (f32[2,256,512]{2,1,0:T(8,128)S(1)}, f32[2,256,512]{2,1,0:T(8,128)}) custom-call(s32[3]{0:T(128)S(1)} %pad_add_fusion.1.at_ref, s32[3]{0:T(128)S(1)} %pad_add_fusion.at_ref.partner_ref, bf16[512,1024]{1,0:T(8,128)(2,1)} %split.1.x_ref, bf16[512,16384]{1,0:T(8,128)(2,1)} %gate_ref.19, bf16[512,16384]{1,0:T(8,128)(2,1)} %up_ref.19, ...), custom_call_target="tpu_custom_call" | custom-call | tf_op jit(solution)/shard_map/sums/pallas_call | solution.py:166
  51.1 5.8 %sums.10 = bf16[2,2,256,512]{3,2,1,0:T(8,128)(2,1)S(1)} custom-call(s32[3]{0:T(128)S(1)} %pad_add_fusion.1.at_ref, s32[3]{0:T(128)S(1)} %pad_add_fusion.at_ref.partner_ref, bf16[512,1024]{1,0:T(8,128)(2,1)} %split.1.x_ref, bf16[512,16384]{1,0:T(8,128)(2,1)} %gate_ref.19, bf16[512,16384]{1,0:T(8,128)(2,1)} %up_ref.19, ...), custom_call_target="tpu_custom_call" | custom-call | tf_op jit(solution)/shard_map/sums/pallas_call | solution.py:166
  57.0 2.1 %collective-permute-start.12 = (bf16[2,2,256,512]{3,2,1,0:T(8,128)(2,1)S(1)}, bf16[2,2,256,512]{3,2,1,0:T(8,128)(2,1)}, u32[]{:S(2)}, u32[]{:S(2)}) collective-permute-start(bf16[2,2,256,512]{3,2,1,0:T(8,128)(2,1)S(1)} %sums.10), channel_id=1, source_target_pairs={{0,1},{1,0},{2,3},{3,2},{4,5},{5,4},{6,7},{7,6},{8,9},{9,8},{10,11... | collective-permute-start | bytes 3145736 | tf_op jit(solution)/shard_map/ppermute | solution.py:17
  59.1 0.2 fusion.10
  59.2 0.2 fusion.9
  59.4 0.1 pad_maximum_fusion
  59.5 2.6 %collective-permute-start.13 = (bf16[2,2,256,512]{3,2,1,0:T(8,128)(2,1)S(1)}, bf16[2,2,256,512]{3,2,1,0:T(8,128)(2,1)S(1)}, u32[]{:S(2)}, u32[]{:S(2)}) collective-permute-start(bf16[2,2,256,512]{3,2,1,0:T(8,128)(2,1)S(1)} %pad_maximum_fusion), channel_id=1, source_target_pairs={{0,2},{1,3},{6,4},{7,5},{8,10},{9,11},{14,12},{15,13},{16,18},{17,... | collective-permute-start | bytes 3145736 | tf_op jit(solution)/shard_map/ppermute | solution.py:334
  62.1 0.9 collective-permute-start.11
  63.1 0.2 multiply_convert_fusion.1
  63.3 0.1 pad_maximum_fusion.1.x_ref
  63.3 0.7 copy-done
  64.1 4.7 %sums.11 = (f32[2,256,512]{2,1,0:T(8,128)S(1)}, f32[2,256,512]{2,1,0:T(8,128)}) custom-call(s32[3]{0:T(128)S(1)} %pad_add_fusion.1.at_ref, s32[3]{0:T(128)S(1)} %pad_add_fusion.at_ref.partner_ref, bf16[256,1024]{1,0:T(8,128)(2,1)S(1)} %pad_maximum_fusion.1.x_ref, bf16[512,16384]{1,0:T(8,128)(2,1)} %gate_ref.19, bf16[512,16384]{1,0:T(8,128)(2,1)} %up_ref.19, ...), custom_call_target="tpu_custom_call" | custom-call | tf_op jit(solution)/shard_map/sums/pallas_call | solution.py:166
  68.8 4.0 %sums.12 = bf16[2,2,256,512]{3,2,1,0:T(8,128)(2,1)S(1)} custom-call(s32[3]{0:T(128)S(1)} %pad_add_fusion.1.at_ref, s32[3]{0:T(128)S(1)} %pad_add_fusion.at_ref.partner_ref, bf16[256,1024]{1,0:T(8,128)(2,1)S(1)} %pad_maximum_fusion.1.x_ref, bf16[512,16384]{1,0:T(8,128)(2,1)} %gate_ref.19, bf16[512,16384]{1,0:T(8,128)(2,1)} %up_ref.19, ...), custom_call_target="tpu_custom_call" | custom-call | tf_op jit(solution)/shard_map/sums/pallas_call | solution.py:166
  72.8 9.5 %collective-permute-done.12 = bf16[2,2,256,512]{3,2,1,0:T(8,128)(2,1)} collective-permute-done((bf16[2,2,256,512]{3,2,1,0:T(8,128)(2,1)S(1)}, bf16[2,2,256,512]{3,2,1,0:T(8,128)(2,1)}, u32[]{:S(2)}, u32[]{:S(2)}) %collective-permute-start.12) | collective-permute-done | bytes 1048608 | tf_op jit(solution)/shard_map/ppermute | solution.py:17
  82.3 1.7 %collective-permute-start.16 = (bf16[2,2,256,512]{3,2,1,0:T(8,128)(2,1)S(1)}, bf16[2,2,256,512]{3,2,1,0:T(8,128)(2,1)S(1)}, u32[]{:S(2)}, u32[]{:S(2)}) collective-permute-start(bf16[2,2,256,512]{3,2,1,0:T(8,128)(2,1)S(1)} %sums.12), channel_id=1, source_target_pairs={{0,1},{1,0},{2,3},{3,2},{4,5},{5,4},{6,7},{7,6},{8,9},{9,8},{10,11... | collective-permute-start | bytes 3145736 | tf_op jit(solution)/shard_map/ppermute | solution.py:17
  84.0 1.7 %fusion.12 = bf16[2,256,512]{2,1,0:T(8,128)(2,1)S(1)} fusion(f32[2,256,512]{2,1,0:T(8,128)S(1)} %get-tuple-element.60, bf16[2,2,256,512]{3,2,1,0:T(8,128)(2,1)S(1)} %collective-permute-done.13, bf16[2,2,256,512]{3,2,1,0:T(8,128)(2,1)} %collective-permute-done.12, f32[256]{0:T(256)S(1)} %rsqrt_bitcast_fusion), kind=kLoop, calls=%fused_computation.24 | loop fusion | flops 1572864 | bytes 2622464 | tf_op jit(solution)/shard_map/convert_element_type | solution.py:303
  85.7 2.0 %fusion.8 = bf16[2,256,512]{2,1,0:T(8,128)(2,1)} fusion(f32[2,256,512]{2,1,0:T(8,128)S(1)} %copy-done.11, bf16[2,2,256,512]{3,2,1,0:T(8,128)(2,1)} %collective-permute-done.12, f32[256]{0:T(256)S(1)} %rsqrt_bitcast_fusion), kind=kLoop, calls=%fused_computation.17 | loop fusion | flops 1048576 | bytes 2098176 | tf_op jit(solution)/shard_map/convert_element_type | solution.py:303
  87.8 3.5 %collective-permute-start.17 = (bf16[2,256,512]{2,1,0:T(8,128)(2,1)}, bf16[2,256,512]{2,1,0:T(8,128)(2,1)}, u32[]{:S(2)}, u32[]{:S(2)}) collective-permute-start(bf16[2,256,512]{2,1,0:T(8,128)(2,1)} %fusion.8), channel_id=1, source_target_pairs={{0,2},{1,3},{2,0},{3,1},{4,6},{5,7},{6,4},{7,5},{8,10},{9,11},{10,... | collective-permute-start | bytes 1572872 | tf_op jit(solution)/shard_map/ppermute | solution.py:17
  91.3 0.9 collective-permute-start.18
  92.2 4.7 %sums.13 = (f32[2,256,512]{2,1,0:T(8,128)S(1)}, f32[2,256,512]{2,1,0:T(8,128)}) custom-call(s32[3]{0:T(128)S(1)} %pad_add_fusion.1.at_ref, s32[3]{0:T(128)S(1)} %pad_add_fusion.at_ref.partner_ref, bf16[256,1024]{1,0:T(8,128)(2,1)S(1)} %pad_maximum_fusion.1.x_ref, bf16[512,16384]{1,0:T(8,128)(2,1)} %gate_ref.19, bf16[512,16384]{1,0:T(8,128)(2,1)} %up_ref.19, ...), custom_call_target="tpu_custom_call" | custom-call | tf_op jit(solution)/shard_map/sums/pallas_call | solution.py:166
  97.0 3.9 %sums.14 = bf16[2,2,256,512]{3,2,1,0:T(8,128)(2,1)S(1)} custom-call(s32[3]{0:T(128)S(1)} %pad_add_fusion.1.at_ref, s32[3]{0:T(128)S(1)} %pad_add_fusion.at_ref.partner_ref, bf16[256,1024]{1,0:T(8,128)(2,1)S(1)} %pad_maximum_fusion.1.x_ref, bf16[512,16384]{1,0:T(8,128)(2,1)} %gate_ref.19, bf16[512,16384]{1,0:T(8,128)(2,1)} %up_ref.19, ...), custom_call_target="tpu_custom_call" | custom-call | tf_op jit(solution)/shard_map/sums/pallas_call | solution.py:166
  100.9 5.7 %collective-permute-done.16 = bf16[2,2,256,512]{3,2,1,0:T(8,128)(2,1)S(1)} collective-permute-done((bf16[2,2,256,512]{3,2,1,0:T(8,128)(2,1)S(1)}, bf16[2,2,256,512]{3,2,1,0:T(8,128)(2,1)S(1)}, u32[]{:S(2)}, u32[]{:S(2)}) %collective-permute-start.16) | collective-permute-done | bytes 1048608 | tf_op jit(solution)/shard_map/ppermute | solution.py:17
  106.6 1.4 %collective-permute-start.19 = (bf16[2,2,256,512]{3,2,1,0:T(8,128)(2,1)S(1)}, bf16[2,2,256,512]{3,2,1,0:T(8,128)(2,1)}, u32[]{:S(2)}, u32[]{:S(2)}) collective-permute-start(bf16[2,2,256,512]{3,2,1,0:T(8,128)(2,1)S(1)} %sums.14), channel_id=1, source_target_pairs={{0,1},{1,0},{2,3},{3,2},{4,5},{5,4},{6,7},{7,6},{8,9},{9,8},{10,11... | collective-permute-start | bytes 3145736 | tf_op jit(solution)/shard_map/ppermute | solution.py:17
  108.0 1.0 fusion.6
  109.0 1.0 fusion.4
  110.1 2.0 %collective-permute-start.21 = (bf16[2,256,512]{2,1,0:T(8,128)(2,1)}, bf16[2,256,512]{2,1,0:T(8,128)(2,1)S(1)}, u32[]{:S(2)}, u32[]{:S(2)}) collective-permute-start(bf16[2,256,512]{2,1,0:T(8,128)(2,1)} %fusion.6), channel_id=1, source_target_pairs={{0,4},{1,5},{2,6},{3,7},{4,0},{5,1},{6,2},{7,3},{8,12},{9,13},{10,... | collective-permute-start | bytes 1572872 | tf_op jit(solution)/shard_map/ppermute | solution.py:17
  112.0 4.7 %sums.15 = (f32[2,256,512]{2,1,0:T(8,128)S(1)}, f32[2,256,512]{2,1,0:T(8,128)}) custom-call(s32[3]{0:T(128)S(1)} %pad_add_fusion.1.at_ref, s32[3]{0:T(128)S(1)} %pad_add_fusion.at_ref.partner_ref, bf16[256,1024]{1,0:T(8,128)(2,1)S(1)} %pad_maximum_fusion.1.x_ref, bf16[512,16384]{1,0:T(8,128)(2,1)} %gate_ref.19, bf16[512,16384]{1,0:T(8,128)(2,1)} %up_ref.19, ...), custom_call_target="tpu_custom_call" | custom-call | tf_op jit(solution)/shard_map/sums/pallas_call | solution.py:166
  116.8 1.3 collective-permute-done.17
  118.1 1.5 %fusion.3 = f32[2,256,512]{2,1,0:T(8,128)S(1)} fusion(bf16[2,256,512]{2,1,0:T(8,128)(2,1)} %collective-permute-done.18, f32[2,256,512]{2,1,0:T(8,128)S(1)} %get-tuple-element.72, bf16[2,256,512]{2,1,0:T(8,128)(2,1)} %collective-permute-done.17, bf16[2,2,256,512]{3,2,1,0:T(8,128)(2,1)S(1)} %copy-done.5, f32[256]{0:T(256)S(1)} %rsqrt_bitcast_fusion), kind=kLoop, calls=%fused_computation.8 | loop fusion | flops 1835008 | bytes 3671040 | tf_op jit(solution)/shard_map/add | solution.py:347
  119.6 15.9 %collective-permute-done.20 = bf16[2,256,512]{2,1,0:T(8,128)(2,1)S(1)} collective-permute-done((bf16[2,256,512]{2,1,0:T(8,128)(2,1)}, bf16[2,256,512]{2,1,0:T(8,128)(2,1)S(1)}, u32[]{:S(2)}, u32[]{:S(2)}) %collective-permute-start.20) | collective-permute-done | bytes 524320 | tf_op jit(solution)/shard_map/ppermute | solution.py:17
  135.5 1.8 %fusion = (f32[2,256,512]{2,1,0:T(8,128)S(1)}, f32[2,256,512]{2,1,0:T(8,128)S(1)}) fusion(f32[2,256,512]{2,1,0:T(8,128)S(1)} %copy-done.12, bf16[2,256,512]{2,1,0:T(8,128)(2,1)S(1)} %collective-permute-done.21, bf16[2,256,512]{2,1,0:T(8,128)(2,1)S(1)} %collective-permute-done.20, bf16[2,2,256,512]{3,2,1,0:T(8,128)(2,1)S(1)} %copy-done.5, ...), kind=kLoop, calls=%fused_computation.2 | loop fusion | flops 2883584 | bytes 6816768 | tf_op jit(solution)/shard_map/add | solution.py:296
  137.3 0.2 fusion.14
  137.5 0.2 fusion.16
  137.7 0.1 collective-permute-start.22
  137.7 1.5 %collective-permute-done.22 = bf16[128,1024]{1,0:T(8,128)(2,1)S(1)} collective-permute-done((bf16[128,1024]{1,0:T(8,128)(2,1)S(1)}, bf16[128,1024]{1,0:T(8,128)(2,1)S(1)}, u32[]{:S(2)}, u32[]{:S(2)}) %collective-permute-start.22) | collective-permute-done | bytes 262176 | tf_op jit(solution)/shard_map/ppermute | solution.py:17
  139.3 0.1 broadcast_select_fusion.1
  139.4 0.8 pad_maximum_fusion.2
  (48 shorter events, 0.2 us)
Async XLA Ops:
  0.1 3.5 %copy-start.8 = (bf16[128,1024]{1,0:T(8,128)(2,1)S(1)}, bf16[128,1024]{1,0:T(8,128)(2,1)}, u32[]{:S(2)}) copy-start(bf16[128,1024]{1,0:T(8,128)(2,1)} %param.6) | copy-start | bytes 786436
  3.1 16.7 %collective-permute-start.5 = (bf16[2,2,512,512]{3,2,1,0:T(8,128)(2,1)}, bf16[2,2,512,512]{3,2,1,0:T(8,128)(2,1)}, u32[]{:S(2)}, u32[]{:S(2)}) collective-permute-start(bf16[2,2,512,512]{3,2,1,0:T(8,128)(2,1)} %cut.2), channel_id=1, source_target_pairs={{0,8},{8,0},{1,9},{9,1},{2,10},{10,2},{3,11},{11,3},{4,12},{12,4},... | collective-permute-start | bytes 6291464 | tf_op jit(solution)/shard_map/ppermute | solution.py:17
  3.8 6.1 %collective-permute-start.2 = (f32[1,128]{1,0:T(1,128)S(1)}, f32[1,128]{1,0:T(1,128)S(1)}, u32[]{:S(2)}, u32[]{:S(2)}) collective-permute-start(f32[1,128]{1,0:T(1,128)S(1)} %bitcast.90), channel_id=1, source_target_pairs={{0,8},{8,0},{1,9},{9,1},{2,10},{10,2},{3,11},{11,3},{4,12},{12,4},... | collective-permute-start | bytes 1544 | tf_op jit(solution)/shard_map/ppermute | solution.py:17
  3.9 11.3 %collective-permute-start = (bf16[128,512]{1,0:T(8,128)(2,1)S(1)}, bf16[128,512]{1,0:T(8,128)(2,1)S(1)}, u32[]{:S(2)}, u32[]{:S(2)}) collective-permute-start(bf16[128,512]{1,0:T(8,128)(2,1)S(1)} %get-tuple-element.81), channel_id=1, source_target_pairs={{8,0},{0,1},{9,2},{1,3},{10,4},{2,5},{11,6},{3,7},{12,8},{4,9},{13... | collective-permute-start | bytes 393224 | tf_op jit(solution)/shard_map/ppermute | solution.py:242
  6.9 8.3 %collective-permute-start.1 = (bf16[128,512]{1,0:T(8,128)(2,1)S(1)}, bf16[128,512]{1,0:T(8,128)(2,1)S(1)}, u32[]{:S(2)}, u32[]{:S(2)}) collective-permute-start(bf16[128,512]{1,0:T(8,128)(2,1)S(1)} %get-tuple-element.82), channel_id=1, source_target_pairs={{0,0},{8,1},{1,2},{9,3},{2,4},{10,5},{3,6},{11,7},{4,8},{12,9},{5,... | collective-permute-start | bytes 393224 | tf_op jit(solution)/shard_map/ppermute | solution.py:242
  9.8 6.9 %collective-permute-start.3 = (f32[2,128]{1,0:T(2,128)S(1)}, f32[2,128]{1,0:T(2,128)S(1)}, u32[]{:S(2)}, u32[]{:S(2)}) collective-permute-start(f32[2,128]{1,0:T(2,128)S(1)} %maximum_select_fusion.1), channel_id=1, source_target_pairs={{0,1},{1,0},{2,3},{3,2},{4,5},{5,4},{6,7},{7,6},{8,9},{9,8},{10,11... | collective-permute-start | bytes 3080 | tf_op jit(solution)/shard_map/ppermute | solution.py:17
  15.2 1.6 %copy-start.2 = (bf16[256,512]{1,0:T(8,128)(2,1)}, bf16[256,512]{1,0:T(8,128)(2,1)S(1)}, u32[]{:S(2)}) copy-start(bf16[256,512]{1,0:T(8,128)(2,1)S(1)} %maximum_select_fusion.own_ref) | copy-start | bytes 786436
  15.2 1.6 %collective-permute-start.4 = (bf16[256,512]{1,0:T(8,128)(2,1)S(1)}, bf16[256,512]{1,0:T(8,128)(2,1)S(1)}, u32[]{:S(2)}, u32[]{:S(2)}) collective-permute-start(bf16[256,512]{1,0:T(8,128)(2,1)S(1)} %maximum_select_fusion.own_ref), channel_id=1, source_target_pairs={{0,8},{8,0},{1,9},{9,1},{2,10},{10,2},{3,11},{11,3},{4,12},{12,4},... | collective-permute-start | bytes 786440 | tf_op jit(solution)/shard_map/ppermute | solution.py:17
  16.8 0.7 copy-start.9
  30.6 10.5 %collective-permute-start.8 = (bf16[4,2,512,512]{3,2,1,0:T(8,128)(2,1)}, bf16[4,2,512,512]{3,2,1,0:T(8,128)(2,1)S(1)}, u32[]{:S(2)}, u32[]{:S(2)}) collective-permute-start(bf16[4,2,512,512]{3,2,1,0:T(8,128)(2,1)} %get-tuple-element.48), channel_id=1, source_target_pairs={{0,8},{8,0},{1,9},{9,1},{2,10},{10,2},{3,11},{11,3},{4,12},{12,4},... | collective-permute-start | bytes 12582920 | tf_op jit(solution)/shard_map/ppermute | solution.py:17
  30.8 31.3 %collective-permute-start.10 = (bf16[4,2,512,512]{3,2,1,0:T(8,128)(2,1)}, bf16[4,2,512,512]{3,2,1,0:T(8,128)(2,1)S(1)}, u32[]{:S(2)}, u32[]{:S(2)}) collective-permute-start(bf16[4,2,512,512]{3,2,1,0:T(8,128)(2,1)} %get-tuple-element.55), channel_id=1, source_target_pairs={{0,8},{8,0},{1,9},{9,1},{2,10},{10,2},{3,11},{11,3},{4,12},{12,4},... | collective-permute-start | bytes 12582920 | tf_op jit(solution)/shard_map/ppermute | solution.py:17
  31.2 25.8 %collective-permute-start.9 = (bf16[2,2,256,512]{3,2,1,0:T(8,128)(2,1)S(1)}, bf16[2,2,256,512]{3,2,1,0:T(8,128)(2,1)S(1)}, u32[]{:S(2)}, u32[]{:S(2)}) collective-permute-start(bf16[2,2,256,512]{3,2,1,0:T(8,128)(2,1)S(1)} %get-tuple-element.43), channel_id=1, source_target_pairs={{0,1},{1,0},{2,3},{3,2},{4,5},{5,4},{6,7},{7,6},{8,9},{9,8},{10,11... | collective-permute-start | bytes 3145736 | tf_op jit(solution)/shard_map/ppermute | solution.py:17
  33.1 7.5 %collective-permute-start.6 = (f32[2,128]{1,0:T(2,128)S(1)}, f32[2,128]{1,0:T(2,128)S(1)}, u32[]{:S(2)}, u32[]{:S(2)}) collective-permute-start(f32[2,128]{1,0:T(2,128)S(1)} %fusion.20), channel_id=1, source_target_pairs={{0,2},{1,3},{2,0},{3,1},{4,6},{5,7},{6,4},{7,5},{8,10},{9,11},{10,... | collective-permute-start | bytes 3080 | tf_op jit(solution)/shard_map/ppermute | solution.py:17
  40.4 51.7 %collective-permute-start.14 = (bf16[3,2,512,512]{3,2,1,0:T(8,128)(2,1)}, bf16[3,2,512,512]{3,2,1,0:T(8,128)(2,1)}, u32[]{:S(2)}, u32[]{:S(2)}) collective-permute-start(bf16[3,2,512,512]{3,2,1,0:T(8,128)(2,1)} %get-tuple-element.46), channel_id=1, source_target_pairs={{0,8},{8,0},{1,9},{9,1},{2,10},{10,2},{3,11},{11,3},{4,12},{12,4},... | collective-permute-start | bytes 9437192 | tf_op jit(solution)/shard_map/ppermute | solution.py:17
  40.5 56.4 %collective-permute-start.15 = (bf16[3,2,512,512]{3,2,1,0:T(8,128)(2,1)}, bf16[3,2,512,512]{3,2,1,0:T(8,128)(2,1)}, u32[]{:S(2)}, u32[]{:S(2)}) collective-permute-start(bf16[3,2,512,512]{3,2,1,0:T(8,128)(2,1)} %get-tuple-element.67), channel_id=1, source_target_pairs={{0,8},{8,0},{1,9},{9,1},{2,10},{10,2},{3,11},{11,3},{4,12},{12,4},... | collective-permute-start | bytes 9437192 | tf_op jit(solution)/shard_map/ppermute | solution.py:17
  41.0 2.0 %copy-start.1 = (bf16[4,2,512,512]{3,2,1,0:T(8,128)(2,1)}, bf16[4,2,512,512]{3,2,1,0:T(8,128)(2,1)S(1)}, u32[]{:S(2)}) copy-start(bf16[4,2,512,512]{3,2,1,0:T(8,128)(2,1)S(1)} %collective-permute-done.8.refs_0_) | copy-start | bytes 12582916
  43.1 16.5 %collective-permute-start.7 = (f32[2,128]{1,0:T(2,128)S(1)}, f32[2,128]{1,0:T(2,128)S(1)}, u32[]{:S(2)}, u32[]{:S(2)}) collective-permute-start(f32[2,128]{1,0:T(2,128)S(1)} %add.121), channel_id=1, source_target_pairs={{0,4},{1,5},{2,6},{3,7},{4,0},{5,1},{6,2},{7,3},{8,12},{9,13},{10,... | collective-permute-start | bytes 3080 | tf_op jit(solution)/shard_map/ppermute | solution.py:17
  51.1 8.1 %copy-start.7 = (f32[2,256,512]{2,1,0:T(8,128)S(1)}, f32[2,256,512]{2,1,0:T(8,128)}, u32[]{:S(2)}) copy-start(f32[2,256,512]{2,1,0:T(8,128)} %get-tuple-element.53) | copy-start | bytes 3145732
  56.9 6.1 %copy-start.3 = (bf16[256,512]{1,0:T(8,128)(2,1)S(1)}, bf16[256,512]{1,0:T(8,128)(2,1)}, u32[]{:S(2)}) copy-start(bf16[256,512]{1,0:T(8,128)(2,1)} %copy-done.2) | copy-start | bytes 786436
  57.0 6.1 %copy-start.10 = (bf16[256,512]{1,0:T(8,128)(2,1)S(1)}, bf16[256,512]{1,0:T(8,128)(2,1)}, u32[]{:S(2)}) copy-start(bf16[256,512]{1,0:T(8,128)(2,1)} %copy-done.9) | copy-start | bytes 786436
  57.0 25.3 %collective-permute-start.12 = (bf16[2,2,256,512]{3,2,1,0:T(8,128)(2,1)S(1)}, bf16[2,2,256,512]{3,2,1,0:T(8,128)(2,1)}, u32[]{:S(2)}, u32[]{:S(2)}) collective-permute-start(bf16[2,2,256,512]{3,2,1,0:T(8,128)(2,1)S(1)} %sums.10), channel_id=1, source_target_pairs={{0,1},{1,0},{2,3},{3,2},{4,5},{5,4},{6,7},{7,6},{8,9},{9,8},{10,11... | collective-permute-start | bytes 3145736 | tf_op jit(solution)/shard_map/ppermute | solution.py:17
  59.5 24.5 %collective-permute-start.13 = (bf16[2,2,256,512]{3,2,1,0:T(8,128)(2,1)S(1)}, bf16[2,2,256,512]{3,2,1,0:T(8,128)(2,1)S(1)}, u32[]{:S(2)}, u32[]{:S(2)}) collective-permute-start(bf16[2,2,256,512]{3,2,1,0:T(8,128)(2,1)S(1)} %pad_maximum_fusion), channel_id=1, source_target_pairs={{0,2},{1,3},{6,4},{7,5},{8,10},{9,11},{14,12},{15,13},{16,18},{17,... | collective-permute-start | bytes 3145736 | tf_op jit(solution)/shard_map/ppermute | solution.py:334
  62.1 2.0 %copy-start = (bf16[4,2,512,512]{3,2,1,0:T(8,128)(2,1)}, bf16[4,2,512,512]{3,2,1,0:T(8,128)(2,1)S(1)}, u32[]{:S(2)}) copy-start(bf16[4,2,512,512]{3,2,1,0:T(8,128)(2,1)S(1)} %collective-permute-done.10.refs_0_) | copy-start | bytes 12582916
  62.1 21.9 %collective-permute-start.11 = (bf16[2,2,256,512]{3,2,1,0:T(8,128)(2,1)S(1)}, bf16[2,2,256,512]{3,2,1,0:T(8,128)(2,1)S(1)}, u32[]{:S(2)}, u32[]{:S(2)}) collective-permute-start(bf16[2,2,256,512]{3,2,1,0:T(8,128)(2,1)S(1)} %pad_maximum_fusion), channel_id=1, source_target_pairs={{2,4},{3,5},{4,2},{5,3},{10,12},{11,13},{12,10},{13,11},{18,20},{1... | collective-permute-start | bytes 3145736 | tf_op jit(solution)/shard_map/ppermute | solution.py:335
  68.8 16.9 %copy-start.11 = (f32[2,256,512]{2,1,0:T(8,128)S(1)}, f32[2,256,512]{2,1,0:T(8,128)}, u32[]{:S(2)}) copy-start(f32[2,256,512]{2,1,0:T(8,128)} %get-tuple-element.62) | copy-start | bytes 3145732
  82.3 24.3 %collective-permute-start.16 = (bf16[2,2,256,512]{3,2,1,0:T(8,128)(2,1)S(1)}, bf16[2,2,256,512]{3,2,1,0:T(8,128)(2,1)S(1)}, u32[]{:S(2)}, u32[]{:S(2)}) collective-permute-start(bf16[2,2,256,512]{3,2,1,0:T(8,128)(2,1)S(1)} %sums.12), channel_id=1, source_target_pairs={{0,1},{1,0},{2,3},{3,2},{4,5},{5,4},{6,7},{7,6},{8,9},{9,8},{10,11... | collective-permute-start | bytes 3145736 | tf_op jit(solution)/shard_map/ppermute | solution.py:17
  84.0 12.9 %copy-start.4 = (bf16[2,2,256,512]{3,2,1,0:T(8,128)(2,1)}, bf16[2,2,256,512]{3,2,1,0:T(8,128)(2,1)S(1)}, u32[]{:S(2)}) copy-start(bf16[2,2,256,512]{3,2,1,0:T(8,128)(2,1)S(1)} %collective-permute-done.11) | copy-start | bytes 3145732
  87.8 30.3 %collective-permute-start.17 = (bf16[2,256,512]{2,1,0:T(8,128)(2,1)}, bf16[2,256,512]{2,1,0:T(8,128)(2,1)}, u32[]{:S(2)}, u32[]{:S(2)}) collective-permute-start(bf16[2,256,512]{2,1,0:T(8,128)(2,1)} %fusion.8), channel_id=1, source_target_pairs={{0,2},{1,3},{2,0},{3,1},{4,6},{5,7},{6,4},{7,5},{8,10},{9,11},{10,... | collective-permute-start | bytes 1572872 | tf_op jit(solution)/shard_map/ppermute | solution.py:17
  91.3 26.8 %collective-permute-start.18 = (bf16[2,256,512]{2,1,0:T(8,128)(2,1)S(1)}, bf16[2,256,512]{2,1,0:T(8,128)(2,1)}, u32[]{:S(2)}, u32[]{:S(2)}) collective-permute-start(bf16[2,256,512]{2,1,0:T(8,128)(2,1)S(1)} %fusion.12), channel_id=1, source_target_pairs={{0,4},{1,5},{2,6},{3,7},{4,0},{5,1},{6,2},{7,3},{8,12},{9,13},{10,... | collective-permute-start | bytes 1572872 | tf_op jit(solution)/shard_map/ppermute | solution.py:17
  97.0 12.1 %copy-start.6 = (f32[2,256,512]{2,1,0:T(8,128)S(1)}, f32[2,256,512]{2,1,0:T(8,128)}, u32[]{:S(2)}) copy-start(f32[2,256,512]{2,1,0:T(8,128)} %get-tuple-element.70) | copy-start | bytes 3145732
  106.6 28.9 %collective-permute-start.19 = (bf16[2,2,256,512]{3,2,1,0:T(8,128)(2,1)S(1)}, bf16[2,2,256,512]{3,2,1,0:T(8,128)(2,1)}, u32[]{:S(2)}, u32[]{:S(2)}) collective-permute-start(bf16[2,2,256,512]{3,2,1,0:T(8,128)(2,1)S(1)} %sums.14), channel_id=1, source_target_pairs={{0,1},{1,0},{2,3},{3,2},{4,5},{5,4},{6,7},{7,6},{8,9},{9,8},{10,11... | collective-permute-start | bytes 3145736 | tf_op jit(solution)/shard_map/ppermute | solution.py:17
  110.1 25.5 %collective-permute-start.20 = (bf16[2,256,512]{2,1,0:T(8,128)(2,1)}, bf16[2,256,512]{2,1,0:T(8,128)(2,1)S(1)}, u32[]{:S(2)}, u32[]{:S(2)}) collective-permute-start(bf16[2,256,512]{2,1,0:T(8,128)(2,1)} %fusion.4), channel_id=1, source_target_pairs={{0,2},{1,3},{2,0},{3,1},{4,6},{5,7},{6,4},{7,5},{8,10},{9,11},{10,... | collective-permute-start | bytes 1572872 | tf_op jit(solution)/shard_map/ppermute | solution.py:17
  110.1 25.5 %collective-permute-start.21 = (bf16[2,256,512]{2,1,0:T(8,128)(2,1)}, bf16[2,256,512]{2,1,0:T(8,128)(2,1)S(1)}, u32[]{:S(2)}, u32[]{:S(2)}) collective-permute-start(bf16[2,256,512]{2,1,0:T(8,128)(2,1)} %fusion.6), channel_id=1, source_target_pairs={{0,4},{1,5},{2,6},{3,7},{4,0},{5,1},{6,2},{7,3},{8,12},{9,13},{10,... | collective-permute-start | bytes 1572872 | tf_op jit(solution)/shard_map/ppermute | solution.py:17
  112.0 6.1 %copy-start.5 = (bf16[2,2,256,512]{3,2,1,0:T(8,128)(2,1)S(1)}, bf16[2,2,256,512]{3,2,1,0:T(8,128)(2,1)}, u32[]{:S(2)}) copy-start(bf16[2,2,256,512]{3,2,1,0:T(8,128)(2,1)} %copy-done.4) | copy-start | bytes 3145732
  116.8 18.7 %copy-start.12 = (f32[2,256,512]{2,1,0:T(8,128)S(1)}, f32[2,256,512]{2,1,0:T(8,128)}, u32[]{:S(2)}) copy-start(f32[2,256,512]{2,1,0:T(8,128)} %get-tuple-element.76) | copy-start | bytes 3145732
  137.7 1.6 %collective-permute-start.22 = (bf16[128,1024]{1,0:T(8,128)(2,1)S(1)}, bf16[128,1024]{1,0:T(8,128)(2,1)S(1)}, u32[]{:S(2)}, u32[]{:S(2)}) collective-permute-start(bf16[128,1024]{1,0:T(8,128)(2,1)S(1)} %fusion.17), channel_id=1, source_target_pairs={{0,8},{8,0},{1,9},{9,1},{2,10},{10,2},{3,11},{11,3},{4,12},{12,4},... | collective-permute-start | bytes 786440 | tf_op jit(solution)/shard_map/ppermute | solution.py:17

commit v6 on v5

--- a/solution.py
+++ b/solution.py
@@ -9,7 +9,7 @@
 
 EPS = 1e-05
 LANES = 128
-VMEM_LIMIT = 52 * 1024 * 1024
+VMEM_LIMIT = 49 * 1024 * 1024
 
 
 def exchange(value, axis, bit):
@@ -21,23 +21,11 @@
     return lax.optimization_barrier((value, *earlier))[0]
 
 
-def split_kernel(own_ref, other_ref, gains_ref, out_ref):
-    rows, depth = own_ref.shape
-    for i, ref in enumerate((own_ref, other_ref)):
-        value = ref[...].astype(jnp.float32) * gains_ref[i : i + 1, :]
-        high = value.astype(jnp.bfloat16)
-        columns = slice(i * depth, (i + 1) * depth)
-        out_ref[:rows, columns] = high
-        out_ref[rows:, columns] = (value - high.astype(jnp.float32)).astype(jnp.bfloat16)
-
-
 def split(own, other, gains):
-    rows, depth = own.shape
-    return pl.pallas_call(
-        split_kernel,
-        out_shape=jax.ShapeDtypeStruct((2 * rows, 2 * depth), jnp.bfloat16),
-        name="split",
-    )(own, other, gains)
+    values = [part.astype(jnp.float32) * gains[i : i + 1] for i, part in enumerate((own, other))]
+    value = jnp.concatenate(values, axis=1)
+    high = lax.reduce_precision(value, exponent_bits=8, mantissa_bits=7)
+    return jnp.concatenate([high, value - high], axis=0).astype(jnp.bfloat16)
 
 
 def cut_copies(groups, lanes, at_ref, gate_ref, up_ref, out_refs, held, in_sems, out_sems):
@@ -242,13 +230,13 @@
         raw.append(lax.ppermute(piece, ("wide", "tensor"), moves))
     values = tokens.astype(jnp.float32)
     squares = jnp.sum(values * values, axis=-1).reshape(1, rows)
+    squares = squares + exchange(squares, "tensor", 1)
     squares_other = exchange(squares, "wide", 1)
     squares = jnp.where(
         half == 0,
         jnp.concatenate([squares, squares_other], axis=0),
         jnp.concatenate([squares_other, squares], axis=0),
     )
-    squares = squares + exchange(squares, "tensor", 1)
     raw = jnp.where(shard % 2 == 1, jnp.concatenate(raw[::-1]), jnp.concatenate(raw))
     masks = jnp.concatenate(
         [
@@ -344,8 +332,8 @@
         second_b = exchange(add(near_b[0], pair_b[0], wide(relay[1]) * scales), "tensor", 4)
         first_b = exchange(add(near_b[1], pair_b[1]), "tensor", 2)
         own = chip_sums(normed, [(0, 0, 0), (0, 0, 1)], stacked=False)
-        early = emit(in_turn(own[0]) + wide(first_a) + wide(second_a) + wide(across[0]) * scales)
-        hidden = [finish(early, pair_0[0]), finish(own[1], pair_0[1], first_b, second_b, wide(across[1]) * scales)]
+        early = emit(in_turn(own[0]) + wide(first_a) + wide(across[0]) * scales)
+        hidden = [finish(early, pair_0[0], second_a), finish(own[1], pair_0[1], first_b, second_b, wide(across[1]) * scales)]
         return jnp.concatenate(give(jnp.concatenate(hidden, axis=1)), axis=1)
     received = []
     normed, _ = normalise(squares)

time: 142 us -> 137 us (0.965); the launches traced: 140 us -> 137 us
  Pallas kernels: 56.5 us -> 48.8 us
  starting transfers between devices: 30.9 us -> 37 us
  waiting for transfers between devices: 35.4 us -> 40.3 us
  local copies, waits for them, and re-layouts: 4.32 us -> 0.82 us
  other arithmetic: 12.7 us -> 9.72 us
    ppermute x19, starting transfers between devices: 23.7 us -> 30.3 us  [exchange(): return lax.ppermute(value, axis, [(i, i ^ bit) for i in range(size)])]
    pallas_call x8, Pallas kernels: 45.2 us -> 39.7 us  [sums(): pl.pallas_call(functools.partial(sums_kernel, places, lanes, side, stacke...]
    unnamed x26 -> x6, local copies, waits for them, and re-layouts: 3.52 us -> 0.02 us
    ppermute x19, waiting for transfers between devices: 35.4 us -> 38.8 us  [exchange(): return lax.ppermute(value, axis, [(i, i ^ bit) for i in range(size)])]
    convert_element_type x6, other arithmetic: 6.05 us -> 2.75 us  [add(): return emit(total.astype(jnp.bfloat16))]
    ppermute x2, starting transfers between devices: 3.68 us -> 0.76 us  [local(): raw.append(lax.ppermute(piece, ('wide', 'tensor'), moves))]
    pallas_call x1 -> x0, Pallas kernels: 2.23 us -> none  [split(): pl.pallas_call(split_kernel, out_shape=jax.ShapeDtypeStruct((2 * rows, 2...]
    ppermute x1, waiting for transfers between devices: 0.01 us -> 1.43 us  [local(): relay = lax.ppermute(third, 'tensor', by_neighbour)]
  transfers between devices with their start and end apart: 23 -> 23, of which waited for: 7 -> 9; matrix products, arithmetic and copies ran while one was open for 7% -> 5% of each run, Pallas kernels for 30% -> 27%
where the time goes in v6:
time: 137 us
  Pallas kernels  48.8 us (36%)
  waiting for transfers between devices  40.3 us (29%)
  starting transfers between devices  37 us (27%)
  other arithmetic  9.72 us (7%)
    pallas_call x8, Pallas kernels, sums(): pl.pallas_call(functools.partial(sums_kernel, places, lanes, side, stacke...  39.7 us
    ppermute x19, waiting for transfers between devices, exchange(): return lax.ppermute(value, axis, [(i, i ^ bit) for i in range(size)])  38.8 us
    ppermute x19, starting transfers between devices, exchange(): return lax.ppermute(value, axis, [(i, i ^ bit) for i in range(size)])  30.3 us
    pallas_call x2, Pallas kernels, cut(): pl.pallas_call(functools.partial(cut_kernel, groups, lanes), in_specs=[pl...  9.07 us
    ppermute x1, starting transfers between devices, local(): relay = lax.ppermute(third, 'tensor', by_neighbour)  3.77 us
    convert_element_type x6, other arithmetic, add(): return emit(total.astype(jnp.bfloat16))  2.75 us
  transfers between devices with their start and end apart: 23, of which 9 were waited for; matrix products, arithmetic and copies ran while one was open for 5% of the time, Pallas kernels for 27%

profile of v6, /device:TPU:0, one launch (start us, length us, event | category | flops | bytes accessed | tf_op | source)
XLA Modules:
  0.0 137.0 jit_solution(13466073292059381570)
XLA Ops:
  0.0 0.1 pad_add_fusion.at_ref.partner_ref
  0.1 3.0 %cut.2 = bf16[2,2,512,512]{3,2,1,0:T(8,128)(2,1)} custom-call(s32[3]{0:T(128)S(1)} %pad_add_fusion.at_ref.partner_ref, bf16[512,16384]{1,0:T(8,128)(2,1)} %gate_ref.19, bf16[512,16384]{1,0:T(8,128)(2,1)} %up_ref.19), custom_call_target="tpu_custom_call" | custom-call | tf_op jit(solution)/shard_map/cut/pallas_call | solution.py:71
  3.1 0.5 collective-permute-start.5
  3.6 0.1 multiply_reduce_fusion
  3.7 2.6 %collective-permute-start.2 = (f32[1,128]{1,0:T(1,128)S(1)}, f32[1,128]{1,0:T(1,128)S(1)}, u32[]{:S(2)}, u32[]{:S(2)}) collective-permute-start(f32[1,128]{1,0:T(1,128)S(1)} %bitcast.87), channel_id=1, source_target_pairs={{0,1},{1,0},{2,3},{3,2},{4,5},{5,4},{6,7},{7,6},{8,9},{9,8},{10,11... | collective-permute-start | bytes 1544 | tf_op jit(solution)/shard_map/ppermute | solution.py:17
  6.4 0.1 collective-permute-start
  6.5 0.7 collective-permute-start.1
  7.2 0.1 pad_add_fusion.1.at_ref
  7.3 0.8 fusion.23
  8.0 0.8 dynamic-slice_convert_fusion.1
  8.9 3.5 %collective-permute-start.3 = (f32[1,128]{1,0:T(1,128)S(1)}, f32[1,128]{1,0:T(1,128)S(1)}, u32[]{:S(2)}, u32[]{:S(2)}) collective-permute-start(f32[1,128]{1,0:T(1,128)S(1)} %bitcast_add_fusion), channel_id=1, source_target_pairs={{0,8},{8,0},{1,9},{9,1},{2,10},{10,2},{3,11},{11,3},{4,12},{12,4},... | collective-permute-start | bytes 1544 | tf_op jit(solution)/shard_map/ppermute | solution.py:17
  12.3 0.1 maximum_select_fusion
  12.4 1.9 %collective-permute-start.4 = (bf16[256,512]{1,0:T(8,128)(2,1)S(1)}, bf16[256,512]{1,0:T(8,128)(2,1)S(1)}, u32[]{:S(2)}, u32[]{:S(2)}) collective-permute-start(bf16[256,512]{1,0:T(8,128)(2,1)S(1)} %maximum_select_fusion), channel_id=1, source_target_pairs={{0,8},{8,0},{1,9},{9,1},{2,10},{10,2},{3,11},{11,3},{4,12},{12,4},... | collective-permute-start | bytes 786440 | tf_op jit(solution)/shard_map/ppermute | solution.py:17
  14.4 1.1 collective-permute-done.4
  15.5 0.2 reduce-precision_convert_fusion
  15.7 0.1 pad_maximum_fusion.1.x_ref
  15.8 9.1 %sums.8 = (bf16[2,2,256,512]{3,2,1,0:T(8,128)(2,1)S(1)}, bf16[4,2,512,512]{3,2,1,0:T(8,128)(2,1)}, bf16[4,2,512,512]{3,2,1,0:T(8,128)(2,1)}) custom-call(s32[3]{0:T(128)S(1)} %pad_add_fusion.1.at_ref, s32[3]{0:T(128)S(1)} %pad_add_fusion.at_ref.partner_ref, bf16[512,1024]{1,0:T(8,128)(2,1)S(1)} %pad_maximum_fusion.1.x_ref, bf16[512,16384]{1,0:T(8,128)(2,1)} %gate_ref.19, ...), custom_call_target="tpu_custom_call" | custom-call | tf_op jit(solution)/shard_map/sums/pallas_call | solution.py:154
  24.9 0.4 collective-permute-start.8
  25.3 0.1 collective-permute-start.10
  25.4 2.9 %collective-permute-start.9 = (bf16[2,2,256,512]{3,2,1,0:T(8,128)(2,1)S(1)}, bf16[2,2,256,512]{3,2,1,0:T(8,128)(2,1)S(1)}, u32[]{:S(2)}, u32[]{:S(2)}) collective-permute-start(bf16[2,2,256,512]{3,2,1,0:T(8,128)(2,1)S(1)} %get-tuple-element.43), channel_id=1, source_target_pairs={{0,1},{1,0},{2,3},{3,2},{4,5},{5,4},{6,7},{7,6},{8,9},{9,8},{10,11... | collective-permute-start | bytes 3145736 | tf_op jit(solution)/shard_map/ppermute | solution.py:17
  28.4 1.8 %collective-permute-start.6 = (f32[2,128]{1,0:T(2,128)S(1)}, f32[2,128]{1,0:T(2,128)S(1)}, u32[]{:S(2)}, u32[]{:S(2)}) collective-permute-start(f32[2,128]{1,0:T(2,128)S(1)} %maximum_select_fusion.1), channel_id=1, source_target_pairs={{0,2},{1,3},{2,0},{3,1},{4,6},{5,7},{6,4},{7,5},{8,10},{9,11},{10,... | collective-permute-start | bytes 3080 | tf_op jit(solution)/shard_map/ppermute | solution.py:17
  30.1 6.1 %cut.3 = (bf16[3,2,512,512]{3,2,1,0:T(8,128)(2,1)}, bf16[3,2,512,512]{3,2,1,0:T(8,128)(2,1)}) custom-call(s32[3]{0:T(128)S(1)} %pad_add_fusion.at_ref.partner_ref, bf16[512,16384]{1,0:T(8,128)(2,1)} %gate_ref.19, bf16[512,16384]{1,0:T(8,128)(2,1)} %up_ref.19), custom_call_target="tpu_custom_call" | custom-call | tf_op jit(solution)/shard_map/cut/pallas_call | solution.py:71
  36.2 0.1 collective-permute-start.14
  36.3 0.5 collective-permute-start.15
  36.8 0.3 collective-permute-done.8.refs_0_
  37.0 3.9 %collective-permute-start.7 = (f32[2,128]{1,0:T(2,128)S(1)}, f32[2,128]{1,0:T(2,128)S(1)}, u32[]{:S(2)}, u32[]{:S(2)}) collective-permute-start(f32[2,128]{1,0:T(2,128)S(1)} %add.121), channel_id=1, source_target_pairs={{0,4},{1,5},{2,6},{3,7},{4,0},{5,1},{6,2},{7,3},{8,12},{9,13},{10,... | collective-permute-start | bytes 3080 | tf_op jit(solution)/shard_map/ppermute | solution.py:17
  40.9 5.1 %sums.9 = (f32[2,256,512]{2,1,0:T(8,128)S(1)}, f32[2,256,512]{2,1,0:T(8,128)S(1)}) custom-call(s32[3]{0:T(128)S(1)} %pad_add_fusion.1.at_ref, s32[3]{0:T(128)S(1)} %pad_add_fusion.at_ref.partner_ref, bf16[512,1024]{1,0:T(8,128)(2,1)S(1)} %pad_maximum_fusion.1.x_ref, bf16[512,16384]{1,0:T(8,128)(2,1)} %gate_ref.19, bf16[512,16384]{1,0:T(8,128)(2,1)} %up_ref.19, ...), custom_call_target="tpu_custom_call" | custom-call | tf_op jit(solution)/shard_map/sums/pallas_call | solution.py:154
  46.0 5.0 %sums.10 = bf16[2,2,256,512]{3,2,1,0:T(8,128)(2,1)S(1)} custom-call(s32[3]{0:T(128)S(1)} %pad_add_fusion.1.at_ref, s32[3]{0:T(128)S(1)} %pad_add_fusion.at_ref.partner_ref, bf16[512,1024]{1,0:T(8,128)(2,1)S(1)} %pad_maximum_fusion.1.x_ref, bf16[512,16384]{1,0:T(8,128)(2,1)} %gate_ref.19, bf16[512,16384]{1,0:T(8,128)(2,1)} %up_ref.19, ...), custom_call_target="tpu_custom_call" | custom-call | tf_op jit(solution)/shard_map/sums/pallas_call | solution.py:154
  51.0 1.0 collective-permute-done.9
  52.0 1.7 %collective-permute-start.12 = (bf16[2,2,256,512]{3,2,1,0:T(8,128)(2,1)S(1)}, bf16[2,2,256,512]{3,2,1,0:T(8,128)(2,1)S(1)}, u32[]{:S(2)}, u32[]{:S(2)}) collective-permute-start(bf16[2,2,256,512]{3,2,1,0:T(8,128)(2,1)S(1)} %sums.10), channel_id=1, source_target_pairs={{0,1},{1,0},{2,3},{3,2},{4,5},{5,4},{6,7},{7,6},{8,9},{9,8},{10,11... | collective-permute-start | bytes 3145736 | tf_op jit(solution)/shard_map/ppermute | solution.py:17
  53.8 0.2 fusion.12
  54.0 0.2 fusion.11
  54.1 0.1 pad_maximum_fusion.2
  54.3 3.8 %collective-permute-start.13 = (bf16[2,2,256,512]{3,2,1,0:T(8,128)(2,1)S(1)}, bf16[2,2,256,512]{3,2,1,0:T(8,128)(2,1)S(1)}, u32[]{:S(2)}, u32[]{:S(2)}) collective-permute-start(bf16[2,2,256,512]{3,2,1,0:T(8,128)(2,1)S(1)} %pad_maximum_fusion.2), channel_id=1, source_target_pairs={{0,2},{1,3},{6,4},{7,5},{8,10},{9,11},{14,12},{15,13},{16,18},{17,... | collective-permute-start | bytes 3145736 | tf_op jit(solution)/shard_map/ppermute | solution.py:322
  58.0 2.1 %collective-permute-start.11 = (bf16[2,2,256,512]{3,2,1,0:T(8,128)(2,1)S(1)}, bf16[2,2,256,512]{3,2,1,0:T(8,128)(2,1)}, u32[]{:S(2)}, u32[]{:S(2)}) collective-permute-start(bf16[2,2,256,512]{3,2,1,0:T(8,128)(2,1)S(1)} %pad_maximum_fusion.2), channel_id=1, source_target_pairs={{2,4},{3,5},{4,2},{5,3},{10,12},{11,13},{12,10},{13,11},{18,20},{1... | collective-permute-start | bytes 3145736 | tf_op jit(solution)/shard_map/ppermute | solution.py:323
  60.2 0.2 multiply_convert_fusion
  60.4 4.1 %sums.11 = (f32[2,256,512]{2,1,0:T(8,128)S(1)}, f32[2,256,512]{2,1,0:T(8,128)S(1)}) custom-call(s32[3]{0:T(128)S(1)} %pad_add_fusion.1.at_ref, s32[3]{0:T(128)S(1)} %pad_add_fusion.at_ref.partner_ref, bf16[256,1024]{1,0:T(8,128)(2,1)S(1)} %pad_maximum_fusion.3.x_ref, bf16[512,16384]{1,0:T(8,128)(2,1)} %gate_ref.19, bf16[512,16384]{1,0:T(8,128)(2,1)} %up_ref.19, ...), custom_call_target="tpu_custom_call" | custom-call | tf_op jit(solution)/shard_map/sums/pallas_call | solution.py:154
  64.5 4.0 %sums.12 = bf16[2,2,256,512]{3,2,1,0:T(8,128)(2,1)S(1)} custom-call(s32[3]{0:T(128)S(1)} %pad_add_fusion.1.at_ref, s32[3]{0:T(128)S(1)} %pad_add_fusion.at_ref.partner_ref, bf16[256,1024]{1,0:T(8,128)(2,1)S(1)} %pad_maximum_fusion.3.x_ref, bf16[512,16384]{1,0:T(8,128)(2,1)} %gate_ref.19, bf16[512,16384]{1,0:T(8,128)(2,1)} %up_ref.19, ...), custom_call_target="tpu_custom_call" | custom-call | tf_op jit(solution)/shard_map/sums/pallas_call | solution.py:154
  68.6 8.3 %collective-permute-done.12 = bf16[2,2,256,512]{3,2,1,0:T(8,128)(2,1)S(1)} collective-permute-done((bf16[2,2,256,512]{3,2,1,0:T(8,128)(2,1)S(1)}, bf16[2,2,256,512]{3,2,1,0:T(8,128)(2,1)S(1)}, u32[]{:S(2)}, u32[]{:S(2)}) %collective-permute-start.12) | collective-permute-done | bytes 1048608 | tf_op jit(solution)/shard_map/ppermute | solution.py:17
  76.9 1.5 %collective-permute-start.16 = (bf16[2,2,256,512]{3,2,1,0:T(8,128)(2,1)S(1)}, bf16[2,2,256,512]{3,2,1,0:T(8,128)(2,1)S(1)}, u32[]{:S(2)}, u32[]{:S(2)}) collective-permute-start(bf16[2,2,256,512]{3,2,1,0:T(8,128)(2,1)S(1)} %sums.12), channel_id=1, source_target_pairs={{0,1},{1,0},{2,3},{3,2},{4,5},{5,4},{6,7},{7,6},{8,9},{9,8},{10,11... | collective-permute-start | bytes 3145736 | tf_op jit(solution)/shard_map/ppermute | solution.py:17
  78.4 1.4 %collective-permute-done.13 = bf16[2,2,256,512]{3,2,1,0:T(8,128)(2,1)S(1)} collective-permute-done((bf16[2,2,256,512]{3,2,1,0:T(8,128)(2,1)S(1)}, bf16[2,2,256,512]{3,2,1,0:T(8,128)(2,1)S(1)}, u32[]{:S(2)}, u32[]{:S(2)}) %collective-permute-start.13) | collective-permute-done | bytes 1048608 | tf_op jit(solution)/shard_map/ppermute | solution.py:322
  79.8 0.2 fusion.14
  80.1 1.0 fusion.10
  81.1 3.9 %collective-permute-start.17 = (bf16[2,256,512]{2,1,0:T(8,128)(2,1)}, bf16[2,256,512]{2,1,0:T(8,128)(2,1)}, u32[]{:S(2)}, u32[]{:S(2)}) collective-permute-start(bf16[2,256,512]{2,1,0:T(8,128)(2,1)} %fusion.10), channel_id=1, source_target_pairs={{0,2},{1,3},{2,0},{3,1},{4,6},{5,7},{6,4},{7,5},{8,10},{9,11},{10,... | collective-permute-start | bytes 1572872 | tf_op jit(solution)/shard_map/ppermute | solution.py:17
  85.0 0.2 collective-permute-start.19
  85.2 4.1 %sums.13 = (f32[2,256,512]{2,1,0:T(8,128)S(1)}, f32[2,256,512]{2,1,0:T(8,128)S(1)}) custom-call(s32[3]{0:T(128)S(1)} %pad_add_fusion.1.at_ref, s32[3]{0:T(128)S(1)} %pad_add_fusion.at_ref.partner_ref, bf16[256,1024]{1,0:T(8,128)(2,1)S(1)} %pad_maximum_fusion.3.x_ref, bf16[512,16384]{1,0:T(8,128)(2,1)} %gate_ref.19, bf16[512,16384]{1,0:T(8,128)(2,1)} %up_ref.19, ...), custom_call_target="tpu_custom_call" | custom-call | tf_op jit(solution)/shard_map/sums/pallas_call | solution.py:154
  89.3 4.3 %sums.14 = bf16[2,2,256,512]{3,2,1,0:T(8,128)(2,1)S(1)} custom-call(s32[3]{0:T(128)S(1)} %pad_add_fusion.1.at_ref, s32[3]{0:T(128)S(1)} %pad_add_fusion.at_ref.partner_ref, bf16[256,1024]{1,0:T(8,128)(2,1)S(1)} %pad_maximum_fusion.3.x_ref, bf16[512,16384]{1,0:T(8,128)(2,1)} %gate_ref.19, bf16[512,16384]{1,0:T(8,128)(2,1)} %up_ref.19, ...), custom_call_target="tpu_custom_call" | custom-call | tf_op jit(solution)/shard_map/sums/pallas_call | solution.py:154
  93.6 7.3 %collective-permute-done.16 = bf16[2,2,256,512]{3,2,1,0:T(8,128)(2,1)S(1)} collective-permute-done((bf16[2,2,256,512]{3,2,1,0:T(8,128)(2,1)S(1)}, bf16[2,2,256,512]{3,2,1,0:T(8,128)(2,1)S(1)}, u32[]{:S(2)}, u32[]{:S(2)}) %collective-permute-start.16) | collective-permute-done | bytes 1048608 | tf_op jit(solution)/shard_map/ppermute | solution.py:17
  100.9 1.2 collective-permute-start.18
  102.1 1.0 fusion.8
  103.1 0.2 fusion.6
  103.3 2.1 %collective-permute-start.20 = (bf16[2,256,512]{2,1,0:T(8,128)(2,1)S(1)}, bf16[2,256,512]{2,1,0:T(8,128)(2,1)S(1)}, u32[]{:S(2)}, u32[]{:S(2)}) collective-permute-start(bf16[2,256,512]{2,1,0:T(8,128)(2,1)S(1)} %fusion.6), channel_id=1, source_target_pairs={{0,2},{1,3},{2,0},{3,1},{4,6},{5,7},{6,4},{7,5},{8,10},{9,11},{10,... | collective-permute-start | bytes 1572872 | tf_op jit(solution)/shard_map/ppermute | solution.py:17
  105.4 1.5 %collective-permute-start.21 = (bf16[2,256,512]{2,1,0:T(8,128)(2,1)}, bf16[2,256,512]{2,1,0:T(8,128)(2,1)}, u32[]{:S(2)}, u32[]{:S(2)}) collective-permute-start(bf16[2,256,512]{2,1,0:T(8,128)(2,1)} %fusion.8), channel_id=1, source_target_pairs={{0,4},{1,5},{2,6},{3,7},{4,0},{5,1},{6,2},{7,3},{8,12},{9,13},{10,... | collective-permute-start | bytes 1572872 | tf_op jit(solution)/shard_map/ppermute | solution.py:17
  106.9 4.1 %sums.15 = (f32[2,256,512]{2,1,0:T(8,128)S(1)}, f32[2,256,512]{2,1,0:T(8,128)S(1)}) custom-call(s32[3]{0:T(128)S(1)} %pad_add_fusion.1.at_ref, s32[3]{0:T(128)S(1)} %pad_add_fusion.at_ref.partner_ref, bf16[256,1024]{1,0:T(8,128)(2,1)S(1)} %pad_maximum_fusion.3.x_ref, bf16[512,16384]{1,0:T(8,128)(2,1)} %gate_ref.19, bf16[512,16384]{1,0:T(8,128)(2,1)} %up_ref.19, ...), custom_call_target="tpu_custom_call" | custom-call | tf_op jit(solution)/shard_map/sums/pallas_call | solution.py:154
  111.0 1.4 %fusion.5 = f32[2,256,512]{2,1,0:T(8,128)S(1)} fusion(f32[2,256,512]{2,1,0:T(8,128)S(1)} %get-tuple-element.72, bf16[2,256,512]{2,1,0:T(8,128)(2,1)} %collective-permute-done.17, bf16[2,2,256,512]{3,2,1,0:T(8,128)(2,1)} %collective-permute-done.11, f32[256]{0:T(256)S(1)} %rsqrt_bitcast_fusion), kind=kLoop, calls=%fused_computation.14 | loop fusion | flops 1310720 | bytes 3146752 | tf_op jit(solution)/shard_map/add | solution.py:335
  112.4 16.0 %collective-permute-done.20 = bf16[2,256,512]{2,1,0:T(8,128)(2,1)S(1)} collective-permute-done((bf16[2,256,512]{2,1,0:T(8,128)(2,1)S(1)}, bf16[2,256,512]{2,1,0:T(8,128)(2,1)S(1)}, u32[]{:S(2)}, u32[]{:S(2)}) %collective-permute-start.20) | collective-permute-done | bytes 524320 | tf_op jit(solution)/shard_map/ppermute | solution.py:17
  128.4 3.3 %collective-permute-done.21 = bf16[2,256,512]{2,1,0:T(8,128)(2,1)} collective-permute-done((bf16[2,256,512]{2,1,0:T(8,128)(2,1)}, bf16[2,256,512]{2,1,0:T(8,128)(2,1)}, u32[]{:S(2)}, u32[]{:S(2)}) %collective-permute-start.21) | collective-permute-done | bytes 524320 | tf_op jit(solution)/shard_map/ppermute | solution.py:17
  131.7 2.3 %fusion.1 = (f32[2,256,512]{2,1,0:T(8,128)S(1)}, f32[2,256,512]{2,1,0:T(8,128)S(1)}) fusion(f32[2,256,512]{2,1,0:T(8,128)S(1)} %get-tuple-element.76, bf16[2,256,512]{2,1,0:T(8,128)(2,1)} %collective-permute-done.21, bf16[2,256,512]{2,1,0:T(8,128)(2,1)S(1)} %collective-permute-done.20, bf16[2,2,256,512]{3,2,1,0:T(8,128)(2,1)} %collective-permute-done.11, ...), kind=kLoop, calls=%fused_computation.7 | loop fusion | flops 3407872 | bytes 7341056 | tf_op jit(solution)/shard_map/add | solution.py:284
  134.1 0.2 fusion.18
  134.3 0.2 fusion.20
  134.5 0.1 collective-permute-start.22
  134.5 1.5 %collective-permute-done.22 = bf16[128,1024]{1,0:T(8,128)(2,1)S(1)} collective-permute-done((bf16[128,1024]{1,0:T(8,128)(2,1)S(1)}, bf16[128,1024]{1,0:T(8,128)(2,1)S(1)}, u32[]{:S(2)}, u32[]{:S(2)}) %collective-permute-start.22) | collective-permute-done | bytes 262176 | tf_op jit(solution)/shard_map/ppermute | solution.py:17
  136.1 0.1 broadcast_select_fusion.1
  136.2 0.8 pad_maximum_fusion.4
  (30 shorter events, 0.3 us)
Async XLA Ops:
  0.1 3.5 %copy-start.2 = (bf16[128,1024]{1,0:T(8,128)(2,1)S(1)}, bf16[128,1024]{1,0:T(8,128)(2,1)}, u32[]{:S(2)}) copy-start(bf16[128,1024]{1,0:T(8,128)(2,1)} %param.6) | copy-start | bytes 786436
  3.1 12.7 %collective-permute-start.5 = (bf16[2,2,512,512]{3,2,1,0:T(8,128)(2,1)}, bf16[2,2,512,512]{3,2,1,0:T(8,128)(2,1)S(1)}, u32[]{:S(2)}, u32[]{:S(2)}) collective-permute-start(bf16[2,2,512,512]{3,2,1,0:T(8,128)(2,1)} %cut.2), channel_id=1, source_target_pairs={{0,8},{8,0},{1,9},{9,1},{2,10},{10,2},{3,11},{11,3},{4,12},{12,4},... | collective-permute-start | bytes 6291464 | tf_op jit(solution)/shard_map/ppermute | solution.py:17
  3.7 5.1 %collective-permute-start.2 = (f32[1,128]{1,0:T(1,128)S(1)}, f32[1,128]{1,0:T(1,128)S(1)}, u32[]{:S(2)}, u32[]{:S(2)}) collective-permute-start(f32[1,128]{1,0:T(1,128)S(1)} %bitcast.87), channel_id=1, source_target_pairs={{0,1},{1,0},{2,3},{3,2},{4,5},{5,4},{6,7},{7,6},{8,9},{9,8},{10,11... | collective-permute-start | bytes 1544 | tf_op jit(solution)/shard_map/ppermute | solution.py:17
  6.4 6.0 %collective-permute-start = (bf16[128,512]{1,0:T(8,128)(2,1)S(1)}, bf16[128,512]{1,0:T(8,128)(2,1)S(1)}, u32[]{:S(2)}, u32[]{:S(2)}) collective-permute-start(bf16[128,512]{1,0:T(8,128)(2,1)S(1)} %get-tuple-element.83), channel_id=1, source_target_pairs={{8,0},{0,1},{9,2},{1,3},{10,4},{2,5},{11,6},{3,7},{12,8},{4,9},{13... | collective-permute-start | bytes 393224 | tf_op jit(solution)/shard_map/ppermute | solution.py:230
  6.5 5.9 %collective-permute-start.1 = (bf16[128,512]{1,0:T(8,128)(2,1)S(1)}, bf16[128,512]{1,0:T(8,128)(2,1)S(1)}, u32[]{:S(2)}, u32[]{:S(2)}) collective-permute-start(bf16[128,512]{1,0:T(8,128)(2,1)S(1)} %get-tuple-element.84), channel_id=1, source_target_pairs={{0,0},{8,1},{1,2},{9,3},{2,4},{10,5},{3,6},{11,7},{4,8},{12,9},{5,... | collective-permute-start | bytes 393224 | tf_op jit(solution)/shard_map/ppermute | solution.py:230
  8.9 5.4 %collective-permute-start.3 = (f32[1,128]{1,0:T(1,128)S(1)}, f32[1,128]{1,0:T(1,128)S(1)}, u32[]{:S(2)}, u32[]{:S(2)}) collective-permute-start(f32[1,128]{1,0:T(1,128)S(1)} %bitcast_add_fusion), channel_id=1, source_target_pairs={{0,8},{8,0},{1,9},{9,1},{2,10},{10,2},{3,11},{11,3},{4,12},{12,4},... | collective-permute-start | bytes 1544 | tf_op jit(solution)/shard_map/ppermute | solution.py:17
  12.4 3.0 %collective-permute-start.4 = (bf16[256,512]{1,0:T(8,128)(2,1)S(1)}, bf16[256,512]{1,0:T(8,128)(2,1)S(1)}, u32[]{:S(2)}, u32[]{:S(2)}) collective-permute-start(bf16[256,512]{1,0:T(8,128)(2,1)S(1)} %maximum_select_fusion), channel_id=1, source_target_pairs={{0,8},{8,0},{1,9},{9,1},{2,10},{10,2},{3,11},{11,3},{4,12},{12,4},... | collective-permute-start | bytes 786440 | tf_op jit(solution)/shard_map/ppermute | solution.py:17
  24.9 12.2 %collective-permute-start.8 = (bf16[4,2,512,512]{3,2,1,0:T(8,128)(2,1)}, bf16[4,2,512,512]{3,2,1,0:T(8,128)(2,1)}, u32[]{:S(2)}, u32[]{:S(2)}) collective-permute-start(bf16[4,2,512,512]{3,2,1,0:T(8,128)(2,1)} %get-tuple-element.48), channel_id=1, source_target_pairs={{0,8},{8,0},{1,9},{9,1},{2,10},{10,2},{3,11},{11,3},{4,12},{12,4},... | collective-permute-start | bytes 12582920 | tf_op jit(solution)/shard_map/ppermute | solution.py:17
  25.3 32.7 %collective-permute-start.10 = (bf16[4,2,512,512]{3,2,1,0:T(8,128)(2,1)}, bf16[4,2,512,512]{3,2,1,0:T(8,128)(2,1)S(1)}, u32[]{:S(2)}, u32[]{:S(2)}) collective-permute-start(bf16[4,2,512,512]{3,2,1,0:T(8,128)(2,1)} %get-tuple-element.55), channel_id=1, source_target_pairs={{0,8},{8,0},{1,9},{9,1},{2,10},{10,2},{3,11},{11,3},{4,12},{12,4},... | collective-permute-start | bytes 12582920 | tf_op jit(solution)/shard_map/ppermute | solution.py:17
  25.4 26.6 %collective-permute-start.9 = (bf16[2,2,256,512]{3,2,1,0:T(8,128)(2,1)S(1)}, bf16[2,2,256,512]{3,2,1,0:T(8,128)(2,1)S(1)}, u32[]{:S(2)}, u32[]{:S(2)}) collective-permute-start(bf16[2,2,256,512]{3,2,1,0:T(8,128)(2,1)S(1)} %get-tuple-element.43), channel_id=1, source_target_pairs={{0,1},{1,0},{2,3},{3,2},{4,5},{5,4},{6,7},{7,6},{8,9},{9,8},{10,11... | collective-permute-start | bytes 3145736 | tf_op jit(solution)/shard_map/ppermute | solution.py:17
  28.4 7.9 %collective-permute-start.6 = (f32[2,128]{1,0:T(2,128)S(1)}, f32[2,128]{1,0:T(2,128)S(1)}, u32[]{:S(2)}, u32[]{:S(2)}) collective-permute-start(f32[2,128]{1,0:T(2,128)S(1)} %maximum_select_fusion.1), channel_id=1, source_target_pairs={{0,2},{1,3},{2,0},{3,1},{4,6},{5,7},{6,4},{7,5},{8,10},{9,11},{10,... | collective-permute-start | bytes 3080 | tf_op jit(solution)/shard_map/ppermute | solution.py:17
  36.2 49.0 %collective-permute-start.14 = (bf16[3,2,512,512]{3,2,1,0:T(8,128)(2,1)}, bf16[3,2,512,512]{3,2,1,0:T(8,128)(2,1)}, u32[]{:S(2)}, u32[]{:S(2)}) collective-permute-start(bf16[3,2,512,512]{3,2,1,0:T(8,128)(2,1)} %get-tuple-element.46), channel_id=1, source_target_pairs={{0,8},{8,0},{1,9},{9,1},{2,10},{10,2},{3,11},{11,3},{4,12},{12,4},... | collective-permute-start | bytes 9437192 | tf_op jit(solution)/shard_map/ppermute | solution.py:17
  36.3 53.0 %collective-permute-start.15 = (bf16[3,2,512,512]{3,2,1,0:T(8,128)(2,1)}, bf16[3,2,512,512]{3,2,1,0:T(8,128)(2,1)S(1)}, u32[]{:S(2)}, u32[]{:S(2)}) collective-permute-start(bf16[3,2,512,512]{3,2,1,0:T(8,128)(2,1)} %get-tuple-element.67), channel_id=1, source_target_pairs={{0,8},{8,0},{1,9},{9,1},{2,10},{10,2},{3,11},{11,3},{4,12},{12,4},... | collective-permute-start | bytes 9437192 | tf_op jit(solution)/shard_map/ppermute | solution.py:17
  37.0 17.2 %collective-permute-start.7 = (f32[2,128]{1,0:T(2,128)S(1)}, f32[2,128]{1,0:T(2,128)S(1)}, u32[]{:S(2)}, u32[]{:S(2)}) collective-permute-start(f32[2,128]{1,0:T(2,128)S(1)} %add.121), channel_id=1, source_target_pairs={{0,4},{1,5},{2,6},{3,7},{4,0},{5,1},{6,2},{7,3},{8,12},{9,13},{10,... | collective-permute-start | bytes 3080 | tf_op jit(solution)/shard_map/ppermute | solution.py:17
  52.0 24.9 %collective-permute-start.12 = (bf16[2,2,256,512]{3,2,1,0:T(8,128)(2,1)S(1)}, bf16[2,2,256,512]{3,2,1,0:T(8,128)(2,1)S(1)}, u32[]{:S(2)}, u32[]{:S(2)}) collective-permute-start(bf16[2,2,256,512]{3,2,1,0:T(8,128)(2,1)S(1)} %sums.10), channel_id=1, source_target_pairs={{0,1},{1,0},{2,3},{3,2},{4,5},{5,4},{6,7},{7,6},{8,9},{9,8},{10,11... | collective-permute-start | bytes 3145736 | tf_op jit(solution)/shard_map/ppermute | solution.py:17
  54.3 25.6 %collective-permute-start.13 = (bf16[2,2,256,512]{3,2,1,0:T(8,128)(2,1)S(1)}, bf16[2,2,256,512]{3,2,1,0:T(8,128)(2,1)S(1)}, u32[]{:S(2)}, u32[]{:S(2)}) collective-permute-start(bf16[2,2,256,512]{3,2,1,0:T(8,128)(2,1)S(1)} %pad_maximum_fusion.2), channel_id=1, source_target_pairs={{0,2},{1,3},{6,4},{7,5},{8,10},{9,11},{14,12},{15,13},{16,18},{17,... | collective-permute-start | bytes 3145736 | tf_op jit(solution)/shard_map/ppermute | solution.py:322
  58.0 2.3 %copy-start.1 = (bf16[4,2,512,512]{3,2,1,0:T(8,128)(2,1)}, bf16[4,2,512,512]{3,2,1,0:T(8,128)(2,1)S(1)}, u32[]{:S(2)}) copy-start(bf16[4,2,512,512]{3,2,1,0:T(8,128)(2,1)S(1)} %collective-permute-done.10.refs_0_) | copy-start | bytes 12582916
  58.0 20.4 %collective-permute-start.11 = (bf16[2,2,256,512]{3,2,1,0:T(8,128)(2,1)S(1)}, bf16[2,2,256,512]{3,2,1,0:T(8,128)(2,1)}, u32[]{:S(2)}, u32[]{:S(2)}) collective-permute-start(bf16[2,2,256,512]{3,2,1,0:T(8,128)(2,1)S(1)} %pad_maximum_fusion.2), channel_id=1, source_target_pairs={{2,4},{3,5},{4,2},{5,3},{10,12},{11,13},{12,10},{13,11},{18,20},{1... | collective-permute-start | bytes 3145736 | tf_op jit(solution)/shard_map/ppermute | solution.py:323
  76.9 24.0 %collective-permute-start.16 = (bf16[2,2,256,512]{3,2,1,0:T(8,128)(2,1)S(1)}, bf16[2,2,256,512]{3,2,1,0:T(8,128)(2,1)S(1)}, u32[]{:S(2)}, u32[]{:S(2)}) collective-permute-start(bf16[2,2,256,512]{3,2,1,0:T(8,128)(2,1)S(1)} %sums.12), channel_id=1, source_target_pairs={{0,1},{1,0},{2,3},{3,2},{4,5},{5,4},{6,7},{7,6},{8,9},{9,8},{10,11... | collective-permute-start | bytes 3145736 | tf_op jit(solution)/shard_map/ppermute | solution.py:17
  81.1 29.9 %collective-permute-start.17 = (bf16[2,256,512]{2,1,0:T(8,128)(2,1)}, bf16[2,256,512]{2,1,0:T(8,128)(2,1)}, u32[]{:S(2)}, u32[]{:S(2)}) collective-permute-start(bf16[2,256,512]{2,1,0:T(8,128)(2,1)} %fusion.10), channel_id=1, source_target_pairs={{0,2},{1,3},{2,0},{3,1},{4,6},{5,7},{6,4},{7,5},{8,10},{9,11},{10,... | collective-permute-start | bytes 1572872 | tf_op jit(solution)/shard_map/ppermute | solution.py:17
  85.0 27.4 %collective-permute-start.19 = (bf16[2,256,512]{2,1,0:T(8,128)(2,1)S(1)}, bf16[2,256,512]{2,1,0:T(8,128)(2,1)}, u32[]{:S(2)}, u32[]{:S(2)}) collective-permute-start(bf16[2,256,512]{2,1,0:T(8,128)(2,1)S(1)} %fusion.14), channel_id=1, source_target_pairs={{0,4},{1,5},{2,6},{3,7},{4,0},{5,1},{6,2},{7,3},{8,12},{9,13},{10,... | collective-permute-start | bytes 1572872 | tf_op jit(solution)/shard_map/ppermute | solution.py:17
  89.3 4.3 %copy-start = (bf16[3,2,512,512]{3,2,1,0:T(8,128)(2,1)}, bf16[3,2,512,512]{3,2,1,0:T(8,128)(2,1)S(1)}, u32[]{:S(2)}) copy-start(bf16[3,2,512,512]{3,2,1,0:T(8,128)(2,1)S(1)} %collective-permute-done.15.refs_0_.refs_1_) | copy-start | bytes 9437188
  100.9 30.8 %collective-permute-start.18 = (bf16[2,2,256,512]{3,2,1,0:T(8,128)(2,1)S(1)}, bf16[2,2,256,512]{3,2,1,0:T(8,128)(2,1)}, u32[]{:S(2)}, u32[]{:S(2)}) collective-permute-start(bf16[2,2,256,512]{3,2,1,0:T(8,128)(2,1)S(1)} %sums.14), channel_id=1, source_target_pairs={{0,1},{1,0},{2,3},{3,2},{4,5},{5,4},{6,7},{7,6},{8,9},{9,8},{10,11... | collective-permute-start | bytes 3145736 | tf_op jit(solution)/shard_map/ppermute | solution.py:17
  103.3 25.1 %collective-permute-start.20 = (bf16[2,256,512]{2,1,0:T(8,128)(2,1)S(1)}, bf16[2,256,512]{2,1,0:T(8,128)(2,1)S(1)}, u32[]{:S(2)}, u32[]{:S(2)}) collective-permute-start(bf16[2,256,512]{2,1,0:T(8,128)(2,1)S(1)} %fusion.6), channel_id=1, source_target_pairs={{0,2},{1,3},{2,0},{3,1},{4,6},{5,7},{6,4},{7,5},{8,10},{9,11},{10,... | collective-permute-start | bytes 1572872 | tf_op jit(solution)/shard_map/ppermute | solution.py:17
  105.4 26.4 %collective-permute-start.21 = (bf16[2,256,512]{2,1,0:T(8,128)(2,1)}, bf16[2,256,512]{2,1,0:T(8,128)(2,1)}, u32[]{:S(2)}, u32[]{:S(2)}) collective-permute-start(bf16[2,256,512]{2,1,0:T(8,128)(2,1)} %fusion.8), channel_id=1, source_target_pairs={{0,4},{1,5},{2,6},{3,7},{4,0},{5,1},{6,2},{7,3},{8,12},{9,13},{10,... | collective-permute-start | bytes 1572872 | tf_op jit(solution)/shard_map/ppermute | solution.py:17
  134.5 1.6 %collective-permute-start.22 = (bf16[128,1024]{1,0:T(8,128)(2,1)S(1)}, bf16[128,1024]{1,0:T(8,128)(2,1)S(1)}, u32[]{:S(2)}, u32[]{:S(2)}) collective-permute-start(bf16[128,1024]{1,0:T(8,128)(2,1)S(1)} %fusion.21), channel_id=1, source_target_pairs={{0,8},{8,0},{1,9},{9,1},{2,10},{10,2},{3,11},{11,3},{4,12},{12,4},... | collective-permute-start | bytes 786440 | tf_op jit(solution)/shard_map/ppermute | solution.py:17
